TPU v7x, 32 devices: a whole 2x2x4 slice. The times are simulated.
32 devices in a mesh: dp: 8 (over y, x, core), mp: 4 (over z).
Axes of the slice: x: 2, y: 2, z: 4, core: 2. Of those that a mesh axis runs over, the one named last changes fastest.
Arguments:
- patches: bfloat16 [1024, 6144], P('dp', 'mp'), may hold values from -200 to 200
- norm_gain: float32 [6144], replicated, may hold values from 0.25 to 1.75
- value_weight: bfloat16 [6144, 3072], P(None, 'mp'), may hold values from -0.078125 to 0.078125
- queries: bfloat16 [1024, 3072], P('dp', 'mp'), may hold values from -100 to 100
- key_vectors: bfloat16 [1024, 3072], P('dp', 'mp'), may hold values from -4 to 4
- head_cotangent: bfloat16 [2048, 3072], P('dp', 'mp'), may hold values from -6 to 6
- image_owner: int32 [8, 8], replicated, may hold values from 0 to 7, as said below
- patch_count: int32 [8, 8], replicated, may hold values from 0 to 32, as said below
Outputs:
- value_grad: float32 [6144, 3072], P('dp', 'mp')
- query_grad: bfloat16 [1024, 3072], P('dp', 'mp')
- key_grad: bfloat16 [1024, 3072], P('dp', 'mp')
Inputs may be any that keep to these rules, and one draw needn't show every extreme that they name: `image_owner`: each row lists every owner once. `patch_count`: 0 marks an empty image slot; each row sums to 128; some owner receives 32 patches from every device.
All inputs are finite; a program needn't handle non-finite values.
Results may differ from a plain program's by a relative error of at most 0.0065.
Values may be sent and summed in bfloat16 or wider, within the bound.
No kernel may reach another device: no remote copies, remote signals or barrier semaphores. Data moves between devices by JAX's collectives and lax.ppermute only.
A program may use at most 128 MiB of HBM per device.

v0:
```python
import jax
import jax.numpy as jnp
from jax import lax
from jax.sharding import PartitionSpec as P

HD = 128


def normalize(rows, norm_gain):
    values = rows.astype(jnp.float32)
    average = jnp.mean(values, axis=-1, keepdims=True)
    centred = values - average
    variance = jnp.mean(centred * centred, axis=-1, keepdims=True)
    return (centred * lax.rsqrt(variance + 1e-06) * norm_gain).astype(jnp.bfloat16)


def normalize_rows(rows, norm_gain):
    total = rows.shape[0]
    size = 512 if total % 512 == 0 else total
    blocks = rows.reshape(total // size, size, rows.shape[1])
    return lax.map(lambda block: normalize(block, norm_gain), blocks).reshape(total, rows.shape[1])


def windows(values, block):
    count = values.shape[0] // block
    grouped = values.reshape((count, block) + values.shape[1:])
    return grouped


def fold_back(parts, block):
    count = parts.shape[0]
    return parts.reshape((count * block,) + parts.shape[2:])


def attention_grads(query_rows, key_rows, value_rows, cotangent, segment, valid, block, reach):
    total, width = query_rows.shape
    heads_here = width // HD
    count = total // block
    span = (2 * reach + 1) * block
    scale = HD ** (-0.5)
    query_heads = query_rows.reshape(count, block, heads_here, HD)
    cot_heads = cotangent.reshape(count, block, heads_here, HD)
    key_heads = windows(key_rows, block).reshape(count, span, heads_here, HD)
    value_heads = windows(value_rows, block).reshape(count, span, heads_here, HD)
    query_seg = segment.reshape(count, block)
    key_seg = windows(segment, block)
    query_valid = valid.reshape(count, block)
    key_valid = windows(valid, block)
    scores = (
        jnp.einsum("bqhd,bkhd->bhqk", query_heads, key_heads, preferred_element_type=jnp.float32)
        * scale
    )
    allowed = (query_seg[:, :, None] == key_seg[:, None, :]) & key_valid[:, None, :]
    scores = jnp.where(allowed[:, None], scores, -1000000000.0)
    peak = jnp.max(scores, axis=-1, keepdims=True)
    weights = jnp.exp(scores - peak)
    weights = weights / jnp.sum(weights, axis=-1, keepdims=True)
    weights = jnp.where(query_valid[:, None, :, None], weights, 0.0)
    value_part = jnp.einsum(
        "bhqk,bqhd->bkhd",
        weights.astype(jnp.bfloat16),
        cot_heads,
        preferred_element_type=jnp.float32,
    )
    prob_grad = jnp.einsum(
        "bqhd,bkhd->bhqk", cot_heads, value_heads, preferred_element_type=jnp.float32
    )
    centre = jnp.sum(weights * prob_grad, axis=-1, keepdims=True)
    score_grad = (weights * (prob_grad - centre)).astype(jnp.bfloat16)
    query_grad = (
        jnp.einsum("bhqk,bkhd->bqhd", score_grad, key_heads, preferred_element_type=jnp.float32)
        * scale
    ).astype(jnp.bfloat16)
    key_part = (
        jnp.einsum("bhqk,bqhd->bkhd", score_grad, query_heads, preferred_element_type=jnp.float32)
        * scale
    )
    value_grad = fold_back(value_part, block).astype(jnp.bfloat16)
    key_grad = fold_back(key_part, block).astype(jnp.bfloat16)
    return (
        value_grad.reshape(total, width),
        query_grad.reshape(total, width),
        key_grad.reshape(total, width),
    )


def weight_sums(normed, value_rows):
    return lax.psum_scatter(
        lax.dot_general(
            normed, value_rows, (((0,), (0,)), ((), ())), preferred_element_type=jnp.float32
        ),
        "dp",
        scatter_dimension=0,
        tiled=True,
    )


def pack_plan(image_owner, patch_count, rows_here, capacity, devices):
    device = lax.axis_index("dp")
    own_list = lax.dynamic_index_in_dim(image_owner, device, 0, keepdims=False)
    own_count = lax.dynamic_index_in_dim(patch_count, device, 0, keepdims=False)
    ends = jnp.cumsum(own_count)
    starts = ends - own_count
    targets = jnp.arange(devices, dtype=jnp.int32)
    matches = own_list[None, :] == targets[:, None]
    send_start = jnp.sum(jnp.where(matches, starts[None, :], 0), axis=1)
    send_count = jnp.sum(jnp.where(matches, own_count[None, :], 0), axis=1)
    slots = jnp.arange(capacity, dtype=jnp.int32)
    send_row = jnp.clip(send_start[:, None] + slots[None, :], 0, rows_here - 1)
    send_valid = slots[None, :] < send_count[:, None]
    incoming = jnp.sum(jnp.where(image_owner == device, patch_count, 0), axis=1)
    recv_valid = (slots[None, :] < incoming[:, None]).reshape(-1)
    row_index = jnp.arange(rows_here, dtype=jnp.int32)
    image_of = jnp.sum((ends[None, :] <= row_index[:, None]).astype(jnp.int32), axis=1)
    picked = image_of[:, None] == targets[None, :]
    row_owner = jnp.sum(jnp.where(picked, own_list[None, :], 0), axis=1)
    row_start = jnp.sum(jnp.where(picked, starts[None, :], 0), axis=1)
    back_index = row_owner * capacity + row_index - row_start
    return (send_row, send_valid, recv_valid, image_of, back_index)


def body(
    patches, norm_gain, value_weight, queries, key_vectors, head_cotangent, image_owner, patch_count
):
    devices = lax.axis_size("dp")
    rows_here = patches.shape[0]
    width = queries.shape[1]
    capacity = head_cotangent.shape[0] // devices
    slot_total = devices * capacity
    send_row, send_valid, recv_valid, image_of, back_index = pack_plan(
        image_owner, patch_count, rows_here, capacity, devices
    )

    def packed(rows):
        return jnp.where(send_valid[:, :, None], rows[send_row], 0)

    moved = (
        lax.all_to_all(packed(patches), "dp", split_axis=0, concat_axis=0, tiled=True),
        lax.all_to_all(packed(queries), "dp", split_axis=0, concat_axis=0, tiled=True),
        lax.all_to_all(packed(key_vectors), "dp", split_axis=0, concat_axis=0, tiled=True),
    )
    features = moved[0].reshape(slot_total, -1)
    whole = lax.all_gather(features, "mp", axis=1, tiled=True)
    normed = normalize_rows(whole, norm_gain)
    value_rows = jnp.dot(normed, value_weight, preferred_element_type=jnp.float32).astype(
        jnp.bfloat16
    )
    segment = jnp.arange(slot_total, dtype=jnp.int32) // capacity
    value_grad, query_grad, key_grad = attention_grads(
        moved[1].reshape(slot_total, width),
        moved[2].reshape(slot_total, width),
        value_rows,
        head_cotangent,
        segment,
        recv_valid,
        capacity,
        0,
    )
    weight_grad = weight_sums(normed, value_grad)
    returned = (
        lax.all_to_all(
            query_grad.reshape(devices, capacity, width),
            "dp",
            split_axis=0,
            concat_axis=0,
            tiled=True,
        ),
        lax.all_to_all(
            key_grad.reshape(devices, capacity, width),
            "dp",
            split_axis=0,
            concat_axis=0,
            tiled=True,
        ),
    )
    query_out = returned[0].reshape(slot_total, width)[back_index]
    key_out = returned[1].reshape(slot_total, width)[back_index]
    return (weight_grad, query_out, key_out)


def solution(mesh):
    return jax.shard_map(
        body,
        mesh=mesh,
        in_specs=(
            P("dp", "mp"),
            P(),
            P(None, "mp"),
            P("dp", "mp"),
            P("dp", "mp"),
            P("dp", "mp"),
            P(),
            P(),
        ),
        out_specs=(P("dp", "mp"), P("dp", "mp"), P("dp", "mp")),
        check_vma=False,
    )
```

profile of v0, /device:TPU:0, one launch (start us, length us, event | category | flops | bytes accessed | tf_op | source)
XLA Modules:
  0.0 237.6 jit_solution(16708023856245612324)
XLA Ops:
  7.2 0.0 copy-start
  7.2 0.0 copy-start.1
  7.2 0.0 all-gather.2.cloned.1.call-start
  7.2 0.7 fusion.34
  8.0 0.2 reduce-window.4
  8.2 0.7 fusion.33
  8.9 0.0 copy-done.15
  8.9 0.1 select_reduce_fusion.4
  9.0 0.1 iota_compare_fusion.4
  9.1 0.1 compare_select_fusion
  9.2 0.1 reshape.270
  9.3 0.0 copy-done
  9.3 0.0 copy-start.2
  9.3 1.3 gather_fusion
  10.6 0.1 broadcast_select_fusion
  10.7 0.0 copy-start.12
  10.7 0.0 copy-start.13
  10.7 0.0 copy-start.10
  10.7 17.8 %all_to_all.25 = bf16[8,32,1536]{2,1,0:T(8,128)(2,1)} all-to-all(bf16[8,32,1536]{2,1,0:T(8,128)(2,1)S(1)} %broadcast_select_fusion), channel_id=1, replica_groups=mesh['dp'=8,'mp'=4] {'dp'}, dimensions={0} | all-to-all | bytes 1572864 | tf_op jit(solution)/shard_map/all_to_all | solution.py:138
  28.5 0.0 all-gather.2.cloned.1.call-update
  28.5 0.0 copy-done.1
  28.5 1.2 gather_fusion.2
  29.7 0.0 copy-done.2
  29.7 1.2 gather_fusion.1
  30.9 1.0 broadcast_select_fusion.2
  31.9 3.5 %all-to-all-start.1 = ((bf16[8,32,768]{2,1,0:T(8,128)(2,1)}), bf16[8,32,768]{2,1,0:T(8,128)(2,1)S(1)}, u32[]{:S(2)}, u32[]{:S(2)}) async-start(bf16[8,32,768]{2,1,0:T(8,128)(2,1)} %get-tuple-element.21), calls=%async_computation.1 | async-start | bytes 786432 | tf_op jit(solution)/shard_map/all_to_all | solution.py:139
  35.4 0.1 select_reduce_fusion.2
  35.5 8.1 %all-to-all-done.1 = bf16[8,32,768]{2,1,0:T(8,128)(2,1)S(1)} async-done(((bf16[8,32,768]{2,1,0:T(8,128)(2,1)}), bf16[8,32,768]{2,1,0:T(8,128)(2,1)S(1)}, u32[]{:S(2)}, u32[]{:S(2)}) %all-to-all-start.1) | async-done | bytes 393248 | tf_op jit(solution)/shard_map/all_to_all | solution.py:139
  43.6 3.5 %all-to-all-start.2 = ((bf16[8,32,768]{2,1,0:T(8,128)(2,1)}), bf16[8,32,768]{2,1,0:T(8,128)(2,1)S(1)}, u32[]{:S(2)}, u32[]{:S(2)}) async-start(bf16[8,32,768]{2,1,0:T(8,128)(2,1)} %get-tuple-element.22), calls=%async_computation.2 | async-start | bytes 786432 | tf_op jit(solution)/shard_map/all_to_all | solution.py:140
  47.1 0.0 reduce-scatter.2.cloned.1.call-start
  47.2 0.1 iota_compare_fusion.2
  47.2 0.0 copy-done.10
  47.2 0.5 reshape.265
  47.7 0.1 compare_and_fusion
  47.9 7.5 %all-to-all-done.2 = bf16[8,32,768]{2,1,0:T(8,128)(2,1)S(1)} async-done(((bf16[8,32,768]{2,1,0:T(8,128)(2,1)}), bf16[8,32,768]{2,1,0:T(8,128)(2,1)S(1)}, u32[]{:S(2)}, u32[]{:S(2)}) %all-to-all-start.2) | async-done | bytes 393248 | tf_op jit(solution)/shard_map/all_to_all | solution.py:140
  55.4 0.3 fusion.8
  55.7 1.1 fusion.38
  56.8 0.4 fusion.11
  57.2 1.0 copy.29
  58.2 0.0 copy-done.5
  58.2 0.0 copy-done.9
  58.2 33.3 %all-gather.2.cloned.1.call-done = bf16[256,6144]{1,0:T(8,128)(2,1)} async-done(((bf16[256,1536]{1,0:T(8,128)(2,1)}), bf16[256,6144]{1,0:T(8,128)(2,1)}) %all-gather.2.cloned.1.call-update) | async-done | bytes 3145744 | tf_op jit(solution)/shard_map/all_gather | solution.py:143
  91.5 2.5 %convert_reduce_fusion = f32[256]{0:T(256)S(1)} fusion(bf16[256,6144]{1,0:T(8,128)(2,1)} %all-gather.2.cloned.1.call-done), kind=kLoop, calls=%fused_computation.7 | loop fusion | flops 3145472 | bytes 3146752 | tf_op jit(solution)/shard_map/while/body/eval_jaxpr/reduce_sum | solution.py:11
  94.1 2.9 %fusion.3 = f32[256]{0:T(256)S(1)} fusion(bf16[256,6144]{1,0:T(8,128)(2,1)} %all-gather.2.cloned.1.call-done, f32[256]{0:T(256)S(1)} %broadcast_multiply_fusion), kind=kLoop, calls=%fused_computation.10 | loop fusion | flops 6291200 | bytes 3147776 | tf_op jit(solution)/shard_map/while/body/eval_jaxpr/reduce_sum | solution.py:13
  96.9 8.8 %fusion.14 = f32[6144,768]{1,0:T(8,128)} fusion(bf16[32,8,6,128]{3,2,1,0:T(8,128)(2,1)S(1)} %bitcast.85, bf16[256,6144]{1,0:T(8,128)(2,1)S(1)} %copy-done.3, f32[6144]{0:T(1024)} %param.9, f32[256]{0:T(256)S(1)} %add_rsqrt_fusion, f32[256]{0:T(256)S(1)} %broadcast_multiply_fusion), kind=kOutput, calls=%fused_computation.31 | convolution fusion | flops 2423783424 | bytes 22439936 | tf_op jit(solution)/shard_map/dot_general | solution.py:89
  105.7 0.0 reduce-scatter.2.cloned.1.call-update
  105.8 7.2 %convolution_convert_fusion.1 = bf16[256,768]{1,0:T(8,128)(2,1)} fusion(bf16[6144,768]{1,0:T(8,128)(2,1)} %param.10, bf16[256,6144]{1,0:T(8,128)(2,1)S(1)} %copy-done.3, f32[6144]{0:T(1024)} %param.9, f32[256]{0:T(256)S(1)} %add_rsqrt_fusion, f32[256]{0:T(256)S(1)} %broadcast_multiply_fusion), kind=kOutput, calls=%fused_computation.23 | convolution fusion | flops 2423980032 | bytes 13002752 | tf_op jit(solution)/shard_map/dot_general | solution.py:145
  113.0 1.6 reshape_reshape.11
  114.6 1.9 multiply_reduce_fusion
  116.5 1.5 multiply_convert_fusion
  118.0 0.0 copy-done.6
  118.0 0.2 fusion.12
  118.2 0.8 copy.75
  119.1 3.7 %all-to-all-start.4 = ((bf16[8,32,768]{2,1,0:T(8,128)(2,1)}), bf16[8,32,768]{2,1,0:T(8,128)(2,1)S(1)}, u32[]{:S(2)}, u32[]{:S(2)}) async-start(bf16[8,32,768]{2,1,0:T(8,128)(2,1)} %bitcast.79), calls=%async_computation.5 | async-start | bytes 786432 | tf_op jit(solution)/shard_map/all_to_all | solution.py:168
  122.7 0.1 convert_reduce_fusion.1
  122.8 0.3 fusion.13
  123.1 0.8 copy.76
  124.0 7.1 %all-to-all-done.4 = bf16[8,32,768]{2,1,0:T(8,128)(2,1)S(1)} async-done(((bf16[8,32,768]{2,1,0:T(8,128)(2,1)}), bf16[8,32,768]{2,1,0:T(8,128)(2,1)S(1)}, u32[]{:S(2)}, u32[]{:S(2)}) %all-to-all-start.4) | async-done | bytes 393248 | tf_op jit(solution)/shard_map/all_to_all | solution.py:168
  131.1 3.5 %all-to-all-start.3 = ((bf16[8,32,768]{2,1,0:T(8,128)(2,1)}), bf16[8,32,768]{2,1,0:T(8,128)(2,1)S(1)}, u32[]{:S(2)}, u32[]{:S(2)}) async-start(bf16[8,32,768]{2,1,0:T(8,128)(2,1)} %bitcast.80), calls=%async_computation.4 | async-start | bytes 786432 | tf_op jit(solution)/shard_map/all_to_all | solution.py:161
  134.5 0.1 select_reduce_fusion.1
  134.6 1.5 gather_fusion.4
  136.2 6.6 %all-to-all-done.3 = bf16[8,32,768]{2,1,0:T(8,128)(2,1)S(1)} async-done(((bf16[8,32,768]{2,1,0:T(8,128)(2,1)}), bf16[8,32,768]{2,1,0:T(8,128)(2,1)S(1)}, u32[]{:S(2)}, u32[]{:S(2)}) %all-to-all-start.3) | async-done | bytes 393248 | tf_op jit(solution)/shard_map/all_to_all | solution.py:161
  142.8 1.5 gather_fusion.3
  144.3 86.4 %reduce-scatter.2.cloned.1.call-done = f32[768,768]{1,0:T(8,128)} async-done(((f32[6144,768]{1,0:T(8,128)}), f32[768,768]{1,0:T(8,128)}) %reduce-scatter.2.cloned.1.call-update) | async-done | bytes 2359312 | tf_op jit(solution)/shard_map/reduce_scatter | solution.py:88
  (26 shorter events, 0.1 us)
Async XLA Ops:
  7.2 2.1 copy-start
  7.2 21.3 %copy-start.1 = (bf16[128,768]{1,0:T(8,128)(2,1)S(1)}, bf16[128,768]{1,0:T(8,128)(2,1)}, u32[]{:S(2)}) copy-start(bf16[128,768]{1,0:T(8,128)(2,1)} %param.12) | copy-start | bytes 589828
  7.2 84.3 %all-gather.2.cloned.1.call-start = ((), (), s32[]{:S(2)}) async-start(), calls=%async_computation.6 | async-start | bytes 3932160 | tf_op jit(solution)/shard_map/all_gather | solution.py:143
  8.2 0.7 copy-start.15
  9.3 20.4 %copy-start.2 = (bf16[128,768]{1,0:T(8,128)(2,1)S(1)}, bf16[128,768]{1,0:T(8,128)(2,1)}, u32[]{:S(2)}) copy-start(bf16[128,768]{1,0:T(8,128)(2,1)} %param.11) | copy-start | bytes 589828
  10.7 24.7 %copy-start.12 = (s32[8,8]{1,0:T(8,128)S(1)}, s32[8,8]{1,0:T(8,128)}, u32[]{:S(2)}) copy-start(s32[8,8]{1,0:T(8,128)} %param.15) | copy-start | bytes 772
  10.7 24.7 %copy-start.13 = (s32[8,8]{1,0:T(8,128)S(1)}, s32[8,8]{1,0:T(8,128)}, u32[]{:S(2)}) copy-start(s32[8,8]{1,0:T(8,128)} %param.14) | copy-start | bytes 772
  10.7 36.5 %copy-start.10 = (bf16[256,768]{1,0:T(8,128)(2,1)S(1)}, bf16[256,768]{1,0:T(8,128)(2,1)}, u32[]{:S(2)}) copy-start(bf16[256,768]{1,0:T(8,128)(2,1)} %param.13) | copy-start | bytes 1179652
  31.9 11.7 %all-to-all-start.1 = ((bf16[8,32,768]{2,1,0:T(8,128)(2,1)}), bf16[8,32,768]{2,1,0:T(8,128)(2,1)S(1)}, u32[]{:S(2)}, u32[]{:S(2)}) async-start(bf16[8,32,768]{2,1,0:T(8,128)(2,1)} %get-tuple-element.21), calls=%async_computation.1 | async-start | bytes 786432 | tf_op jit(solution)/shard_map/all_to_all | solution.py:139
  43.6 14.5 %copy-start.5 = (bf16[8,32,768]{2,1,0:T(8,128)(2,1)}, bf16[8,32,768]{2,1,0:T(8,128)(2,1)S(1)}, u32[]{:S(2)}) copy-start(bf16[8,32,768]{2,1,0:T(8,128)(2,1)S(1)} %all-to-all-done.1) | copy-start | bytes 1179652
  43.6 11.7 %all-to-all-start.2 = ((bf16[8,32,768]{2,1,0:T(8,128)(2,1)}), bf16[8,32,768]{2,1,0:T(8,128)(2,1)S(1)}, u32[]{:S(2)}, u32[]{:S(2)}) async-start(bf16[8,32,768]{2,1,0:T(8,128)(2,1)} %get-tuple-element.22), calls=%async_computation.2 | async-start | bytes 786432 | tf_op jit(solution)/shard_map/all_to_all | solution.py:140
  47.1 183.6 %reduce-scatter.2.cloned.1.call-start = ((), (), s32[]{:S(2)}) async-start(), calls=%async_computation.7 | async-start | bytes 21233664 | tf_op jit(solution)/shard_map/reduce_scatter | solution.py:88
  47.2 11.0 %copy-start.14 = (pred[8,32]{1,0:T(8,128)(4,1)}, pred[8,32]{1,0:T(8,128)(4,1)S(1)}, u32[]{:S(2)}) copy-start(pred[8,32]{1,0:T(8,128)(4,1)S(1)} %iota_compare_fusion.2) | copy-start | bytes 772
  47.7 10.5 %copy-start.9 = (bf16[8,32,6,128]{3,2,1,0:T(8,128)(2,1)}, bf16[8,32,6,128]{3,2,1,0:T(8,128)(2,1)S(1)}, u32[]{:S(2)}) copy-start(bf16[8,32,6,128]{3,2,1,0:T(8,128)(2,1)S(1)} %reshape.265) | copy-start | bytes 1179652
  55.4 2.8 %copy-start.7 = (bf16[8,32,768]{2,1,0:T(8,128)(2,1)}, bf16[8,32,768]{2,1,0:T(8,128)(2,1)S(1)}, u32[]{:S(2)}) copy-start(bf16[8,32,768]{2,1,0:T(8,128)(2,1)S(1)} %all-to-all-done.2) | copy-start | bytes 1179652
  56.8 1.4 copy-start.11
  91.5 5.4 %copy-start.3 = (bf16[256,6144]{1,0:T(8,128)(2,1)S(1)}, bf16[256,6144]{1,0:T(8,128)(2,1)}, u32[]{:S(2)}) copy-start(bf16[256,6144]{1,0:T(8,128)(2,1)} %all-gather.2.cloned.1.call-done) | copy-start | bytes 9437188
  91.5 5.4 %copy-start.4 = (bf16[8,32,6,128]{3,2,1,0:T(8,128)(2,1)S(1)}, bf16[8,32,6,128]{3,2,1,0:T(8,128)(2,1)}, u32[]{:S(2)}) copy-start(bf16[8,32,6,128]{3,2,1,0:T(8,128)(2,1)} %copy.29) | copy-start | bytes 1179652
  113.0 5.0 %copy-start.6 = (bf16[8,32,768]{2,1,0:T(8,128)(2,1)S(1)}, bf16[8,32,768]{2,1,0:T(8,128)(2,1)}, u32[]{:S(2)}) copy-start(bf16[8,32,768]{2,1,0:T(8,128)(2,1)} %copy-done.5) | copy-start | bytes 1179652
  113.0 9.8 %copy-start.16 = (s32[8,1]{0,1:T(1,128)S(1)}, s32[8,1]{0,1:T(1,128)}, u32[]{:S(2)}) copy-start(s32[8,1]{0,1:T(1,128)} %copy-done.15) | copy-start | bytes 100
  113.0 9.9 %copy-start.8 = (bf16[8,32,768]{2,1,0:T(8,128)(2,1)S(1)}, bf16[8,32,768]{2,1,0:T(8,128)(2,1)}, u32[]{:S(2)}) copy-start(bf16[8,32,768]{2,1,0:T(8,128)(2,1)} %copy-done.7) | copy-start | bytes 1179652
  119.1 12.0 %all-to-all-start.4 = ((bf16[8,32,768]{2,1,0:T(8,128)(2,1)}), bf16[8,32,768]{2,1,0:T(8,128)(2,1)S(1)}, u32[]{:S(2)}, u32[]{:S(2)}) async-start(bf16[8,32,768]{2,1,0:T(8,128)(2,1)} %bitcast.79), calls=%async_computation.5 | async-start | bytes 786432 | tf_op jit(solution)/shard_map/all_to_all | solution.py:168
  131.1 11.7 %all-to-all-start.3 = ((bf16[8,32,768]{2,1,0:T(8,128)(2,1)}), bf16[8,32,768]{2,1,0:T(8,128)(2,1)S(1)}, u32[]{:S(2)}, u32[]{:S(2)}) async-start(bf16[8,32,768]{2,1,0:T(8,128)(2,1)} %bitcast.80), calls=%async_computation.4 | async-start | bytes 786432 | tf_op jit(solution)/shard_map/all_to_all | solution.py:161
Sparse Core Ops, SparseCore 0:
  28.6 62.8 all-gather.1
  105.9 124.7 reduce-scatter.1
where the time goes:
time: 238 us
  waiting for transfers between devices  149 us (63%)
  matrix products  19.2 us (8%)
  blocking collectives  17.8 us (7%)
  between operations  14.3 us (6%)
  starting transfers between devices  14.1 us (6%)
  local copies, waits for them, and re-layouts  12.3 us (5%)
  other arithmetic  10.9 us (5%)
    reduce_scatter x1, waiting for transfers between devices, weight_sums(): lax.psum_scatter(lax.dot_general(normed, value_rows, (((0,), (0,)), ((),...  86.4 us
    all_gather x1, waiting for transfers between devices, body(): whole = lax.all_gather(features, 'mp', axis=1, tiled=True)  33.3 us
    all_to_all x1, blocking collectives, body(): lax.all_to_all(packed(patches), 'dp', split_axis=0, concat_axis=0, tiled=...  17.8 us
    dot_general x1, matrix products, weight_sums(): lax.dot_general(normed, value_rows, (((0,), (0,)), ((), ())), preferred_e...  8.81 us
    all_to_all x1, waiting for transfers between devices, body(): lax.all_to_all(packed(queries), 'dp', split_axis=0, concat_axis=0, tiled=...  8.14 us
    all_to_all x1, waiting for transfers between devices, body(): lax.all_to_all(packed(key_vectors), 'dp', split_axis=0, concat_axis=0, ti...  7.52 us
    dot_general x1, matrix products, body(): jnp.dot(normed, value_weight, preferred_element_type=jnp.float32)  7.19 us
    all_to_all x1, waiting for transfers between devices, body(): lax.all_to_all(key_grad.reshape(devices, capacity, width), 'dp', split_ax...  7.11 us
  transfers between devices with their start and end apart: 6, of which 6 were waited for; matrix products, arithmetic and copies ran while one was open for 10% of the time, Pallas kernels for 0%

commit v1 on v0

v1 whole, which is shorter than its diff:
```python
import jax
import jax.numpy as jnp
from jax import lax
from jax.sharding import PartitionSpec as P

HD = 128


def normalize(rows, norm_gain):
    values = rows.astype(jnp.float32)
    average = jnp.mean(values, axis=-1, keepdims=True)
    centred = values - average
    variance = jnp.mean(centred * centred, axis=-1, keepdims=True)
    return (centred * lax.rsqrt(variance + 1e-06) * norm_gain).astype(jnp.bfloat16)


def row_plan(image_owner, patch_count, rows_here, capacity, devices):
    device = lax.axis_index("dp")
    own_list = lax.dynamic_index_in_dim(image_owner, device, 0, keepdims=False)
    own_count = lax.dynamic_index_in_dim(patch_count, device, 0, keepdims=False)
    ends = jnp.cumsum(own_count)
    starts = ends - own_count
    row_index = jnp.arange(rows_here, dtype=jnp.int32)
    image_of = jnp.sum((ends[None, :] <= row_index[:, None]).astype(jnp.int32), axis=1)
    picked = image_of[:, None] == jnp.arange(devices, dtype=jnp.int32)[None, :]
    row_owner = jnp.sum(jnp.where(picked, own_list[None, :], 0), axis=1)
    row_start = jnp.sum(jnp.where(picked, starts[None, :], 0), axis=1)
    return image_of, row_owner * capacity + row_index - row_start


def attention_grads(query_rows, key_rows, value_rows, cotangent, segment):
    total, width = query_rows.shape
    heads = width // HD
    scale = HD ** (-0.5)

    def split(rows):
        return rows.reshape(total, heads, HD)

    query, key, value, cot = split(query_rows), split(key_rows), split(value_rows), split(cotangent)
    scores = jnp.einsum("qhd,khd->hqk", query, key, preferred_element_type=jnp.float32) * scale
    allowed = segment[:, None] == segment[None, :]
    scores = jnp.where(allowed[None], scores, -1000000000.0)
    weights = jnp.exp(scores - jnp.max(scores, axis=-1, keepdims=True))
    weights = weights / jnp.sum(weights, axis=-1, keepdims=True)
    value_grad = jnp.einsum(
        "hqk,qhd->khd", weights.astype(jnp.bfloat16), cot, preferred_element_type=jnp.float32
    )
    prob_grad = jnp.einsum("qhd,khd->hqk", cot, value, preferred_element_type=jnp.float32)
    centre = jnp.sum(weights * prob_grad, axis=-1, keepdims=True)
    score_grad = (weights * (prob_grad - centre)).astype(jnp.bfloat16)
    query_grad = jnp.einsum("hqk,khd->qhd", score_grad, key, preferred_element_type=jnp.float32)
    key_grad = jnp.einsum("hqk,qhd->khd", score_grad, query, preferred_element_type=jnp.float32)

    def join(rows):
        return rows.astype(jnp.bfloat16).reshape(total, width)

    return join(value_grad), join(query_grad * scale), join(key_grad * scale)


def general_body(
    patches, norm_gain, value_weight, queries, key_vectors, head_cotangent, image_owner, patch_count
):
    devices = lax.axis_size("dp")
    rows_here = patches.shape[0]
    width = queries.shape[1]
    capacity = head_cotangent.shape[0] // devices
    segment, index = row_plan(image_owner, patch_count, rows_here, capacity, devices)
    slots = lax.all_to_all(
        head_cotangent.reshape(devices, capacity, width), "dp", split_axis=0, concat_axis=0, tiled=True
    )
    cotangent = slots.reshape(devices * capacity, width)[index]
    normed = normalize(lax.all_gather(patches, "mp", axis=1, tiled=True), norm_gain)
    values = jnp.dot(normed, value_weight, preferred_element_type=jnp.float32).astype(jnp.bfloat16)
    value_rows, query_grad, key_grad = attention_grads(
        queries, key_vectors, values, cotangent, segment
    )
    all_value_rows = lax.all_gather(value_rows, "dp", axis=0, tiled=True)
    columns = jnp.swapaxes(normed.reshape(rows_here, devices, -1), 0, 1)
    columns = lax.all_to_all(columns, "dp", split_axis=0, concat_axis=0, tiled=True)
    columns = columns.reshape(devices * rows_here, -1)
    weight_grad = lax.dot_general(
        columns, all_value_rows, (((0,), (0,)), ((), ())), preferred_element_type=jnp.float32
    )
    return weight_grad, query_grad, key_grad


def solution(mesh):
    return jax.shard_map(
        general_body,
        mesh=mesh,
        in_specs=(
            P("dp", "mp"),
            P(),
            P(None, "mp"),
            P("dp", "mp"),
            P("dp", "mp"),
            P("dp", "mp"),
            P(),
            P(),
        ),
        out_specs=(P("dp", "mp"), P("dp", "mp"), P("dp", "mp")),
        check_vma=False,
    )
```

time: 238 us -> 97.6 us (0.41)
  waiting for transfers between devices: 149 us -> 48.2 us
  blocking collectives: 17.8 us -> 0 us
  matrix products: 19.2 us -> 11.8 us
  starting transfers between devices: 14.1 us -> 8.91 us
  local copies, waits for them, and re-layouts: 12.3 us -> 7.44 us
  other arithmetic: 10.9 us -> 6.65 us
    reduce_scatter x1 -> x0, waiting for transfers between devices: 86.4 us -> none  [weight_sums(): lax.psum_scatter(lax.dot_general(normed, value_rows, (((0,), (0,)), ((),...]
    all_to_all x1 -> x0, blocking collectives: 17.8 us -> none  [body(): lax.all_to_all(packed(patches), 'dp', split_axis=0, concat_axis=0, tiled=...]
    dot_general x7, matrix products: 19.2 us -> 11.8 us  [the longest x1 5.64 us: general_body(): jnp.dot(normed, value_weight, preferred_element_type=jnp.float32)]
    all_to_all x4 -> x2, waiting for transfers between devices: 29.4 us -> 22.1 us  [the longest x1 17.6 us: general_body(): lax.all_to_all(columns, 'dp', split_axis=0, concat_axis=0, tiled=True)]
    all_gather x1 -> x2, waiting for transfers between devices: 33.3 us -> 26.1 us  [the longest x1 25.2 us: general_body(): lax.all_gather(patches, 'mp', axis=1, tiled=True)]
    gather x5 -> x2, local copies, waits for them, and re-layouts: 6.73 us -> 1.03 us  [general_body(): cotangent = slots.reshape(devices * capacity, width)[index]]
    all_to_all x4 -> x2, starting transfers between devices: 14 us -> 8.83 us  [the longest x1 5.18 us: general_body(): lax.all_to_all(head_cotangent.reshape(devices, capacity, width), 'dp', sp...]
    unnamed x34 -> x11, local copies, waits for them, and re-layouts: 0.08 us -> 4.86 us
  transfers between devices with their start and end apart: 6 -> 4, of which waited for: 6 -> 4; matrix products, arithmetic and copies ran while one was open for 10% -> 20% of each run, Pallas kernels for 0% -> 0%
where the time goes in v1:
time: 97.6 us; the launch traced here: 97.2 us
  waiting for transfers between devices  48.2 us (49%)
  between operations  14.2 us (15%)
  matrix products  11.8 us (12%)
  starting transfers between devices  8.91 us (9%)
  local copies, waits for them, and re-layouts  7.44 us (8%)
  other arithmetic  6.65 us (7%)
    all_gather x1, waiting for transfers between devices, general_body(): lax.all_gather(patches, 'mp', axis=1, tiled=True)  25.2 us
    all_to_all x1, waiting for transfers between devices, general_body(): lax.all_to_all(columns, 'dp', split_axis=0, concat_axis=0, tiled=True)  17.6 us
    dot_general x1, matrix products, general_body(): jnp.dot(normed, value_weight, preferred_element_type=jnp.float32)  5.64 us
    all_to_all x1, starting transfers between devices, general_body(): lax.all_to_all(head_cotangent.reshape(devices, capacity, width), 'dp', sp...  5.18 us
    unnamed x11, local copies, waits for them, and re-layouts  4.86 us
    all_to_all x1, waiting for transfers between devices, general_body(): lax.all_to_all(head_cotangent.reshape(devices, capacity, width), 'dp', sp...  4.51 us
    dot_general x1, matrix products, general_body(): lax.dot_general(columns, all_value_rows, (((0,), (0,)), ((), ())), prefer...  4.24 us
    all_to_all x1, starting transfers between devices, general_body(): lax.all_to_all(columns, 'dp', split_axis=0, concat_axis=0, tiled=True)  3.65 us
  transfers between devices with their start and end apart: 4, of which 4 were waited for; matrix products, arithmetic and copies ran while one was open for 20% of the time, Pallas kernels for 0%

profile of v1, /device:TPU:0, one launch (start us, length us, event | category | flops | bytes accessed | tf_op | source)
XLA Modules:
  0.0 97.2 jit_solution(5959448944369848382)
XLA Ops:
  7.2 0.0 copy-start.1
  7.2 0.0 all-gather.3.cloned.1.call-start
  7.2 2.0 %copy.51 = bf16[128,1536]{0,1:T(8,128)(2,1)} copy(bf16[128,1536]{1,0:T(8,128)(2,1)} %param.8) | data formatting | bytes 786432 | tf_op args[0]
  9.2 0.0 all-gather.3.cloned.1.call-update
  9.2 5.2 %all-to-all-start.1 = ((bf16[8,32,768]{2,1,0:T(8,128)(2,1)}), bf16[8,32,768]{2,1,0:T(8,128)(2,1)S(1)}, u32[]{:S(2)}, u32[]{:S(2)}) async-start(bf16[8,32,768]{2,1,0:T(8,128)(2,1)} %bitcast.63), calls=%async_computation.1 | async-start | bytes 786432 | tf_op jit(solution)/shard_map/all_to_all | solution.py:68
  14.4 0.0 all-gather.5.cloned.1.call-start
  14.4 0.7 fusion.14
  15.1 0.2 reduce-window.4
  15.3 1.1 %copy.54 = bf16[128,768]{0,1:T(8,128)(2,1)S(1)} copy(bf16[128,768]{1,0:T(8,128)(2,1)} %param.11) | data formatting | bytes 393216 | tf_op args[3]
  16.4 0.0 copy-done.1
  16.4 0.2 copy.55
  16.6 0.1 convert_reduce_fusion.1
  16.7 0.7 fusion.13
  17.4 0.1 select_reduce_fusion.1
  17.5 0.1 broadcast_compare_fusion
  17.6 0.3 fusion.8
  17.8 0.4 fusion.15
  18.2 4.5 %all-to-all-done.1 = bf16[8,32,768]{2,1,0:T(8,128)(2,1)S(1)} async-done(((bf16[8,32,768]{2,1,0:T(8,128)(2,1)}), bf16[8,32,768]{2,1,0:T(8,128)(2,1)S(1)}, u32[]{:S(2)}, u32[]{:S(2)}) %all-to-all-start.1) | async-done | bytes 393248 | tf_op jit(solution)/shard_map/all_to_all | solution.py:68
  22.7 0.9 gather_fusion
  23.6 0.2 copy.53
  23.8 0.0 copy-start.2
  23.8 1.0 %convolution_convert_fusion.1 = bf16[6,128,128]{2,1,0:T(8,128)(2,1)} fusion(bf16[128,6,128]{0,2,1:T(8,128)(2,1)S(1)} %bitcast.65, f32[6,128]{1,0:T(8,128)S(1)} %get-tuple-element.17, f32[6,128,128]{1,2,0:T(8,128)S(1)} %fusion.8), kind=kOutput, calls=%fused_computation.18 | convolution fusion | flops 25559936 | bytes 789504 | tf_op jit(solution)/shard_map/hqk,qhd->khd/dot_general | solution.py:45
  24.7 0.0 all-gather.5.cloned.1.call-update
  24.8 25.2 %all-gather.3.cloned.1.call-done = bf16[128,6144]{0,1:T(8,128)(2,1)} async-done(((bf16[128,1536]{0,1:T(8,128)(2,1)}), bf16[128,6144]{0,1:T(8,128)(2,1)}) %all-gather.3.cloned.1.call-update) | async-done | bytes 1572880 | tf_op jit(solution)/shard_map/all_gather | solution.py:72
  50.0 0.0 copy-start
  50.0 2.3 %convert_reduce_fusion = f32[128]{0:T(128)S(1)} fusion(bf16[128,6144]{0,1:T(8,128)(2,1)} %all-gather.3.cloned.1.call-done), kind=kLoop, calls=%fused_computation.3 | loop fusion | flops 1572736 | bytes 1573376 | tf_op jit(solution)/shard_map/reduce_sum | solution.py:11
  52.3 0.0 copy-done
  52.4 0.8 fusion.3
  53.2 0.0 copy-done.2
  53.2 1.9 %fusion.5 = bf16[128,6144]{0,1:T(8,128)(2,1)} fusion(bf16[128,6144]{0,1:T(8,128)(2,1)S(1)} %copy-done, f32[6144]{0:T(1024)S(1)} %copy-done.2, f32[128]{0:T(128)S(1)} %add_rsqrt_fusion, f32[128]{0:T(128)S(1)} %broadcast_multiply_fusion), kind=kLoop, calls=%fused_computation.8 | loop fusion | flops 3932160 | bytes 3171328 | tf_op jit(solution)/shard_map/convert_element_type | solution.py:14
  55.1 3.7 %all-to-all-start = ((bf16[8,128,768]{1,2,0:T(8,128)(2,1)}), bf16[8,128,768]{1,2,0:T(8,128)(2,1)S(1)}, u32[]{:S(2)}, u32[]{:S(2)}) async-start(bf16[8,128,768]{1,2,0:T(8,128)(2,1)} %bitcast.1), calls=%async_computation | async-start | bytes 3145728 | tf_op jit(solution)/shard_map/all_to_all | solution.py:79
  58.7 5.6 %convolution_convert_fusion = bf16[128,768]{1,0:T(8,128)(2,1)S(1)} fusion(bf16[128,6144]{0,1:T(8,128)(2,1)} %fusion.5, bf16[6144,768]{1,0:T(8,128)(2,1)} %param.10), kind=kOutput, calls=%fused_computation.17 | convolution fusion | flops 1208057856 | bytes 11206656 | tf_op jit(solution)/shard_map/dot_general | solution.py:73
  64.3 0.2 copy.59
  64.5 0.3 multiply_reduce_fusion
  64.8 0.1 multiply_convert_fusion
  64.9 0.3 fusion.9
  65.1 0.8 copy.65
  66.0 0.2 fusion.10
  66.2 0.8 copy.64
  67.0 17.6 %all-to-all-done = bf16[8,128,768]{1,2,0:T(8,128)(2,1)S(1)} async-done(((bf16[8,128,768]{1,2,0:T(8,128)(2,1)}), bf16[8,128,768]{1,2,0:T(8,128)(2,1)S(1)}, u32[]{:S(2)}, u32[]{:S(2)}) %all-to-all-start) | async-done | bytes 1572896 | tf_op jit(solution)/shard_map/all_to_all | solution.py:79
  84.6 0.7 copy.52
  85.3 0.8 all-gather.5.cloned.1.call-done
  86.1 4.2 %fusion.16 = f32[768,768]{1,0:T(8,128)} fusion(bf16[1024,768]{1,0:T(8,128)(2,1)S(1)} %bitcast.60, bf16[1024,768]{0,1:T(8,128)(2,1)} %all-gather.5.cloned.1.call-done), kind=kOutput, calls=%fused_computation.42 | convolution fusion | flops 1207959552 | bytes 5505024 | tf_op jit(solution)/shard_map/dot_general | solution.py:81
  (4 shorter events, 0.0 us)
Async XLA Ops:
  7.2 9.2 %copy-start.1 = (bf16[128,768]{1,0:T(8,128)(2,1)S(1)}, bf16[128,768]{1,0:T(8,128)(2,1)}, u32[]{:S(2)}) copy-start(bf16[128,768]{1,0:T(8,128)(2,1)} %param.12) | copy-start | bytes 589828
  7.2 42.8 %all-gather.3.cloned.1.call-start = ((), (), s32[]{:S(2)}) async-start(), calls=%async_computation.2 | async-start | bytes 1966080 | tf_op jit(solution)/shard_map/all_gather | solution.py:72
  9.2 13.5 %all-to-all-start.1 = ((bf16[8,32,768]{2,1,0:T(8,128)(2,1)}), bf16[8,32,768]{2,1,0:T(8,128)(2,1)S(1)}, u32[]{:S(2)}, u32[]{:S(2)}) async-start(bf16[8,32,768]{2,1,0:T(8,128)(2,1)} %bitcast.63), calls=%async_computation.1 | async-start | bytes 786432 | tf_op jit(solution)/shard_map/all_to_all | solution.py:68
  14.4 71.8 %all-gather.5.cloned.1.call-start = ((), (), s32[]{:S(2)}) async-start(), calls=%async_computation.3 | async-start | bytes 1769472 | tf_op jit(solution)/shard_map/all_gather | solution.py:77
  23.8 29.4 %copy-start.2 = (f32[6144]{0:T(1024)S(1)}, f32[6144]{0:T(1024)}, u32[]{:S(2)}) copy-start(f32[6144]{0:T(1024)} %param.9) | copy-start | bytes 73732
  50.0 2.4 %copy-start = (bf16[128,6144]{0,1:T(8,128)(2,1)S(1)}, bf16[128,6144]{0,1:T(8,128)(2,1)}, u32[]{:S(2)}) copy-start(bf16[128,6144]{0,1:T(8,128)(2,1)} %all-gather.3.cloned.1.call-done) | copy-start | bytes 4718596
  55.1 29.5 %all-to-all-start = ((bf16[8,128,768]{1,2,0:T(8,128)(2,1)}), bf16[8,128,768]{1,2,0:T(8,128)(2,1)S(1)}, u32[]{:S(2)}, u32[]{:S(2)}) async-start(bf16[8,128,768]{1,2,0:T(8,128)(2,1)} %bitcast.1), calls=%async_computation | async-start | bytes 3145728 | tf_op jit(solution)/shard_map/all_to_all | solution.py:79
Sparse Core Ops, SparseCore 0:
  10.2 39.7 all-gather.2
  51.9 34.2 all-gather.4

commit v2 on v1

--- a/solution.py
+++ b/solution.py
@@ -1,9 +1,14 @@
+import functools
+
 import jax
 import jax.numpy as jnp
 from jax import lax
+from jax.experimental import pallas as pl
+from jax.experimental.pallas import tpu as pltpu
 from jax.sharding import PartitionSpec as P
 
 HD = 128
+EXTRA = 16
 
 
 def normalize(rows, norm_gain):
@@ -84,9 +89,358 @@
     return weight_grad, query_grad, key_grad
 
 
+def split3(value):
+    high = value.astype(jnp.bfloat16)
+    rest = value - high.astype(jnp.float32)
+    middle = rest.astype(jnp.bfloat16)
+    low = (rest - middle.astype(jnp.float32)).astype(jnp.bfloat16)
+    return high, middle, low
+
+
+def pre_kernel(place, x_ref, own_ref, other_ref):
+    core = place[1]
+    rows, columns = x_ref.shape
+    half = columns // 2
+    values = x_ref[...].astype(jnp.float32)
+    mean = jnp.sum(values, axis=-1, keepdims=True) * (1.0 / columns)
+    centred = values - mean
+    spread = jnp.sum(centred * centred, axis=-1, keepdims=True)
+
+    @pl.when(core == 0)
+    def _():
+        own_ref[:rows, :] = x_ref[:, :half]
+        other_ref[...] = x_ref[:, half:]
+
+    @pl.when(core == 1)
+    def _():
+        own_ref[:rows, :] = x_ref[:, half:]
+        other_ref[...] = x_ref[:, :half]
+
+    lane = lax.broadcasted_iota(jnp.int32, (rows, 128), 1)
+    table = jnp.zeros((rows, 128), jnp.float32)
+    for index, part in enumerate(split3(mean) + split3(spread)):
+        table = jnp.where(lane == index, part.astype(jnp.float32), table)
+    own_ref[rows:, :] = jnp.zeros((EXTRA, half), jnp.bfloat16)
+    own_ref[rows:, :rows] = table.T[:EXTRA, :].astype(jnp.bfloat16)
+
+
+def image_plan(owner_ref, count_ref, device, row, images, capacity):
+    image = jnp.zeros(row.shape, jnp.int32)
+    position = jnp.zeros(row.shape, jnp.int32)
+    start = jnp.int32(0)
+    for index in range(images):
+        end = start + count_ref[device, index]
+        inside = (row >= start) & (row < end)
+        image = jnp.where(inside, index, image)
+        position = jnp.where(inside, owner_ref[device, index] * capacity + row - start, position)
+        start = end
+    return image, position
+
+
+def weights_kernel(images, place, owner_ref, count_ref, query_ref, key_ref, weights_ref):
+    rows, width = query_ref.shape
+    device = place[0] * 2 + place[1]
+    down = lax.broadcasted_iota(jnp.int32, (rows, rows), 0)
+    across = lax.broadcasted_iota(jnp.int32, (rows, rows), 1)
+    image_down, _ = image_plan(owner_ref, count_ref, device, down, images, 1)
+    image_across, _ = image_plan(owner_ref, count_ref, device, across, images, 1)
+    allowed = image_down == image_across
+    for head in range(width // HD):
+        columns = slice(head * HD, (head + 1) * HD)
+        scores = lax.dot_general(
+            query_ref[:, columns], key_ref[:, columns], (((1,), (1,)), ((), ())),
+            preferred_element_type=jnp.float32,
+        ) * (HD ** (-0.5))
+        scores = jnp.where(allowed, scores, -1000000000.0)
+        weights = jnp.exp(scores - jnp.max(scores, axis=-1, keepdims=True))
+        weights_ref[head] = weights / jnp.sum(weights, axis=-1, keepdims=True)
+
+
+def value_kernel(images, place, owner_ref, count_ref, slots_ref, weights_ref, cot_ref, value_ref):
+    slots, width = slots_ref.shape
+    rows = cot_ref.shape[0]
+    device = place[0] * 2 + place[1]
+    row = lax.broadcasted_iota(jnp.int32, (rows, slots), 0)
+    _, position = image_plan(owner_ref, count_ref, device, row, images, slots // images)
+    pick = position == lax.broadcasted_iota(jnp.int32, (rows, slots), 1)
+    pick = jnp.where(pick, 1.0, 0.0).astype(jnp.bfloat16)
+    cot_ref[...] = jnp.dot(
+        pick, slots_ref[...], preferred_element_type=jnp.float32
+    ).astype(jnp.bfloat16)
+    for head in range(width // HD):
+        columns = slice(head * HD, (head + 1) * HD)
+        value_ref[:, columns] = lax.dot_general(
+            weights_ref[head].astype(jnp.bfloat16), cot_ref[:, columns], (((0,), (0,)), ((), ())),
+            preferred_element_type=jnp.float32,
+        ).astype(jnp.bfloat16)
+
+
+def column_stats(mean, rstd):
+    rows = mean.shape[1]
+    both = jnp.concatenate([mean, rstd, jnp.zeros((126, rows), jnp.float32)], axis=0).T
+    return both[:, 0:1], both[:, 1:2]
+
+
+def norm_kernel(
+    first, place, gain_ref, stats_in, own, one, two, near, far, *rest
+):
+    if first:
+        stats_out, all_ref, x_ref, y_ref, xy_ref, source, sems = rest
+    else:
+        all_ref, x_ref, y_ref, xy_ref, source, sems = rest
+    chip, core, layer = place[0], place[1], place[2]
+    outer = (layer == 0) | (layer == 3)
+    rows = x_ref.shape[0]
+    for index, ref in enumerate((own, one, two)):
+        pltpu.make_async_copy(ref, source.at[index], sems.at[index]).start()
+
+    @pl.when(outer)
+    def _():
+        pltpu.make_async_copy(far, source.at[3], sems.at[3]).start()
+
+    @pl.when(jnp.logical_not(outer))
+    def _():
+        pltpu.make_async_copy(near, source.at[3], sems.at[3]).start()
+
+    for index, ref in enumerate((own, one, two, far)):
+        pltpu.make_async_copy(ref, source.at[index], sems.at[index]).wait()
+
+    if first:
+        means, spreads = [], []
+        for index in range(4):
+            part = source[index, rows:, :rows].astype(jnp.float32)
+            means.append(part[0:1] + part[1:2] + part[2:3])
+            spreads.append(part[3:4] + part[4:5] + part[5:6])
+        mean = (means[0] + means[1] + means[2] + means[3]) * 0.25
+        shift = sum((part - mean) * (part - mean) for part in means)
+        columns = 2 * x_ref.shape[1]
+        spread = spreads[0] + spreads[1] + spreads[2] + spreads[3] + shift * columns
+        rstd = lax.rsqrt(spread * (1.0 / (4 * columns)) + 1e-06)
+        stats_out[...] = jnp.concatenate([mean, rstd, jnp.zeros((6, rows), jnp.float32)], axis=0)
+    else:
+        mean, rstd = stats_in[0:1, :], stats_in[1:2, :]
+    mean, rstd = column_stats(mean, rstd)
+    for offset, ref in enumerate((None, x_ref, y_ref, xy_ref)):
+        block = chip ^ offset
+        values = source[block ^ layer, :rows, :].astype(jnp.float32)
+        gain = gain_ref[pl.ds(2 * block + core, 1), :]
+        normed = ((values - mean) * rstd * gain).astype(jnp.bfloat16)
+        all_ref[offset] = normed
+        if ref is not None:
+            ref[...] = normed
+
+
+def project_kernel(order, normed_ref, weight_ref, total_ref):
+    part = jnp.dot(normed_ref[0], weight_ref[...], preferred_element_type=jnp.float32)
+
+    @pl.when(pl.program_id(0) == 0)
+    def _():
+        total_ref[...] = part
+
+    @pl.when(pl.program_id(0) > 0)
+    def _():
+        total_ref[...] += part
+
+
+def backward_kernel(
+    order, normed_ref, weight_ref, first_ref, query_ref, key_ref, cot_ref, weights_ref, query_out, key_out, total
+):
+    step = pl.program_id(0)
+    part = jnp.dot(normed_ref[0], weight_ref[...], preferred_element_type=jnp.float32)
+
+    @pl.when(step == 0)
+    def _():
+        total[...] = first_ref[...] + part
+
+    @pl.when(step > 0)
+    def _():
+        total[...] += part
+
+    @pl.when(step == pl.num_programs(0) - 1)
+    def _():
+        scale = HD ** (-0.5)
+        for head in range(query_ref.shape[1] // HD):
+            columns = slice(head * HD, (head + 1) * HD)
+            values = total[:, columns].astype(jnp.bfloat16)
+            weights = weights_ref[head]
+            prob_grad = lax.dot_general(
+                cot_ref[:, columns], values, (((1,), (1,)), ((), ())), preferred_element_type=jnp.float32
+            )
+            centre = jnp.sum(weights * prob_grad, axis=-1, keepdims=True)
+            score_grad = (weights * (prob_grad - centre)).astype(jnp.bfloat16)
+            query_out[:, columns] = (
+                jnp.dot(score_grad, key_ref[:, columns], preferred_element_type=jnp.float32) * scale
+            ).astype(jnp.bfloat16)
+            key_out[:, columns] = (
+                lax.dot_general(
+                    score_grad, query_ref[:, columns], (((0,), (0,)), ((), ())),
+                    preferred_element_type=jnp.float32,
+                ) * scale
+            ).astype(jnp.bfloat16)
+
+
+def gradient_kernel(*refs):
+    n0, n1, n2, n3, v0, v1, v2, v3 = refs[:8]
+    normed = jnp.concatenate([n0[0], n1[...], n2[...], n3[...]], axis=0)
+    values = jnp.concatenate([v0[...], v1[...], v2[...], v3[...]], axis=0)
+    part = lax.dot_general(
+        normed, values, (((0,), (0,)), ((), ())), preferred_element_type=jnp.float32
+    )
+    if len(refs) == 10:
+        refs[9][...] = refs[8][...] + part
+    else:
+        refs[8][...] = part
+
+
+def shape(dims, dtype=jnp.bfloat16):
+    return jax.ShapeDtypeStruct(dims, dtype)
+
+
+def cost(flops, moved):
+    return pl.CostEstimate(flops=flops, bytes_accessed=moved, transcendentals=0)
+
+
+VMEM_LIMIT = 40 * 1024 * 1024
+SMEM = pl.BlockSpec(memory_space=pltpu.SMEM)
+WHOLE = pl.BlockSpec(memory_space=pltpu.VMEM)
+ANY = pl.BlockSpec(memory_space=pl.ANY)
+
+
+def call(kernel, name, out_shape, in_specs, out_specs, flops, moved, scratch=()):
+    return pl.pallas_call(
+        kernel,
+        name=name,
+        out_shape=out_shape,
+        in_specs=in_specs,
+        out_specs=out_specs,
+        scratch_shapes=list(scratch),
+        cost_estimate=cost(flops, moved),
+        compiler_params=pltpu.CompilerParams(vmem_limit_bytes=VMEM_LIMIT),
+    )
+
+
+def across(rows, distance):
+    return lax.ppermute(rows, "dp", [(i, i ^ distance) for i in range(8)])
+
+
+def line_gather(rows):
+    one = lax.ppermute(rows, "mp", [(0, 1), (1, 0), (2, 3), (3, 2)])
+    two = lax.ppermute(rows, "mp", [(0, 2), (2, 0), (1, 3), (3, 1)])
+    near = lax.ppermute(rows, "mp", [(1, 2), (2, 1)])
+    far = lax.ppermute(two, "mp", [(2, 3), (1, 0)])
+    return one, two, near, far
+
+
+def fast_body(
+    patches, norm_gain, value_weight, queries, key_vectors, head_cotangent, image_owner, patch_count
+):
+    rows, columns = patches.shape
+    half = columns // 2
+    width = queries.shape[1]
+    heads = width // HD
+    images = image_owner.shape[1]
+    slots = head_cotangent.shape[0]
+    device = lax.axis_index("dp").astype(jnp.int32)
+    chip, core, layer = device // 2, device % 2, lax.axis_index("mp").astype(jnp.int32)
+    place = jnp.stack([chip, core, layer])
+    block = shape((rows, half))
+
+    own, other = call(
+        pre_kernel, "split_rows", (shape((rows + EXTRA, half)), block), [SMEM, WHOLE], (WHOLE, WHOLE),
+        rows * columns * 6, rows * columns * 4,
+    )(place, patches)
+    received = lax.all_to_all(
+        head_cotangent.reshape(8, slots // 8, width), "dp", split_axis=0, concat_axis=0, tiled=True
+    ).reshape(slots, width)
+    first = line_gather(own)
+    mate = across(other, 1)
+    second = line_gather(mate)
+
+    weights = call(
+        functools.partial(weights_kernel, images), "attention_weights",
+        shape((heads, rows, rows), jnp.float32), [SMEM] * 3 + [WHOLE] * 2, WHOLE,
+        rows * rows * width * 2, rows * width * 8,
+    )(place, image_owner, patch_count, queries, key_vectors)
+    cotangent, value_rows = call(
+        functools.partial(value_kernel, images), "value_rows",
+        (shape((rows, width)), shape((rows, width))), [SMEM] * 3 + [WHOLE] * 2, (WHOLE, WHOLE),
+        rows * rows * width * 6, rows * width * 10,
+    )(place, image_owner, patch_count, received, weights)
+    chip_values = [value_rows] + [across(value_rows, distance) for distance in (2, 4, 6)]
+    mate_values = [across(part, 1) for part in chip_values]
+
+    gain = norm_gain.reshape(8, half)
+    stats_shape = shape((8, rows), jnp.float32)
+    stack = shape((4, rows, half))
+
+    def norm(is_first, stats, own_rows, gathered):
+        height = own_rows.shape[0]
+        outs = ((stats_shape,) if is_first else ()) + (stack, block, block, block)
+        return call(
+            functools.partial(norm_kernel, is_first), "norm_columns",
+            outs, [SMEM, WHOLE, WHOLE] + [ANY] * 5, (WHOLE,) * len(outs),
+            rows * half * 24, rows * half * 24,
+            (pltpu.VMEM((4, height, half), jnp.bfloat16), pltpu.SemaphoreType.DMA((4,))),
+        )(place, gain, stats, own_rows, *gathered)
+
+    def exchange(blocks):
+        return [across(part, distance) for part, distance in zip(blocks, (2, 4, 6))]
+
+    stats, first_all, *first_blocks = norm(True, jnp.zeros((8, rows), jnp.float32), own, first)
+    mate_stats = across(stats, 1)
+    first_columns = exchange(first_blocks)
+    second_all, *second_blocks = norm(False, mate_stats, mate, second)
+    second_columns = exchange(second_blocks)
+    other_all = across(second_all, 1)
+
+    offsets = jnp.arange(4, dtype=jnp.int32)
+    order = (chip ^ offsets) * 2
+    step_specs = [
+        pl.BlockSpec((1, rows, half), lambda j, order: (j, 0, 0)),
+        pl.BlockSpec((half, width), lambda j, order: (order[j], 0)),
+    ]
+
+    def full(dims):
+        return pl.BlockSpec(dims, lambda j, order: (0,) * len(dims))
+
+    flat = (rows, width)
+    total = pl.pallas_call(
+        project_kernel, name="project_own_half",
+        grid_spec=pltpu.PrefetchScalarGridSpec(
+            num_scalar_prefetch=1, grid=(4,), in_specs=step_specs, out_specs=full(flat)
+        ),
+        out_shape=shape(flat, jnp.float32),
+        cost_estimate=cost(rows * half * 8 * width, half * width * 8),
+        compiler_params=pltpu.CompilerParams(vmem_limit_bytes=VMEM_LIMIT),
+    )(order + core, first_all, value_weight)
+    query_grad, key_grad = pl.pallas_call(
+        backward_kernel, name="attention_backward",
+        grid_spec=pltpu.PrefetchScalarGridSpec(
+            num_scalar_prefetch=1, grid=(4,),
+            in_specs=step_specs + [full(flat)] * 4 + [full((heads, rows, rows))],
+            out_specs=(full(flat), full(flat)),
+            scratch_shapes=[pltpu.VMEM(flat, jnp.float32)],
+        ),
+        out_shape=(shape(flat), shape(flat)),
+        cost_estimate=cost(rows * half * 10 * width, half * width * 8),
+        compiler_params=pltpu.CompilerParams(vmem_limit_bytes=VMEM_LIMIT),
+    )(order + 1 - core, other_all, value_weight, total, queries, key_vectors, cotangent, weights)
+
+    grad_shape = shape((half, width), jnp.float32)
+    grad_cost = (8 * rows * half * width, 8 * rows * (half + width) + 8 * half * width)
+    partial_grad = call(
+        gradient_kernel, "gradient_first", grad_shape, [WHOLE] * 8, WHOLE, *grad_cost
+    )(first_all, *first_columns, *chip_values)
+    weight_grad = call(
+        gradient_kernel, "gradient_second", grad_shape, [WHOLE] * 9, WHOLE, *grad_cost
+    )(second_all, *second_columns, *mate_values, partial_grad)
+    return weight_grad, query_grad, key_grad
+
+
 def solution(mesh):
+    fast = mesh.shape["dp"] == 8 and mesh.shape["mp"] == 4
     return jax.shard_map(
-        general_body,
+        fast_body if fast else general_body,
         mesh=mesh,
         in_specs=(
             P("dp", "mp"),

time: 97.6 us -> 84.6 us (0.87)
  waiting for transfers between devices: 48.2 us -> 23.1 us
  starting transfers between devices: 8.91 us -> 33.8 us
  Pallas kernels: 0 us -> 16.6 us
  between operations: 14.2 us -> 0.93 us
  matrix products: 11.8 us -> 0 us
  other arithmetic: 6.65 us -> 0.09 us
  local copies, waits for them, and re-layouts: 7.44 us -> 9.31 us
    ppermute x0 -> x24, starting transfers between devices: none -> 30.1 us  [the longest x16 11.6 us: across(): return lax.ppermute(rows, 'dp', [(i, i ^ distance) for i in range(8)])]
    all_gather x2 -> x0, waiting for transfers between devices: 26.1 us -> none  [the longest x1 25.2 us: general_body(): lax.all_gather(patches, 'mp', axis=1, tiled=True)]
    ppermute x0 -> x24, waiting for transfers between devices: none -> 23.1 us  [the longest x16 16.2 us: across(): return lax.ppermute(rows, 'dp', [(i, i ^ distance) for i in range(8)])]
    all_to_all x2 -> x1, waiting for transfers between devices: 22.1 us -> 0.01 us  [fast_body(): lax.all_to_all(head_cotangent.reshape(8, slots // 8, width), 'dp', split_...]
    pallas_call x0 -> x9, Pallas kernels: none -> 16.6 us  [the longest x2 4.9 us: norm(): call(functools.partial(norm_kernel, is_first), 'norm_columns', outs, [SME...]
    dot_general x7 -> x0, matrix products: 11.8 us -> none  [the longest x1 5.64 us: general_body(): jnp.dot(normed, value_weight, preferred_element_type=jnp.float32)]
    all_to_all x2 -> x1, starting transfers between devices: 8.83 us -> 3.72 us  [fast_body(): lax.all_to_all(head_cotangent.reshape(8, slots // 8, width), 'dp', split_...]
    unnamed x11 -> x28, local copies, waits for them, and re-layouts: 4.86 us -> 9.3 us
  transfers between devices with their start and end apart: 4 -> 25, of which waited for: 4 -> 8; matrix products, arithmetic and copies ran while one was open for 20% -> 0% of each run, Pallas kernels for 0% -> 15%
where the time goes in v2:
time: 84.6 us; the launch traced here: 83.9 us
  starting transfers between devices  33.8 us (40%)
  waiting for transfers between devices  23.1 us (27%)
  Pallas kernels  16.6 us (20%)
  local copies, waits for them, and re-layouts  9.31 us (11%)
  between operations  0.93 us (1%)
    ppermute x16, waiting for transfers between devices, across(): return lax.ppermute(rows, 'dp', [(i, i ^ distance) for i in range(8)])  16.2 us
    ppermute x16, starting transfers between devices, across(): return lax.ppermute(rows, 'dp', [(i, i ^ distance) for i in range(8)])  11.6 us
    unnamed x28, local copies, waits for them, and re-layouts  9.3 us
    ppermute x2, starting transfers between devices, line_gather(): two = lax.ppermute(rows, 'mp', [(0, 2), (2, 0), (1, 3), (3, 1)])  7.97 us
    ppermute x2, waiting for transfers between devices, line_gather(): two = lax.ppermute(rows, 'mp', [(0, 2), (2, 0), (1, 3), (3, 1)])  6.91 us
    ppermute x2, starting transfers between devices, line_gather(): one = lax.ppermute(rows, 'mp', [(0, 1), (1, 0), (2, 3), (3, 2)])  6.6 us
    pallas_call x2, Pallas kernels, norm(): call(functools.partial(norm_kernel, is_first), 'norm_columns', outs, [SME...  4.9 us
    all_to_all x1, starting transfers between devices, fast_body(): lax.all_to_all(head_cotangent.reshape(8, slots // 8, width), 'dp', split_...  3.72 us
  transfers between devices with their start and end apart: 25, of which 8 were waited for; matrix products, arithmetic and copies ran while one was open for 0% of the time, Pallas kernels for 15%

profile of v2, /device:TPU:0, one launch (start us, length us, event | category | flops | bytes accessed | tf_op | source)
XLA Modules:
  0.0 83.9 jit_solution(12563466905789413365)
XLA Ops:
  0.7 0.1 pad_add_fusion.place
  0.7 1.0 %copy-done.5 = bf16[128,1536]{1,0:T(8,128)(2,1)S(1)} copy-done((bf16[128,1536]{1,0:T(8,128)(2,1)S(1)}, bf16[128,1536]{1,0:T(8,128)(2,1)}, u32[]{:S(2)}) %copy-start.5) | copy-done | bytes 393240
  1.7 0.9 %split_rows.1 = (bf16[144,768]{1,0:T(8,128)(2,1)S(1)}, bf16[128,768]{1,0:T(8,128)(2,1)S(1)}) custom-call(s32[3]{0:T(128)S(1)} %pad_add_fusion.place, bf16[128,1536]{1,0:T(8,128)(2,1)S(1)} %copy-done.5), custom_call_target="tpu_custom_call" | custom-call | flops 1179648 | bytes 786432 | tf_op jit(solution)/shard_map/split_rows/pallas_call | solution.py:348
  2.6 0.5 collective-permute-start.5
  3.1 3.6 %collective-permute-start.1 = (bf16[144,768]{1,0:T(8,128)(2,1)S(1)}, bf16[144,768]{1,0:T(8,128)(2,1)S(1)}, u32[]{:S(2)}, u32[]{:S(2)}) collective-permute-start(bf16[144,768]{1,0:T(8,128)(2,1)S(1)} %get-tuple-element.18.own), channel_id=1, source_target_pairs={{0,2},{2,0},{1,3},{3,1},{4,6},{6,4},{5,7},{7,5},{8,10},{10,8},{9,1... | collective-permute-start | bytes 663560 | tf_op jit(solution)/shard_map/ppermute | solution.py:328
  6.8 3.7 %all-to-all-start = ((bf16[8,32,768]{2,1,0:T(8,128)(2,1)}), bf16[8,32,768]{2,1,0:T(8,128)(2,1)S(1)}, u32[]{:S(2)}, u32[]{:S(2)}) async-start(bf16[8,32,768]{2,1,0:T(8,128)(2,1)} %bitcast.8), calls=%async_computation | async-start | bytes 786432 | tf_op jit(solution)/shard_map/all_to_all | solution.py:352
  10.5 0.7 collective-permute-start.2
  11.2 4.3 %collective-permute-start.7 = (bf16[128,768]{1,0:T(8,128)(2,1)S(1)}, bf16[128,768]{1,0:T(8,128)(2,1)S(1)}, u32[]{:S(2)}, u32[]{:S(2)}) collective-permute-start(bf16[128,768]{1,0:T(8,128)(2,1)S(1)} %collective-permute-done.5.own), channel_id=1, source_target_pairs={{0,2},{2,0},{1,3},{3,1},{4,6},{6,4},{5,7},{7,5},{8,10},{10,8},{9,1... | collective-permute-start | bytes 589832 | tf_op jit(solution)/shard_map/ppermute | solution.py:328
  15.5 6.3 %collective-permute-done.1.two = bf16[144,768]{1,0:T(8,128)(2,1)S(1)} collective-permute-done((bf16[144,768]{1,0:T(8,128)(2,1)S(1)}, bf16[144,768]{1,0:T(8,128)(2,1)S(1)}, u32[]{:S(2)}, u32[]{:S(2)}) %collective-permute-start.1) | collective-permute-done | bytes 221216 | tf_op jit(solution)/shard_map/ppermute | solution.py:328
  21.9 1.3 %collective-permute-start.3 = (bf16[144,768]{1,0:T(8,128)(2,1)S(1)}, bf16[144,768]{1,0:T(8,128)(2,1)S(1)}, u32[]{:S(2)}, u32[]{:S(2)}) collective-permute-start(bf16[144,768]{1,0:T(8,128)(2,1)S(1)} %collective-permute-done.1.two), channel_id=1, source_target_pairs={{2,3},{1,0},{6,7},{5,4},{10,11},{9,8},{14,15},{13,12},{18,19},{17,... | collective-permute-start | bytes 663560 | tf_op jit(solution)/shard_map/ppermute | solution.py:330
  23.2 0.7 collective-permute-start.8
  23.9 6.6 %collective-permute-start.6 = (bf16[128,768]{1,0:T(8,128)(2,1)S(1)}, bf16[128,768]{1,0:T(8,128)(2,1)S(1)}, u32[]{:S(2)}, u32[]{:S(2)}) collective-permute-start(bf16[128,768]{1,0:T(8,128)(2,1)S(1)} %collective-permute-done.5.own), channel_id=1, source_target_pairs={{0,1},{1,0},{2,3},{3,2},{4,5},{5,4},{6,7},{7,6},{8,9},{9,8},{10,11... | collective-permute-start | bytes 589832 | tf_op jit(solution)/shard_map/ppermute | solution.py:327
  30.4 0.6 collective-permute-done.7.two
  31.0 1.3 %collective-permute-start.9 = (bf16[128,768]{1,0:T(8,128)(2,1)S(1)}, bf16[128,768]{1,0:T(8,128)(2,1)S(1)}, u32[]{:S(2)}, u32[]{:S(2)}) collective-permute-start(bf16[128,768]{1,0:T(8,128)(2,1)S(1)} %collective-permute-done.7.two), channel_id=1, source_target_pairs={{2,3},{1,0},{6,7},{5,4},{10,11},{9,8},{14,15},{13,12},{18,19},{17,... | collective-permute-start | bytes 589832 | tf_op jit(solution)/shard_map/ppermute | solution.py:330
  32.3 0.0 copy-start.1
  32.3 0.9 %copy-done.1 = bf16[128,768]{1,0:T(8,128)(2,1)S(1)} copy-done((bf16[128,768]{1,0:T(8,128)(2,1)S(1)}, bf16[128,768]{1,0:T(8,128)(2,1)}, u32[]{:S(2)}) %copy-start.1) | copy-done | bytes 196632
  33.2 0.9 %copy-done.3 = bf16[128,768]{1,0:T(8,128)(2,1)S(1)} copy-done((bf16[128,768]{1,0:T(8,128)(2,1)S(1)}, bf16[128,768]{1,0:T(8,128)(2,1)}, u32[]{:S(2)}) %copy-start.3) | copy-done | bytes 196632
  34.2 0.7 copy-done.6
  34.9 0.7 copy-done.8
  35.5 1.1 %attention_weights.1.weights_ref = f32[6,128,128]{2,1,0:T(8,128)S(1)} custom-call(s32[3]{0:T(128)S(1)} %pad_add_fusion.place, s32[8,8]{1,0:T(8,128)S(1)} %copy-done.6, s32[8,8]{1,0:T(8,128)S(1)} %copy-done.8, bf16[128,768]{1,0:T(8,128)(2,1)S(1)} %copy-done.1, bf16[128,768]{1,0:T(8,128)(2,1)S(1)} %copy-done.3), custom_call_target="tpu_custom_call" | custom-call | flops 25165824 | bytes 786432 | tf_op jit(solution)/shard_map/attention_weights/pallas_call | solution.py:359
  36.7 0.0 copy-start.7
  36.7 0.7 copy-done.7
  37.4 0.7 copy-done.9
  38.1 1.1 %value_rows.1 = (bf16[128,768]{1,0:T(8,128)(2,1)S(1)}, bf16[128,768]{1,0:T(8,128)(2,1)S(1)}) custom-call(s32[3]{0:T(128)S(1)} %pad_add_fusion.place, s32[8,8]{1,0:T(8,128)S(1)} %copy-done.7, s32[8,8]{1,0:T(8,128)S(1)} %copy-done.9, bf16[256,768]{1,0:T(8,128)(2,1)S(1)} %bitcast.7, f32[6,128,128]{2,1,0:T(8,128)S(1)} %attention_weights.1.weights_ref), custom_call_target="tpu_custom_call" | custom-call | flops 75497472 | bytes 983040 | tf_op jit(solution)/shard_map/value_rows/pallas_call | solution.py:364
  39.2 0.0 collective-permute-done.one
  39.2 2.8 %collective-permute-start.18 = (bf16[128,768]{1,0:T(8,128)(2,1)S(1)}, bf16[128,768]{1,0:T(8,128)(2,1)S(1)}, u32[]{:S(2)}, u32[]{:S(2)}) collective-permute-start(bf16[128,768]{1,0:T(8,128)(2,1)S(1)} %get-tuple-element.25.refs_4_), channel_id=1, source_target_pairs={{0,24},{4,28},{8,16},{12,20},{16,8},{20,12},{24,0},{28,4},{1,25},{... | collective-permute-start | bytes 589832 | tf_op jit(solution)/shard_map/ppermute | solution.py:323
  42.0 0.0 collective-permute-done.3.far
  42.0 2.1 %norm_columns.2 = (f32[8,128]{1,0:T(8,128)S(1)}, bf16[4,128,768]{2,1,0:T(8,128)(2,1)S(1)}, bf16[128,768]{1,0:T(8,128)(2,1)S(1)}, bf16[128,768]{1,0:T(8,128)(2,1)S(1)}, bf16[128,768]{1,0:T(8,128)(2,1)S(1)}) custom-call(s32[3]{0:T(128)S(1)} %pad_add_fusion.place, f32[8,768]{1,0:T(8,128)S(1)} %reshape.15.gain_ref, f32[8,128]{1,0:T(8,128)S(1)} %broadcast_in_dim.3.stats_in, ...), custom_call_target="tpu_custom_call" | custom-call | flops 2359296 | bytes 2359296 | tf_op jit(solution)/shard_map/norm_columns/pallas_call | solution.py:379
  44.1 0.1 collective-permute-start.4
  44.2 0.0 collective-permute-done.8.near
  44.2 0.0 collective-permute-done.6.one
  44.2 1.1 %collective-permute-done.4.stats_in = f32[8,128]{1,0:T(8,128)S(1)} collective-permute-done((f32[8,128]{1,0:T(8,128)S(1)}, f32[8,128]{1,0:T(8,128)S(1)}, u32[]{:S(2)}, u32[]{:S(2)}) %collective-permute-start.4) | collective-permute-done | bytes 4128 | tf_op jit(solution)/shard_map/ppermute | solution.py:323
  45.4 0.0 collective-permute-done.9.far
  45.4 2.8 %norm_columns.3 = (bf16[4,128,768]{2,1,0:T(8,128)(2,1)S(1)}, bf16[128,768]{1,0:T(8,128)(2,1)}, bf16[128,768]{1,0:T(8,128)(2,1)}, bf16[128,768]{1,0:T(8,128)(2,1)}) custom-call(s32[3]{0:T(128)S(1)} %pad_add_fusion.place, f32[8,768]{1,0:T(8,128)S(1)} %reshape.15.gain_ref, f32[8,128]{1,0:T(8,128)S(1)} %collective-permute-done.4.stats_in, ...), custom_call_target="tpu_custom_call" | custom-call | flops 2359296 | bytes 2359296 | tf_op jit(solution)/shard_map/norm_columns/pallas_call | solution.py:379
  48.1 0.2 collective-permute-start.23
  48.4 0.5 collective-permute-start.16
  48.9 0.3 collective-permute-start.14
  49.2 0.0 collective-permute-done.18.refs_7_
  49.2 1.8 %collective-permute-start.20 = (bf16[128,768]{1,0:T(8,128)(2,1)S(1)}, bf16[128,768]{1,0:T(8,128)(2,1)S(1)}, u32[]{:S(2)}, u32[]{:S(2)}) collective-permute-start(bf16[128,768]{1,0:T(8,128)(2,1)S(1)} %get-tuple-element.27), channel_id=1, source_target_pairs={{0,8},{4,12},{8,0},{12,4},{16,24},{20,28},{24,16},{28,20},{1,9},{5... | collective-permute-start | bytes 589832 | tf_op jit(solution)/shard_map/ppermute | solution.py:323
  50.9 4.6 %collective-permute-done.16.refs_6_ = bf16[128,768]{1,0:T(8,128)(2,1)S(1)} collective-permute-done((bf16[128,768]{1,0:T(8,128)(2,1)S(1)}, bf16[128,768]{1,0:T(8,128)(2,1)S(1)}, u32[]{:S(2)}, u32[]{:S(2)}) %collective-permute-start.16) | collective-permute-done | bytes 196640 | tf_op jit(solution)/shard_map/ppermute | solution.py:323
  55.5 0.5 collective-permute-start.21
  56.0 0.6 collective-permute-done.14.refs_5_
  56.6 1.5 %collective-permute-start.22 = (bf16[128,768]{1,0:T(8,128)(2,1)S(1)}, bf16[128,768]{1,0:T(8,128)(2,1)S(1)}, u32[]{:S(2)}, u32[]{:S(2)}) collective-permute-start(bf16[128,768]{1,0:T(8,128)(2,1)S(1)} %get-tuple-element.29), channel_id=1, source_target_pairs={{0,24},{4,28},{8,16},{12,20},{16,8},{20,12},{24,0},{28,4},{1,25},{... | collective-permute-start | bytes 589832 | tf_op jit(solution)/shard_map/ppermute | solution.py:323
  58.1 0.0 collective-permute-done.13.refs_4_
  58.1 0.0 collective-permute-start.19
  58.1 2.7 %collective-permute-done.20.refs_1_ = bf16[128,768]{1,0:T(8,128)(2,1)S(1)} collective-permute-done((bf16[128,768]{1,0:T(8,128)(2,1)S(1)}, bf16[128,768]{1,0:T(8,128)(2,1)S(1)}, u32[]{:S(2)}, u32[]{:S(2)}) %collective-permute-start.20) | collective-permute-done | bytes 196640 | tf_op jit(solution)/shard_map/ppermute | solution.py:323
  60.9 0.0 collective-permute-start.17
  60.9 5.2 %collective-permute-done.21.refs_2_ = bf16[128,768]{1,0:T(8,128)(2,1)S(1)} collective-permute-done((bf16[128,768]{1,0:T(8,128)(2,1)S(1)}, bf16[128,768]{1,0:T(8,128)(2,1)S(1)}, u32[]{:S(2)}, u32[]{:S(2)}) %collective-permute-start.21) | collective-permute-done | bytes 196640 | tf_op jit(solution)/shard_map/ppermute | solution.py:323
  66.1 0.5 collective-permute-start.10
  66.6 0.3 collective-permute-start.11
  67.0 0.0 collective-permute-done.17.refs_6_
  67.0 2.6 %collective-permute-start.12 = (bf16[128,768]{1,0:T(8,128)(2,1)}, bf16[128,768]{1,0:T(8,128)(2,1)S(1)}, u32[]{:S(2)}, u32[]{:S(2)}) collective-permute-start(bf16[128,768]{1,0:T(8,128)(2,1)} %get-tuple-element.24), channel_id=1, source_target_pairs={{0,24},{4,28},{8,16},{12,20},{16,8},{20,12},{24,0},{28,4},{1,25},{... | collective-permute-start | bytes 589832 | tf_op jit(solution)/shard_map/ppermute | solution.py:323
  69.6 3.7 %copy-done = bf16[6144,768]{1,0:T(8,128)(2,1)S(1)} copy-done((bf16[6144,768]{1,0:T(8,128)(2,1)S(1)}, bf16[6144,768]{1,0:T(8,128)(2,1)}, u32[]{:S(2)}) %copy-start) | copy-done | bytes 9437208
  73.3 2.0 %project_own_half.1.first_ref = f32[128,768]{1,0:T(8,128)S(1)} custom-call(s32[4]{0:T(128)S(1)} %fusion.order, bf16[4,128,768]{2,1,0:T(8,128)(2,1)S(1)} %get-tuple-element.26.refs_0_.normed_ref, bf16[6144,768]{1,0:T(8,128)(2,1)S(1)} %copy-done), custom_call_target="tpu_custom_call" | custom-call | flops 603979776 | bytes 4718592 | tf_op jit(solution)/shard_map/project_own_half/pallas_call | solution.py:407
  75.3 0.0 slice-start.2
  75.3 0.8 gradient_first.1.refs_8_
  76.2 0.0 copy-start.2
  76.2 0.0 copy-start.4
  76.2 0.0 collective-permute-done.10.refs_1_
  76.2 1.9 %collective-permute-done.11.refs_2_ = bf16[128,768]{1,0:T(8,128)(2,1)S(1)} collective-permute-done((bf16[128,768]{1,0:T(8,128)(2,1)}, bf16[128,768]{1,0:T(8,128)(2,1)S(1)}, u32[]{:S(2)}, u32[]{:S(2)}) %collective-permute-start.11) | collective-permute-done | bytes 196640 | tf_op jit(solution)/shard_map/ppermute | solution.py:323
  78.1 0.0 collective-permute-done.12.refs_3_
  78.1 2.2 %gradient_second.1 = f32[768,768]{1,0:T(8,128)} custom-call(bf16[4,128,768]{2,1,0:T(8,128)(2,1)S(1)} %get-tuple-element.21.refs_0_, bf16[128,768]{1,0:T(8,128)(2,1)S(1)} %collective-permute-done.10.refs_1_, bf16[128,768]{1,0:T(8,128)(2,1)S(1)} %collective-permute-done.11.refs_2_, bf16[128,768]{1,0:T(8,128)(2,1)S(1)} %collective-permute-done.12.refs_3_, ...), custom_call_target="tpu_custom_call" | custom-call | flops 603979776 | bytes 6291456 | tf_op jit(solution)/shard_map/gradient_second/pallas_call | solution.py:434
  80.3 0.0 collective-permute-done.23.normed_ref
  80.4 3.5 %attention_backward.1 = (bf16[128,768]{1,0:T(8,128)(2,1)}, bf16[128,768]{1,0:T(8,128)(2,1)}) custom-call(s32[4]{0:T(128)S(1)} %add_subtract_fusion.order, bf16[4,128,768]{2,1,0:T(8,128)(2,1)S(1)} %collective-permute-done.23.normed_ref, bf16[6144,768]{1,0:T(8,128)(2,1)S(1)} %bitcast.6, f32[128,768]{1,0:T(8,128)S(1)} %project_own_half.1.first_ref, ...), custom_call_target="tpu_custom_call" | custom-call | flops 754974720 | bytes 4718592 | tf_op jit(solution)/shard_map/attention_backward/pallas_call | solution.py:416
  (29 shorter events, 0.1 us)
Async XLA Ops:
  0.6 41.3 %copy-start.10 = (f32[6144]{0:T(1024)S(1)}, f32[6144]{0:T(1024)}, u32[]{:S(2)}) copy-start(f32[6144]{0:T(1024)} %param.9) | copy-start | bytes 73732
  0.7 1.0 %copy-start.5 = (bf16[128,1536]{1,0:T(8,128)(2,1)S(1)}, bf16[128,1536]{1,0:T(8,128)(2,1)}, u32[]{:S(2)}) copy-start(bf16[128,1536]{1,0:T(8,128)(2,1)} %x_ref.1) | copy-start | bytes 1179652
  2.6 8.5 %collective-permute-start.5 = (bf16[128,768]{1,0:T(8,128)(2,1)S(1)}, bf16[128,768]{1,0:T(8,128)(2,1)S(1)}, u32[]{:S(2)}, u32[]{:S(2)}) collective-permute-start(bf16[128,768]{1,0:T(8,128)(2,1)S(1)} %get-tuple-element.20), channel_id=1, source_target_pairs={{0,4},{4,0},{8,12},{12,8},{16,20},{20,16},{24,28},{28,24},{1,5},{5... | collective-permute-start | bytes 589832 | tf_op jit(solution)/shard_map/ppermute | solution.py:323
  3.1 18.7 %collective-permute-start.1 = (bf16[144,768]{1,0:T(8,128)(2,1)S(1)}, bf16[144,768]{1,0:T(8,128)(2,1)S(1)}, u32[]{:S(2)}, u32[]{:S(2)}) collective-permute-start(bf16[144,768]{1,0:T(8,128)(2,1)S(1)} %get-tuple-element.18.own), channel_id=1, source_target_pairs={{0,2},{2,0},{1,3},{3,1},{4,6},{6,4},{5,7},{7,5},{8,10},{10,8},{9,1... | collective-permute-start | bytes 663560 | tf_op jit(solution)/shard_map/ppermute | solution.py:328
  6.8 29.9 %all-to-all-start = ((bf16[8,32,768]{2,1,0:T(8,128)(2,1)}), bf16[8,32,768]{2,1,0:T(8,128)(2,1)S(1)}, u32[]{:S(2)}, u32[]{:S(2)}) async-start(bf16[8,32,768]{2,1,0:T(8,128)(2,1)} %bitcast.8), calls=%async_computation | async-start | bytes 786432 | tf_op jit(solution)/shard_map/all_to_all | solution.py:352
  10.5 13.3 %collective-permute-start.2 = (bf16[144,768]{1,0:T(8,128)(2,1)S(1)}, bf16[144,768]{1,0:T(8,128)(2,1)S(1)}, u32[]{:S(2)}, u32[]{:S(2)}) collective-permute-start(bf16[144,768]{1,0:T(8,128)(2,1)S(1)} %get-tuple-element.18.own), channel_id=1, source_target_pairs={{1,2},{2,1},{5,6},{6,5},{9,10},{10,9},{13,14},{14,13},{17,18},{18,... | collective-permute-start | bytes 663560 | tf_op jit(solution)/shard_map/ppermute | solution.py:329
  11.2 19.8 %collective-permute-start.7 = (bf16[128,768]{1,0:T(8,128)(2,1)S(1)}, bf16[128,768]{1,0:T(8,128)(2,1)S(1)}, u32[]{:S(2)}, u32[]{:S(2)}) collective-permute-start(bf16[128,768]{1,0:T(8,128)(2,1)S(1)} %collective-permute-done.5.own), channel_id=1, source_target_pairs={{0,2},{2,0},{1,3},{3,1},{4,6},{6,4},{5,7},{7,5},{8,10},{10,8},{9,1... | collective-permute-start | bytes 589832 | tf_op jit(solution)/shard_map/ppermute | solution.py:328
  15.5 23.7 %collective-permute-start = (bf16[144,768]{1,0:T(8,128)(2,1)S(1)}, bf16[144,768]{1,0:T(8,128)(2,1)S(1)}, u32[]{:S(2)}, u32[]{:S(2)}) collective-permute-start(bf16[144,768]{1,0:T(8,128)(2,1)S(1)} %get-tuple-element.18.own), channel_id=1, source_target_pairs={{0,1},{1,0},{2,3},{3,2},{4,5},{5,4},{6,7},{7,6},{8,9},{9,8},{10,11... | collective-permute-start | bytes 663560 | tf_op jit(solution)/shard_map/ppermute | solution.py:327
  21.9 20.1 %collective-permute-start.3 = (bf16[144,768]{1,0:T(8,128)(2,1)S(1)}, bf16[144,768]{1,0:T(8,128)(2,1)S(1)}, u32[]{:S(2)}, u32[]{:S(2)}) collective-permute-start(bf16[144,768]{1,0:T(8,128)(2,1)S(1)} %collective-permute-done.1.two), channel_id=1, source_target_pairs={{2,3},{1,0},{6,7},{5,4},{10,11},{9,8},{14,15},{13,12},{18,19},{17,... | collective-permute-start | bytes 663560 | tf_op jit(solution)/shard_map/ppermute | solution.py:330
  23.2 21.1 %collective-permute-start.8 = (bf16[128,768]{1,0:T(8,128)(2,1)S(1)}, bf16[128,768]{1,0:T(8,128)(2,1)S(1)}, u32[]{:S(2)}, u32[]{:S(2)}) collective-permute-start(bf16[128,768]{1,0:T(8,128)(2,1)S(1)} %collective-permute-done.5.own), channel_id=1, source_target_pairs={{1,2},{2,1},{5,6},{6,5},{9,10},{10,9},{13,14},{14,13},{17,18},{18,... | collective-permute-start | bytes 589832 | tf_op jit(solution)/shard_map/ppermute | solution.py:329
  23.9 20.4 %collective-permute-start.6 = (bf16[128,768]{1,0:T(8,128)(2,1)S(1)}, bf16[128,768]{1,0:T(8,128)(2,1)S(1)}, u32[]{:S(2)}, u32[]{:S(2)}) collective-permute-start(bf16[128,768]{1,0:T(8,128)(2,1)S(1)} %collective-permute-done.5.own), channel_id=1, source_target_pairs={{0,1},{1,0},{2,3},{3,2},{4,5},{5,4},{6,7},{7,6},{8,9},{9,8},{10,11... | collective-permute-start | bytes 589832 | tf_op jit(solution)/shard_map/ppermute | solution.py:327
  31.0 14.4 %collective-permute-start.9 = (bf16[128,768]{1,0:T(8,128)(2,1)S(1)}, bf16[128,768]{1,0:T(8,128)(2,1)S(1)}, u32[]{:S(2)}, u32[]{:S(2)}) collective-permute-start(bf16[128,768]{1,0:T(8,128)(2,1)S(1)} %collective-permute-done.7.two), channel_id=1, source_target_pairs={{2,3},{1,0},{6,7},{5,4},{10,11},{9,8},{14,15},{13,12},{18,19},{17,... | collective-permute-start | bytes 589832 | tf_op jit(solution)/shard_map/ppermute | solution.py:330
  32.3 0.9 %copy-start.1 = (bf16[128,768]{1,0:T(8,128)(2,1)S(1)}, bf16[128,768]{1,0:T(8,128)(2,1)}, u32[]{:S(2)}) copy-start(bf16[128,768]{1,0:T(8,128)(2,1)} %query_ref.3) | copy-start | bytes 589828
  33.2 0.9 %copy-start.3 = (bf16[128,768]{1,0:T(8,128)(2,1)S(1)}, bf16[128,768]{1,0:T(8,128)(2,1)}, u32[]{:S(2)}) copy-start(bf16[128,768]{1,0:T(8,128)(2,1)} %key_ref.3) | copy-start | bytes 589828
  34.2 0.7 copy-start.6
  34.8 0.7 copy-start.8
  36.7 0.7 copy-start.7
  37.4 0.7 copy-start.9
  39.2 10.0 %collective-permute-start.18 = (bf16[128,768]{1,0:T(8,128)(2,1)S(1)}, bf16[128,768]{1,0:T(8,128)(2,1)S(1)}, u32[]{:S(2)}, u32[]{:S(2)}) collective-permute-start(bf16[128,768]{1,0:T(8,128)(2,1)S(1)} %get-tuple-element.25.refs_4_), channel_id=1, source_target_pairs={{0,24},{4,28},{8,16},{12,20},{16,8},{20,12},{24,0},{28,4},{1,25},{... | collective-permute-start | bytes 589832 | tf_op jit(solution)/shard_map/ppermute | solution.py:323
  44.1 1.2 %collective-permute-start.4 = (f32[8,128]{1,0:T(8,128)S(1)}, f32[8,128]{1,0:T(8,128)S(1)}, u32[]{:S(2)}, u32[]{:S(2)}) collective-permute-start(f32[8,128]{1,0:T(8,128)S(1)} %get-tuple-element.19), channel_id=1, source_target_pairs={{0,4},{4,0},{8,12},{12,8},{16,20},{20,16},{24,28},{28,24},{1,5},{5... | collective-permute-start | bytes 12296 | tf_op jit(solution)/shard_map/ppermute | solution.py:323
  48.1 32.2 %collective-permute-start.23 = (bf16[4,128,768]{2,1,0:T(8,128)(2,1)S(1)}, bf16[4,128,768]{2,1,0:T(8,128)(2,1)S(1)}, u32[]{:S(2)}, u32[]{:S(2)}) collective-permute-start(bf16[4,128,768]{2,1,0:T(8,128)(2,1)S(1)} %get-tuple-element.21.refs_0_), channel_id=1, source_target_pairs={{0,4},{4,0},{8,12},{12,8},{16,20},{20,16},{24,28},{28,24},{1,5},{5... | collective-permute-start | bytes 2359304 | tf_op jit(solution)/shard_map/ppermute | solution.py:323
  48.4 7.2 %collective-permute-start.16 = (bf16[128,768]{1,0:T(8,128)(2,1)S(1)}, bf16[128,768]{1,0:T(8,128)(2,1)S(1)}, u32[]{:S(2)}, u32[]{:S(2)}) collective-permute-start(bf16[128,768]{1,0:T(8,128)(2,1)S(1)} %get-tuple-element.25.refs_4_), channel_id=1, source_target_pairs={{0,16},{4,20},{8,24},{12,28},{16,0},{20,4},{24,8},{28,12},{1,17},{... | collective-permute-start | bytes 589832 | tf_op jit(solution)/shard_map/ppermute | solution.py:323
  48.9 7.8 %collective-permute-start.14 = (bf16[128,768]{1,0:T(8,128)(2,1)S(1)}, bf16[128,768]{1,0:T(8,128)(2,1)S(1)}, u32[]{:S(2)}, u32[]{:S(2)}) collective-permute-start(bf16[128,768]{1,0:T(8,128)(2,1)S(1)} %get-tuple-element.25.refs_4_), channel_id=1, source_target_pairs={{0,8},{4,12},{8,0},{12,4},{16,24},{20,28},{24,16},{28,20},{1,9},{5... | collective-permute-start | bytes 589832 | tf_op jit(solution)/shard_map/ppermute | solution.py:323
  49.2 9.0 %collective-permute-start.13 = (bf16[128,768]{1,0:T(8,128)(2,1)S(1)}, bf16[128,768]{1,0:T(8,128)(2,1)S(1)}, u32[]{:S(2)}, u32[]{:S(2)}) collective-permute-start(bf16[128,768]{1,0:T(8,128)(2,1)S(1)} %get-tuple-element.25.refs_4_), channel_id=1, source_target_pairs={{0,4},{4,0},{8,12},{12,8},{16,20},{20,16},{24,28},{28,24},{1,5},{5... | collective-permute-start | bytes 589832 | tf_op jit(solution)/shard_map/ppermute | solution.py:323
  49.2 11.7 %collective-permute-start.20 = (bf16[128,768]{1,0:T(8,128)(2,1)S(1)}, bf16[128,768]{1,0:T(8,128)(2,1)S(1)}, u32[]{:S(2)}, u32[]{:S(2)}) collective-permute-start(bf16[128,768]{1,0:T(8,128)(2,1)S(1)} %get-tuple-element.27), channel_id=1, source_target_pairs={{0,8},{4,12},{8,0},{12,4},{16,24},{20,28},{24,16},{28,20},{1,9},{5... | collective-permute-start | bytes 589832 | tf_op jit(solution)/shard_map/ppermute | solution.py:323
  55.5 10.6 %collective-permute-start.21 = (bf16[128,768]{1,0:T(8,128)(2,1)S(1)}, bf16[128,768]{1,0:T(8,128)(2,1)S(1)}, u32[]{:S(2)}, u32[]{:S(2)}) collective-permute-start(bf16[128,768]{1,0:T(8,128)(2,1)S(1)} %get-tuple-element.28), channel_id=1, source_target_pairs={{0,16},{4,20},{8,24},{12,28},{16,0},{20,4},{24,8},{28,12},{1,17},{... | collective-permute-start | bytes 589832 | tf_op jit(solution)/shard_map/ppermute | solution.py:323
  56.6 9.4 %collective-permute-start.22 = (bf16[128,768]{1,0:T(8,128)(2,1)S(1)}, bf16[128,768]{1,0:T(8,128)(2,1)S(1)}, u32[]{:S(2)}, u32[]{:S(2)}) collective-permute-start(bf16[128,768]{1,0:T(8,128)(2,1)S(1)} %get-tuple-element.29), channel_id=1, source_target_pairs={{0,24},{4,28},{8,16},{12,20},{16,8},{20,12},{24,0},{28,4},{1,25},{... | collective-permute-start | bytes 589832 | tf_op jit(solution)/shard_map/ppermute | solution.py:323
  58.1 8.5 %collective-permute-start.19 = (bf16[128,768]{1,0:T(8,128)(2,1)S(1)}, bf16[128,768]{1,0:T(8,128)(2,1)S(1)}, u32[]{:S(2)}, u32[]{:S(2)}) collective-permute-start(bf16[128,768]{1,0:T(8,128)(2,1)S(1)} %collective-permute-done.18.refs_7_), channel_id=1, source_target_pairs={{0,4},{4,0},{8,12},{12,8},{16,20},{20,16},{24,28},{28,24},{1,5},{5... | collective-permute-start | bytes 589832 | tf_op jit(solution)/shard_map/ppermute | solution.py:323
  60.9 6.1 %collective-permute-start.17 = (bf16[128,768]{1,0:T(8,128)(2,1)S(1)}, bf16[128,768]{1,0:T(8,128)(2,1)S(1)}, u32[]{:S(2)}, u32[]{:S(2)}) collective-permute-start(bf16[128,768]{1,0:T(8,128)(2,1)S(1)} %collective-permute-done.16.refs_6_), channel_id=1, source_target_pairs={{0,4},{4,0},{8,12},{12,8},{16,20},{20,16},{24,28},{28,24},{1,5},{5... | collective-permute-start | bytes 589832 | tf_op jit(solution)/shard_map/ppermute | solution.py:323
  66.1 10.1 %collective-permute-start.15 = (bf16[128,768]{1,0:T(8,128)(2,1)S(1)}, bf16[128,768]{1,0:T(8,128)(2,1)S(1)}, u32[]{:S(2)}, u32[]{:S(2)}) collective-permute-start(bf16[128,768]{1,0:T(8,128)(2,1)S(1)} %collective-permute-done.14.refs_5_), channel_id=1, source_target_pairs={{0,4},{4,0},{8,12},{12,8},{16,20},{20,16},{24,28},{28,24},{1,5},{5... | collective-permute-start | bytes 589832 | tf_op jit(solution)/shard_map/ppermute | solution.py:323
  66.1 10.1 %collective-permute-start.10 = (bf16[128,768]{1,0:T(8,128)(2,1)}, bf16[128,768]{1,0:T(8,128)(2,1)S(1)}, u32[]{:S(2)}, u32[]{:S(2)}) collective-permute-start(bf16[128,768]{1,0:T(8,128)(2,1)} %get-tuple-element.22), channel_id=1, source_target_pairs={{0,8},{4,12},{8,0},{12,4},{16,24},{20,28},{24,16},{28,20},{1,9},{5... | collective-permute-start | bytes 589832 | tf_op jit(solution)/shard_map/ppermute | solution.py:323
  66.6 11.5 %collective-permute-start.11 = (bf16[128,768]{1,0:T(8,128)(2,1)}, bf16[128,768]{1,0:T(8,128)(2,1)S(1)}, u32[]{:S(2)}, u32[]{:S(2)}) collective-permute-start(bf16[128,768]{1,0:T(8,128)(2,1)} %get-tuple-element.23), channel_id=1, source_target_pairs={{0,16},{4,20},{8,24},{12,28},{16,0},{20,4},{24,8},{28,12},{1,17},{... | collective-permute-start | bytes 589832 | tf_op jit(solution)/shard_map/ppermute | solution.py:323
  67.0 11.1 %collective-permute-start.12 = (bf16[128,768]{1,0:T(8,128)(2,1)}, bf16[128,768]{1,0:T(8,128)(2,1)S(1)}, u32[]{:S(2)}, u32[]{:S(2)}) collective-permute-start(bf16[128,768]{1,0:T(8,128)(2,1)} %get-tuple-element.24), channel_id=1, source_target_pairs={{0,24},{4,28},{8,16},{12,20},{16,8},{20,12},{24,0},{28,4},{1,25},{... | collective-permute-start | bytes 589832 | tf_op jit(solution)/shard_map/ppermute | solution.py:323
  69.6 3.7 %copy-start = (bf16[6144,768]{1,0:T(8,128)(2,1)S(1)}, bf16[6144,768]{1,0:T(8,128)(2,1)}, u32[]{:S(2)}) copy-start(bf16[6144,768]{1,0:T(8,128)(2,1)} %weight_ref.3) | copy-start | bytes 28311556
  73.3 7.1 %slice-start = ((s8[9437184]{0:T(1024)(128)(4,1)}), s8[4194304]{0:T(1024)(128)(4,1)S(1)}, s32[]{:S(2)}) async-start(s8[9437184]{0:T(1024)(128)(4,1)} %bitcast.5), calls=%async_computation.1 | async-start | bytes 8388608
  73.3 7.1 %slice-start.1 = ((s8[9437184]{0:T(1024)(128)(4,1)}), s8[4194304]{0:T(1024)(128)(4,1)S(1)}, s32[]{:S(2)}) async-start(s8[9437184]{0:T(1024)(128)(4,1)} %bitcast.5), calls=%async_computation.2 | async-start | bytes 8388608
  75.3 5.0 %slice-start.2 = ((s8[9437184]{0:T(1024)(128)(4,1)}), s8[1048576]{0:T(1024)(128)(4,1)S(1)}, s32[]{:S(2)}) async-start(s8[9437184]{0:T(1024)(128)(4,1)} %bitcast.5), calls=%async_computation.3 | async-start | bytes 2097152
  76.2 4.2 %copy-start.2 = (bf16[128,768]{1,0:T(8,128)(2,1)S(1)}, bf16[128,768]{1,0:T(8,128)(2,1)}, u32[]{:S(2)}) copy-start(bf16[128,768]{1,0:T(8,128)(2,1)} %query_ref.3) | copy-start | bytes 589828
  76.2 4.2 %copy-start.4 = (bf16[128,768]{1,0:T(8,128)(2,1)S(1)}, bf16[128,768]{1,0:T(8,128)(2,1)}, u32[]{:S(2)}) copy-start(bf16[128,768]{1,0:T(8,128)(2,1)} %key_ref.3) | copy-start | bytes 589828

commit v3 on v1

--- a/solution.py
+++ b/solution.py
@@ -1,9 +1,15 @@
+import functools
+
 import jax
 import jax.numpy as jnp
 from jax import lax
+from jax.experimental import pallas as pl
+from jax.experimental.pallas import tpu as pltpu
 from jax.sharding import PartitionSpec as P
 
 HD = 128
+HEADER = 8
+LATE = (1, 3, 5)
 
 
 def normalize(rows, norm_gain):
@@ -84,9 +90,292 @@
     return weight_grad, query_grad, key_grad
 
 
+def image_plan(info, row, images, capacity):
+    image = jnp.zeros(row.shape, jnp.int32)
+    position = jnp.zeros(row.shape, jnp.int32)
+    start = jnp.int32(0)
+    for index in range(images):
+        end = start + info[HEADER + images + index]
+        inside = (row >= start) & (row < end)
+        image = jnp.where(inside, index, image)
+        position = jnp.where(inside, info[HEADER + index] * capacity + row - start, position)
+        start = end
+    return image, position
+
+
+def weights_kernel(images, info, gain_in, query_ref, key_ref, weights_ref, gain_ref):
+    gain_ref[...] = gain_in[...]
+    rows, width = query_ref.shape
+    down = lax.broadcasted_iota(jnp.int32, (rows, rows), 0)
+    across = lax.broadcasted_iota(jnp.int32, (rows, rows), 1)
+    allowed = image_plan(info, down, images, 1)[0] == image_plan(info, across, images, 1)[0]
+    for head in range(width // HD):
+        columns = slice(head * HD, (head + 1) * HD)
+        scores = lax.dot_general(
+            query_ref[:, columns], key_ref[:, columns], (((1,), (1,)), ((), ())),
+            preferred_element_type=jnp.float32,
+        ) * (HD ** (-0.5))
+        scores = jnp.where(allowed, scores, -1000000000.0)
+        weights = jnp.exp(scores - jnp.max(scores, axis=-1, keepdims=True))
+        weights_ref[head] = weights / jnp.sum(weights, axis=-1, keepdims=True)
+
+
+def value_kernel(images, info, slots_ref, weights_ref, cot_ref, value_ref):
+    slots, width = slots_ref.shape
+    rows = cot_ref.shape[0]
+    row = lax.broadcasted_iota(jnp.int32, (rows, slots), 0)
+    _, position = image_plan(info, row, images, slots // images)
+    pick = position == lax.broadcasted_iota(jnp.int32, (rows, slots), 1)
+    pick = jnp.where(pick, 1.0, 0.0).astype(jnp.bfloat16)
+    cot_ref[...] = jnp.dot(
+        pick, slots_ref[...], preferred_element_type=jnp.float32
+    ).astype(jnp.bfloat16)
+    for head in range(width // HD):
+        columns = slice(head * HD, (head + 1) * HD)
+        value_ref[:, columns] = lax.dot_general(
+            weights_ref[head].astype(jnp.bfloat16), cot_ref[:, columns], (((0,), (0,)), ((), ())),
+            preferred_element_type=jnp.float32,
+        ).astype(jnp.bfloat16)
+
+
+def spread_of(values):
+    mean = jnp.sum(values, axis=-1, keepdims=True) * (1.0 / values.shape[1])
+    centred = values - mean
+    return mean, jnp.sum(centred * centred, axis=-1, keepdims=True)
+
+
+def stats_kernel(own, one, two, stats_ref):
+    rows = own.shape[0]
+    lane = lax.broadcasted_iota(jnp.int32, (rows, 128), 1)
+    table = jnp.zeros((rows, 128), jnp.float32)
+    for index, ref in enumerate((own, one, two)):
+        mean, spread = spread_of(ref[...].astype(jnp.float32))
+        table = jnp.where(lane == index, mean, table)
+        table = jnp.where(lane == index + 3, spread, table)
+    stats_ref[...] = table
+
+
+def norm_kernel(info, stats_ref, gain_ref, own, one, two, near, far, *rest):
+    values, outs, (packed_ref, source, sems) = rest[:4], rest[4:12], rest[12:]
+    device, layer = 2 * info[0] + info[1], info[2]
+    outer = (layer == 0) | (layer == 3)
+    rows, half = outs[0].shape
+
+    def copy(index, ref):
+        return pltpu.make_async_copy(ref, source.at[index], sems.at[index])
+
+    @pl.when(outer)
+    def _():
+        copy(3, far).start()
+
+    @pl.when(jnp.logical_not(outer))
+    def _():
+        copy(3, near).start()
+
+    for index, ref in enumerate((own, one, two)):
+        copy(index, ref).start()
+    for index, ref in enumerate(values):
+        packed_ref[index] = ref[...]
+    copy(3, far).wait()
+    columns = 8 * half
+    last_mean, last_spread = spread_of(source[3].astype(jnp.float32))
+    table = stats_ref[...]
+    means = [table[:, index:index + 1] for index in range(3)] + [last_mean]
+    mean = sum(means) * 0.25
+    shift = sum((part - mean) * (part - mean) for part in means) * (2 * half)
+    spread = table[:, 3:4] + table[:, 4:5] + table[:, 5:6] + last_spread + shift
+    rstd = lax.rsqrt(spread * (1.0 / columns) + 1e-06)
+    for index, ref in enumerate((own, one, two)):
+        copy(index, ref).wait()
+
+    for offset, out in enumerate(outs):
+        block = device ^ offset
+        start = pl.multiple_of((block % 2) * half, half)
+        values = source[(block // 2) ^ layer, :, pl.ds(start, half)]
+        gain = gain_ref[pl.ds(block, 1), :]
+        out[...] = ((values.astype(jnp.float32) - mean) * rstd * gain).astype(jnp.bfloat16)
+
+
+def backward_kernel(info, weight_ref, query_ref, key_ref, cot_ref, weights_ref, *refs):
+    normed, (query_out, key_out, total) = refs[:8], refs[8:]
+    device = 2 * info[0] + info[1]
+    half = normed[0].shape[1]
+    for offset, ref in enumerate(normed):
+        start = pl.multiple_of((device ^ offset) * half, half)
+        part = jnp.dot(ref[...], weight_ref[pl.ds(start, half), :], preferred_element_type=jnp.float32)
+        total[...] = total[...] + part if offset else part
+    scale = HD ** (-0.5)
+    for head in range(query_ref.shape[1] // HD):
+        columns = slice(head * HD, (head + 1) * HD)
+        weights = weights_ref[head]
+        prob_grad = lax.dot_general(
+            cot_ref[:, columns], total[:, columns].astype(jnp.bfloat16), (((1,), (1,)), ((), ())),
+            preferred_element_type=jnp.float32,
+        )
+        centre = jnp.sum(weights * prob_grad, axis=-1, keepdims=True)
+        score_grad = (weights * (prob_grad - centre)).astype(jnp.bfloat16)
+        query_out[:, columns] = (
+            jnp.dot(score_grad, key_ref[:, columns], preferred_element_type=jnp.float32) * scale
+        ).astype(jnp.bfloat16)
+        key_out[:, columns] = (
+            lax.dot_general(
+                score_grad, query_ref[:, columns], (((0,), (0,)), ((), ())),
+                preferred_element_type=jnp.float32,
+            ) * scale
+        ).astype(jnp.bfloat16)
+
+
+def joined(offsets, normed, chip_values, mate_values):
+    right = [mate_values[offset // 2] if offset % 2 else chip_values[offset // 2][...] for offset in offsets]
+    return jnp.concatenate([ref[...] for ref in normed], axis=0), jnp.concatenate(right, axis=0)
+
+
+def gradient_first_kernel(offsets, *refs):
+    count = len(offsets)
+    left, right = joined(offsets, refs[:count], refs[count:count + 4], refs[count + 4])
+    refs[count + 5][...] = lax.dot_general(
+        left, right, (((0,), (0,)), ((), ())), preferred_element_type=jnp.float32
+    )
+
+
+def gradient_last_kernel(offsets, before, *refs):
+    count = len(offsets)
+    left, right = joined(offsets, refs[:count], refs[count:count + 4], refs[count + 4])
+    out_ref, ready, done = refs[count + 5:]
+    blocks, _, columns = ready.shape
+    copies = []
+    for block in range(blocks):
+        part = slice(block * columns, (block + 1) * columns)
+        ready[block] = before[:, part] + lax.dot_general(
+            left, right[:, part], (((0,), (0,)), ((), ())), preferred_element_type=jnp.float32
+        )
+        copies.append(
+            pltpu.make_async_copy(ready.at[block], out_ref.at[:, pl.ds(block * columns, columns)], done.at[block])
+        )
+        copies[-1].start()
+    for copy in copies:
+        copy.wait()
+
+
+def shape(dims, dtype=jnp.bfloat16):
+    return jax.ShapeDtypeStruct(dims, dtype)
+
+
+VMEM_LIMIT = 24 * 1024 * 1024
+BIG = 56 * 1024 * 1024
+SMEM = pl.BlockSpec(memory_space=pltpu.SMEM)
+WHOLE = pl.BlockSpec(memory_space=pltpu.VMEM)
+ANY = pl.BlockSpec(memory_space=pl.ANY)
+
+
+def call(kernel, name, out_shape, in_specs, out_specs, scratch=(), limit=VMEM_LIMIT, after=()):
+    used = len(in_specs)
+
+    def body(*refs):
+        return kernel(*refs[:used], *refs[used + len(after):])
+
+    made = pl.pallas_call(
+        body,
+        name=name,
+        out_shape=out_shape,
+        in_specs=list(in_specs) + [ANY] * len(after),
+        out_specs=out_specs,
+        scratch_shapes=list(scratch),
+        cost_estimate=pl.CostEstimate(flops=1, bytes_accessed=1, transcendentals=0),
+        compiler_params=pltpu.CompilerParams(vmem_limit_bytes=limit),
+    )
+    return lambda *args: made(*args, *after)
+
+
+def across(rows, distance):
+    return lax.ppermute(rows, "dp", [(i, i ^ distance) for i in range(8)])
+
+
+def between_chips(blocks):
+    return lax.all_to_all(
+        blocks, "dp", split_axis=0, concat_axis=0, tiled=True,
+        axis_index_groups=[[0, 2, 4, 6], [1, 3, 5, 7]],
+    )
+
+
+def fast_body(
+    patches, norm_gain, value_weight, queries, key_vectors, head_cotangent, image_owner, patch_count
+):
+    rows, columns = patches.shape
+    half = columns // 2
+    width = queries.shape[1]
+    heads = width // HD
+    images = image_owner.shape[1]
+    slots = head_cotangent.shape[0]
+    device = lax.axis_index("dp").astype(jnp.int32)
+    place = [device // 2, device % 2, lax.axis_index("mp").astype(jnp.int32)]
+    info = jnp.concatenate([
+        jnp.stack(place + [jnp.int32(0)] * (HEADER - 3)),
+        lax.dynamic_index_in_dim(image_owner, device, 0, keepdims=False),
+        lax.dynamic_index_in_dim(patch_count, device, 0, keepdims=False),
+    ])
+    flat = (rows, width)
+
+    received = lax.all_to_all(
+        head_cotangent.reshape(8, slots // 8, width), "dp", split_axis=0, concat_axis=0, tiled=True
+    ).reshape(slots, width)
+    two = lax.ppermute(patches, "mp", [(0, 2), (2, 0), (1, 3), (3, 1)])
+    one = lax.ppermute(patches, "mp", [(0, 1), (1, 0), (2, 3), (3, 2)])
+
+    weights, gain = call(
+        functools.partial(weights_kernel, images), "attention_weights",
+        (shape((heads, rows, rows), jnp.float32), shape((8, half), jnp.float32)), [SMEM] + [WHOLE] * 3, (WHOLE, WHOLE),
+    )(info, norm_gain.reshape(8, half), queries, key_vectors)
+    cotangent, value_rows = call(
+        functools.partial(value_kernel, images), "value_rows",
+        (shape(flat), shape(flat)), [SMEM, WHOLE, WHOLE], (WHOLE, WHOLE),
+    )(info, received, weights)
+    middle, passed, first_one, _ = lax.optimization_barrier((patches, two, one, value_rows))
+    near = lax.ppermute(middle, "mp", [(1, 2), (2, 1)])
+    far = lax.ppermute(passed, "mp", [(2, 3), (1, 0)])
+    chip_values = [value_rows] + [across(value_rows, distance) for distance in (2, 4, 6)]
+
+    block = shape((rows, half))
+    stats = call(
+        stats_kernel, "partial_stats", shape((rows, 128), jnp.float32), [WHOLE] * 3, WHOLE,
+    )(middle, first_one, passed)
+    *normed, packed = call(
+        norm_kernel, "norm_rows", (block,) * 8 + (shape((4,) + flat),),
+        [SMEM, WHOLE, WHOLE] + [ANY] * 5 + [WHOLE] * 4, (WHOLE,) * 9,
+        (pltpu.VMEM((4, rows, columns), jnp.bfloat16), pltpu.SemaphoreType.DMA((4,))),
+    )(info, stats, gain, patches, one, two, near, far, *chip_values)
+
+    query_grad, key_grad = call(
+        backward_kernel, "attention_backward", (shape(flat), shape(flat)),
+        [SMEM] + [WHOLE] * 13, (WHOLE,) * 2, (pltpu.VMEM(flat, jnp.float32),),
+    )(info, value_weight, queries, key_vectors, cotangent, weights, *normed)
+    mate_values = across(packed, 1)
+
+    held = lax.optimization_barrier([normed[offset] for offset in LATE] + [query_grad])
+    sent = list(normed)
+    for offset, part in zip(LATE, held):
+        sent[offset] = part
+    moved = [sent[0]] + [across(sent[offset], offset) for offset in range(1, 8)]
+    early = [offset for offset in range(8) if offset not in LATE]
+    late = [offset for offset in range(8) if offset not in early]
+
+    grad = shape((half, width), jnp.float32)
+    partial = call(
+        functools.partial(gradient_first_kernel, early), "gradient_first", grad, [WHOLE] * (len(early) + 5), WHOLE
+    )(*[moved[offset] for offset in early], *chip_values, mate_values)
+    blocks = width // 256
+    weight_grad = call(
+        functools.partial(gradient_last_kernel, late), "gradient_last", grad, [WHOLE] * (len(late) + 6), ANY,
+        (pltpu.VMEM((blocks, half, 256), jnp.float32), pltpu.SemaphoreType.DMA((blocks,))),
+        after=(query_grad,),
+    )(partial, *[moved[offset] for offset in late], *chip_values, mate_values)
+    return weight_grad, query_grad, key_grad
+
+
 def solution(mesh):
+    fast = mesh.shape["dp"] == 8 and mesh.shape["mp"] == 4
     return jax.shard_map(
-        general_body,
+        fast_body if fast else general_body,
         mesh=mesh,
         in_specs=(
             P("dp", "mp"),

time: 97.6 us -> 65.2 us (0.67)
  waiting for transfers between devices: 48.2 us -> 21.1 us
  starting transfers between devices: 8.91 us -> 22.9 us
  between operations: 14.2 us -> 0.72 us
  Pallas kernels: 0 us -> 13 us
  matrix products: 11.8 us -> 0 us
  other arithmetic: 6.65 us -> 0 us
    all_gather x2 -> x0, waiting for transfers between devices: 26.1 us -> none  [the longest x1 25.2 us: general_body(): lax.all_gather(patches, 'mp', axis=1, tiled=True)]
    ppermute x0 -> x15, starting transfers between devices: none -> 19.2 us  [the longest x11 11.5 us: across(): return lax.ppermute(rows, 'dp', [(i, i ^ distance) for i in range(8)])]
    all_to_all x2 -> x1, waiting for transfers between devices: 22.1 us -> 3.93 us  [fast_body(): lax.all_to_all(head_cotangent.reshape(8, slots // 8, width), 'dp', split_...]
    ppermute x0 -> x15, waiting for transfers between devices: none -> 17.1 us  [the longest x11 11.5 us: across(): return lax.ppermute(rows, 'dp', [(i, i ^ distance) for i in range(8)])]
    pallas_call x0 -> x7, Pallas kernels: none -> 13 us  [call(): return lambda *args: made(*args, *after)]
    dot_general x7 -> x0, matrix products: 11.8 us -> none  [the longest x1 5.64 us: general_body(): jnp.dot(normed, value_weight, preferred_element_type=jnp.float32)]
    all_to_all x2 -> x1, starting transfers between devices: 8.83 us -> 3.72 us  [fast_body(): lax.all_to_all(head_cotangent.reshape(8, slots // 8, width), 'dp', split_...]
    reduce_sum x4 -> x0, other arithmetic: 3.35 us -> none  [the longest x1 2.35 us: normalize(): average = jnp.mean(values, axis=-1, keepdims=True)]
  transfers between devices with their start and end apart: 4 -> 16, of which waited for: 4 -> 9; matrix products, arithmetic and copies ran while one was open for 20% -> 2% of each run, Pallas kernels for 0% -> 13%
where the time goes in v3:
time: 65.2 us; the launch traced here: 64.8 us
  starting transfers between devices  22.9 us (35%)
  waiting for transfers between devices  21.1 us (32%)
  Pallas kernels  13 us (20%)
  local copies, waits for them, and re-layouts  7.09 us (11%)
  between operations  0.72 us (1%)
    pallas_call x7, Pallas kernels, call(): return lambda *args: made(*args, *after)  13 us
    ppermute x11, waiting for transfers between devices, across(): return lax.ppermute(rows, 'dp', [(i, i ^ distance) for i in range(8)])  11.5 us
    ppermute x11, starting transfers between devices, across(): return lax.ppermute(rows, 'dp', [(i, i ^ distance) for i in range(8)])  11.5 us
    unnamed x14, local copies, waits for them, and re-layouts  5.56 us
    all_to_all x1, waiting for transfers between devices, fast_body(): lax.all_to_all(head_cotangent.reshape(8, slots // 8, width), 'dp', split_...  3.93 us
    all_to_all x1, starting transfers between devices, fast_body(): lax.all_to_all(head_cotangent.reshape(8, slots // 8, width), 'dp', split_...  3.72 us
    ppermute x1, starting transfers between devices, fast_body(): one = lax.ppermute(patches, 'mp', [(0, 1), (1, 0), (2, 3), (3, 2)])  3.09 us
    ppermute x1, starting transfers between devices, fast_body(): two = lax.ppermute(patches, 'mp', [(0, 2), (2, 0), (1, 3), (3, 1)])  2.59 us
  transfers between devices with their start and end apart: 16, of which 9 were waited for; matrix products, arithmetic and copies ran while one was open for 2% of the time, Pallas kernels for 13%

profile of v3, /device:TPU:0, one launch (start us, length us, event | category | flops | bytes accessed | tf_op | source)
XLA Modules:
  0.0 64.8 jit_solution(12516133248749862137)
XLA Ops:
  0.6 0.0 copy-start.1
  0.6 3.1 %collective-permute-start.1 = (bf16[128,1536]{1,0:T(8,128)(2,1)}, bf16[128,1536]{1,0:T(8,128)(2,1)S(1)}, u32[]{:S(2)}, u32[]{:S(2)}) collective-permute-start(bf16[128,1536]{1,0:T(8,128)(2,1)} %refs_3_.4), channel_id=1, source_target_pairs={{0,1},{1,0},{2,3},{3,2},{4,5},{5,4},{6,7},{7,6},{8,9},{9,8},{10,11... | collective-permute-start | bytes 1179656 | tf_op jit(solution)/shard_map/ppermute | solution.py:323
  3.7 2.6 %collective-permute-start = (bf16[128,1536]{1,0:T(8,128)(2,1)}, bf16[128,1536]{1,0:T(8,128)(2,1)S(1)}, u32[]{:S(2)}, u32[]{:S(2)}) collective-permute-start(bf16[128,1536]{1,0:T(8,128)(2,1)} %refs_3_.4), channel_id=1, source_target_pairs={{0,2},{2,0},{1,3},{3,1},{4,6},{6,4},{5,7},{7,5},{8,10},{10,8},{9,1... | collective-permute-start | bytes 1179656 | tf_op jit(solution)/shard_map/ppermute | solution.py:322
  6.3 3.7 %all-to-all-start = ((bf16[8,32,768]{2,1,0:T(8,128)(2,1)}), bf16[8,32,768]{2,1,0:T(8,128)(2,1)S(1)}, u32[]{:S(2)}, u32[]{:S(2)}) async-start(bf16[8,32,768]{2,1,0:T(8,128)(2,1)} %bitcast.10), calls=%async_computation | async-start | bytes 786432 | tf_op jit(solution)/shard_map/all_to_all | solution.py:319
  10.0 0.7 %reshape.17.refs_1_ = f32[8,768]{1,0:T(8,128)S(1)} reshape(f32[6144]{0:T(1024)} %param.9) | data formatting | bytes 49152 | tf_op jit(solution)/shard_map/reshape | solution.py:328
  10.8 0.7 %dynamic-slice_bitcast_fusion = (s32[8]{0:T(128)S(1)}, s32[8]{0:T(128)S(1)}) fusion(s32[8,8]{1,0:T(8,128)} %param.15, s32[]{:T(128)S(6)} %select_n.18, s32[8,8]{1,0:T(8,128)} %param.14), kind=kLoop, calls=%fused_computation | loop fusion | bytes 132 | tf_op jit(solution)/shard_map/jit(dynamic_index_in_dim)/squeeze | solution.py:315
  11.5 0.1 concatenate.3.refs_0_
  11.6 0.0 copy-start.2
  11.6 0.9 %copy-done.2 = bf16[128,768]{1,0:T(8,128)(2,1)S(1)} copy-done((bf16[128,768]{1,0:T(8,128)(2,1)S(1)}, bf16[128,768]{1,0:T(8,128)(2,1)}, u32[]{:S(2)}) %copy-start.2) | copy-done | bytes 196632
  12.5 0.0 copy-start.4
  12.5 0.9 %copy-done.4 = bf16[128,768]{1,0:T(8,128)(2,1)S(1)} copy-done((bf16[128,768]{1,0:T(8,128)(2,1)S(1)}, bf16[128,768]{1,0:T(8,128)(2,1)}, u32[]{:S(2)}) %copy-start.4) | copy-done | bytes 196632
  13.4 1.0 %attention_weights.1 = (f32[6,128,128]{2,1,0:T(8,128)S(1)}, f32[8,768]{1,0:T(8,128)S(1)}) custom-call(s32[24]{0:T(128)S(1)} %concatenate.3.refs_0_, f32[8,768]{1,0:T(8,128)S(1)} %reshape.17.refs_1_, bf16[128,768]{1,0:T(8,128)(2,1)S(1)} %copy-done.2, bf16[128,768]{1,0:T(8,128)(2,1)S(1)} %copy-done.4), custom_call_target="tpu_custom_call" | custom-call | flops 1 | bytes 1 | tf_op jit(solution)/shard_map/attention_weights/pallas_call | solution.py:287
  14.5 3.9 %all-to-all-done = bf16[8,32,768]{2,1,0:T(8,128)(2,1)S(1)} async-done(((bf16[8,32,768]{2,1,0:T(8,128)(2,1)}), bf16[8,32,768]{2,1,0:T(8,128)(2,1)S(1)}, u32[]{:S(2)}, u32[]{:S(2)}) %all-to-all-start) | async-done | bytes 393248 | tf_op jit(solution)/shard_map/all_to_all | solution.py:319
  18.4 0.0 copy-start.3
  18.4 0.0 copy-start.5
  18.4 1.0 %value_rows.1 = (bf16[128,768]{1,0:T(8,128)(2,1)S(1)}, bf16[128,768]{1,0:T(8,128)(2,1)S(1)}) custom-call(s32[24]{0:T(128)S(1)} %concatenate.3.refs_0_, bf16[256,768]{1,0:T(8,128)(2,1)S(1)} %bitcast.9, f32[6,128,128]{2,1,0:T(8,128)S(1)} %get-tuple-element.24.refs_2_.refs_5_), custom_call_target="tpu_custom_call" | custom-call | flops 1 | bytes 1 | tf_op jit(solution)/shard_map/value_rows/pallas_call | solution.py:287
  19.4 2.0 %collective-permute-done.1.refs_1_.refs_4_ = bf16[128,1536]{1,0:T(8,128)(2,1)S(1)} collective-permute-done((bf16[128,1536]{1,0:T(8,128)(2,1)}, bf16[128,1536]{1,0:T(8,128)(2,1)S(1)}, u32[]{:S(2)}, u32[]{:S(2)}) %collective-permute-start.1) | collective-permute-done | bytes 393248 | tf_op jit(solution)/shard_map/ppermute | solution.py:323
  21.4 2.6 %collective-permute-done.refs_2_.refs_5_ = bf16[128,1536]{1,0:T(8,128)(2,1)S(1)} collective-permute-done((bf16[128,1536]{1,0:T(8,128)(2,1)}, bf16[128,1536]{1,0:T(8,128)(2,1)S(1)}, u32[]{:S(2)}, u32[]{:S(2)}) %collective-permute-start) | collective-permute-done | bytes 393248 | tf_op jit(solution)/shard_map/ppermute | solution.py:322
  23.9 0.7 %collective-permute-start.2 = (bf16[128,1536]{1,0:T(8,128)(2,1)}, bf16[128,1536]{1,0:T(8,128)(2,1)S(1)}, u32[]{:S(2)}, u32[]{:S(2)}) collective-permute-start(bf16[128,1536]{1,0:T(8,128)(2,1)} %refs_3_.4), channel_id=1, source_target_pairs={{1,2},{2,1},{5,6},{6,5},{9,10},{10,9},{13,14},{14,13},{17,18},{18,... | collective-permute-start | bytes 1179656 | tf_op jit(solution)/shard_map/ppermute | solution.py:334
  24.6 1.3 %collective-permute-start.3 = (bf16[128,1536]{1,0:T(8,128)(2,1)S(1)}, bf16[128,1536]{1,0:T(8,128)(2,1)S(1)}, u32[]{:S(2)}, u32[]{:S(2)}) collective-permute-start(bf16[128,1536]{1,0:T(8,128)(2,1)S(1)} %collective-permute-done.refs_2_.refs_5_), channel_id=1, source_target_pairs={{2,3},{1,0},{6,7},{5,4},{10,11},{9,8},{14,15},{13,12},{18,19},{17,... | collective-permute-start | bytes 1179656 | tf_op jit(solution)/shard_map/ppermute | solution.py:335
  25.9 2.5 %collective-permute-start.6 = (bf16[128,768]{1,0:T(8,128)(2,1)S(1)}, bf16[128,768]{1,0:T(8,128)(2,1)S(1)}, u32[]{:S(2)}, u32[]{:S(2)}) collective-permute-start(bf16[128,768]{1,0:T(8,128)(2,1)S(1)} %get-tuple-element.25.refs_8_.refs_5_.refs_4_), channel_id=1, source_target_pairs={{0,24},{4,28},{8,16},{12,20},{16,8},{20,12},{24,0},{28,4},{1,25},{... | collective-permute-start | bytes 589832 | tf_op jit(solution)/shard_map/ppermute | solution.py:291
  28.4 0.5 collective-permute-start.5
  28.9 0.5 collective-permute-start.4
  29.4 0.0 copy-done.1
  29.4 0.6 partial_stats.1.refs_1_
  30.1 2.7 %collective-permute-done.6.refs_11_.refs_8_.refs_7_ = bf16[128,768]{1,0:T(8,128)(2,1)S(1)} collective-permute-done((bf16[128,768]{1,0:T(8,128)(2,1)S(1)}, bf16[128,768]{1,0:T(8,128)(2,1)S(1)}, u32[]{:S(2)}, u32[]{:S(2)}) %collective-permute-start.6) | collective-permute-done | bytes 196640 | tf_op jit(solution)/shard_map/ppermute | solution.py:291
  32.8 2.0 %collective-permute-done.5.refs_10_.refs_7_.refs_6_ = bf16[128,768]{1,0:T(8,128)(2,1)S(1)} collective-permute-done((bf16[128,768]{1,0:T(8,128)(2,1)S(1)}, bf16[128,768]{1,0:T(8,128)(2,1)S(1)}, u32[]{:S(2)}, u32[]{:S(2)}) %collective-permute-start.5) | collective-permute-done | bytes 196640 | tf_op jit(solution)/shard_map/ppermute | solution.py:291
  34.8 0.0 collective-permute-done.4.refs_9_.refs_6_.refs_5_
  34.8 0.0 collective-permute-done.2.refs_6_
  34.8 1.1 %collective-permute-done.3.refs_7_ = bf16[128,1536]{1,0:T(8,128)(2,1)S(1)} collective-permute-done((bf16[128,1536]{1,0:T(8,128)(2,1)S(1)}, bf16[128,1536]{1,0:T(8,128)(2,1)S(1)}, u32[]{:S(2)}, u32[]{:S(2)}) %collective-permute-start.3) | collective-permute-done | bytes 393248 | tf_op jit(solution)/shard_map/ppermute | solution.py:335
  35.9 2.7 %norm_rows.1 = (bf16[128,768]{1,0:T(8,128)(2,1)S(1)}, bf16[128,768]{1,0:T(8,128)(2,1)S(1)}, bf16[128,768]{1,0:T(8,128)(2,1)S(1)}, bf16[128,768]{1,0:T(8,128)(2,1...) custom-call(s32[24]{0:T(128)S(1)} %concatenate.3.refs_0_, ...), custom_call_target="tpu_custom_call" | custom-call | flops 1 | bytes 1 | tf_op jit(solution)/shard_map/norm_rows/pallas_call | solution.py:287
  38.6 0.1 collective-permute-start.11
  38.6 1.6 %collective-permute-start.7 = (bf16[128,768]{1,0:T(8,128)(2,1)S(1)}, bf16[128,768]{1,0:T(8,128)(2,1)S(1)}, u32[]{:S(2)}, u32[]{:S(2)}) collective-permute-start(bf16[128,768]{1,0:T(8,128)(2,1)S(1)} %get-tuple-element.31.refs_8_), channel_id=1, source_target_pairs={{0,8},{4,12},{8,0},{12,4},{16,24},{20,28},{24,16},{28,20},{1,9},{5... | collective-permute-start | bytes 589832 | tf_op jit(solution)/shard_map/ppermute | solution.py:291
  40.2 1.5 %collective-permute-start.8 = (bf16[128,768]{1,0:T(8,128)(2,1)S(1)}, bf16[128,768]{1,0:T(8,128)(2,1)S(1)}, u32[]{:S(2)}, u32[]{:S(2)}) collective-permute-start(bf16[128,768]{1,0:T(8,128)(2,1)S(1)} %get-tuple-element.32.refs_10_), channel_id=1, source_target_pairs={{0,16},{4,20},{8,24},{12,28},{16,0},{20,4},{24,8},{28,12},{1,17},{... | collective-permute-start | bytes 589832 | tf_op jit(solution)/shard_map/ppermute | solution.py:291
  41.7 0.5 collective-permute-start.9
  42.2 1.7 %collective-permute-start.10 = (bf16[128,768]{1,0:T(8,128)(2,1)S(1)}, bf16[128,768]{1,0:T(8,128)(2,1)S(1)}, u32[]{:S(2)}, u32[]{:S(2)}) collective-permute-start(bf16[128,768]{1,0:T(8,128)(2,1)S(1)} %get-tuple-element.34.refs_13_), channel_id=1, source_target_pairs={{0,28},{4,24},{8,20},{12,16},{16,12},{20,8},{24,4},{28,0},{1,29},{... | collective-permute-start | bytes 589832 | tf_op jit(solution)/shard_map/ppermute | solution.py:291
  43.8 0.0 copy-done.3
  43.8 0.0 copy-done.5
  43.8 0.0 copy-start
  43.9 3.7 %copy-done = bf16[6144,768]{1,0:T(8,128)(2,1)S(1)} copy-done((bf16[6144,768]{1,0:T(8,128)(2,1)S(1)}, bf16[6144,768]{1,0:T(8,128)(2,1)}, u32[]{:S(2)}) %copy-start) | copy-done | bytes 9437208
  47.5 4.6 %attention_backward.1 = (bf16[128,768]{1,0:T(8,128)(2,1)}, bf16[128,768]{1,0:T(8,128)(2,1)}) custom-call(s32[24]{0:T(128)S(1)} %concatenate.3.refs_0_, bf16[6144,768]{1,0:T(8,128)(2,1)S(1)} %copy-done, bf16[128,768]{1,0:T(8,128)(2,1)S(1)} %copy-done.3, bf16[128,768]{1,0:T(8,128)(2,1)S(1)} %copy-done.5, bf16[128,768]{1,0:T(8,128)(2,1)S(1)} %get-tuple-element.39.refs_4_, ...), custom_call_target="tpu_custom_call" | custom-call | flops 1 | bytes 1 | tf_op jit(solution)/shard_map/attention_backward/pallas_call | solution.py:287
  52.1 0.0 copy-start.6
  52.1 0.0 collective-permute-done.7.refs_1_
  52.1 0.9 %collective-permute-start.12 = (bf16[128,768]{1,0:T(8,128)(2,1)S(1)}, bf16[128,768]{1,0:T(8,128)(2,1)S(1)}, u32[]{:S(2)}, u32[]{:S(2)}) collective-permute-start(bf16[128,768]{1,0:T(8,128)(2,1)S(1)} %get-tuple-element.41.refs_7_), channel_id=1, source_target_pairs={{0,4},{4,0},{8,12},{12,8},{16,20},{20,16},{24,28},{28,24},{1,5},{5... | collective-permute-start | bytes 589832 | tf_op jit(solution)/shard_map/ppermute | solution.py:291
  53.1 2.5 %collective-permute-done.8.refs_2_ = bf16[128,768]{1,0:T(8,128)(2,1)S(1)} collective-permute-done((bf16[128,768]{1,0:T(8,128)(2,1)S(1)}, bf16[128,768]{1,0:T(8,128)(2,1)S(1)}, u32[]{:S(2)}, u32[]{:S(2)}) %collective-permute-start.8) | collective-permute-done | bytes 196640 | tf_op jit(solution)/shard_map/ppermute | solution.py:291
  55.6 0.0 collective-permute-start.13
  55.6 0.0 collective-permute-done.9.refs_3_
  55.6 1.8 %collective-permute-start.14 = (bf16[128,768]{1,0:T(8,128)(2,1)S(1)}, bf16[128,768]{1,0:T(8,128)(2,1)S(1)}, u32[]{:S(2)}, u32[]{:S(2)}) collective-permute-start(bf16[128,768]{1,0:T(8,128)(2,1)S(1)} %get-tuple-element.43.refs_11_), channel_id=1, source_target_pairs={{0,20},{4,16},{8,28},{12,24},{16,4},{20,0},{24,12},{28,8},{1,21},{... | collective-permute-start | bytes 589832 | tf_op jit(solution)/shard_map/ppermute | solution.py:291
  57.4 0.0 collective-permute-done.10.refs_4_
  57.4 0.0 collective-permute-done.11.refs_9_.refs_8_
  57.4 1.1 %gradient_first.1.refs_0_ = f32[768,768]{1,0:T(8,128)S(1)} custom-call(bf16[128,768]{1,0:T(8,128)(2,1)S(1)} %get-tuple-element.30.refs_0_.refs_6_, bf16[128,768]{1,0:T(8,128)(2,1)S(1)} %collective-permute-done.7.refs_1_, bf16[128,768]{1,0:T(8,128)(2,1)S(1)} %collective-permute-done.8.refs_2_, bf16[128,768]{1,0:T(8,128)(2,1)S(1)} %collective-permute-done.9.refs_3_, ...), custom_call_target="tpu_custom_call" | custom-call | flops 1 | bytes 1 | tf_op jit(solution)/shard_map/gradient_first/pallas_call | solution.py:287
  58.5 0.0 collective-permute-done.12.refs_1_
  58.5 2.7 %collective-permute-done.13.refs_2_ = bf16[128,768]{1,0:T(8,128)(2,1)S(1)} collective-permute-done((bf16[128,768]{1,0:T(8,128)(2,1)S(1)}, bf16[128,768]{1,0:T(8,128)(2,1)S(1)}, u32[]{:S(2)}, u32[]{:S(2)}) %collective-permute-start.13) | collective-permute-done | bytes 196640 | tf_op jit(solution)/shard_map/ppermute | solution.py:291
  61.2 1.6 %collective-permute-done.14.refs_3_ = bf16[128,768]{1,0:T(8,128)(2,1)S(1)} collective-permute-done((bf16[128,768]{1,0:T(8,128)(2,1)S(1)}, bf16[128,768]{1,0:T(8,128)(2,1)S(1)}, u32[]{:S(2)}, u32[]{:S(2)}) %collective-permute-start.14) | collective-permute-done | bytes 196640 | tf_op jit(solution)/shard_map/ppermute | solution.py:291
  62.8 0.0 copy-done.6
  62.8 2.0 %gradient_last.1 = f32[768,768]{1,0:T(8,128)} custom-call(f32[768,768]{1,0:T(8,128)S(1)} %gradient_first.1.refs_0_, bf16[128,768]{1,0:T(8,128)(2,1)S(1)} %collective-permute-done.12.refs_1_, bf16[128,768]{1,0:T(8,128)(2,1)S(1)} %collective-permute-done.13.refs_2_, bf16[128,768]{1,0:T(8,128)(2,1)S(1)} %collective-permute-done.14.refs_3_, ...), custom_call_target="tpu_custom_call" | custom-call | flops 1 | bytes 1 | tf_op jit(solution)/shard_map/gradient_last/pallas_call | solution.py:287
  (1 shorter events, 0.0 us)
Async XLA Ops:
  0.6 28.8 %copy-start.1 = (bf16[128,1536]{1,0:T(8,128)(2,1)S(1)}, bf16[128,1536]{1,0:T(8,128)(2,1)}, u32[]{:S(2)}) copy-start(bf16[128,1536]{1,0:T(8,128)(2,1)} %refs_3_.4) | copy-start | bytes 1179652
  0.6 20.7 %collective-permute-start.1 = (bf16[128,1536]{1,0:T(8,128)(2,1)}, bf16[128,1536]{1,0:T(8,128)(2,1)S(1)}, u32[]{:S(2)}, u32[]{:S(2)}) collective-permute-start(bf16[128,1536]{1,0:T(8,128)(2,1)} %refs_3_.4), channel_id=1, source_target_pairs={{0,1},{1,0},{2,3},{3,2},{4,5},{5,4},{6,7},{7,6},{8,9},{9,8},{10,11... | collective-permute-start | bytes 1179656 | tf_op jit(solution)/shard_map/ppermute | solution.py:323
  3.7 20.2 %collective-permute-start = (bf16[128,1536]{1,0:T(8,128)(2,1)}, bf16[128,1536]{1,0:T(8,128)(2,1)S(1)}, u32[]{:S(2)}, u32[]{:S(2)}) collective-permute-start(bf16[128,1536]{1,0:T(8,128)(2,1)} %refs_3_.4), channel_id=1, source_target_pairs={{0,2},{2,0},{1,3},{3,1},{4,6},{6,4},{5,7},{7,5},{8,10},{10,8},{9,1... | collective-permute-start | bytes 1179656 | tf_op jit(solution)/shard_map/ppermute | solution.py:322
  6.3 12.1 %all-to-all-start = ((bf16[8,32,768]{2,1,0:T(8,128)(2,1)}), bf16[8,32,768]{2,1,0:T(8,128)(2,1)S(1)}, u32[]{:S(2)}, u32[]{:S(2)}) async-start(bf16[8,32,768]{2,1,0:T(8,128)(2,1)} %bitcast.10), calls=%async_computation | async-start | bytes 786432 | tf_op jit(solution)/shard_map/all_to_all | solution.py:319
  11.6 0.9 %copy-start.2 = (bf16[128,768]{1,0:T(8,128)(2,1)S(1)}, bf16[128,768]{1,0:T(8,128)(2,1)}, u32[]{:S(2)}) copy-start(bf16[128,768]{1,0:T(8,128)(2,1)} %refs_2_.3) | copy-start | bytes 589828
  12.5 0.9 %copy-start.4 = (bf16[128,768]{1,0:T(8,128)(2,1)S(1)}, bf16[128,768]{1,0:T(8,128)(2,1)}, u32[]{:S(2)}) copy-start(bf16[128,768]{1,0:T(8,128)(2,1)} %refs_3_.5) | copy-start | bytes 589828
  18.4 25.5 %copy-start.3 = (bf16[128,768]{1,0:T(8,128)(2,1)S(1)}, bf16[128,768]{1,0:T(8,128)(2,1)}, u32[]{:S(2)}) copy-start(bf16[128,768]{1,0:T(8,128)(2,1)} %refs_2_.3) | copy-start | bytes 589828
  18.4 25.5 %copy-start.5 = (bf16[128,768]{1,0:T(8,128)(2,1)S(1)}, bf16[128,768]{1,0:T(8,128)(2,1)}, u32[]{:S(2)}) copy-start(bf16[128,768]{1,0:T(8,128)(2,1)} %refs_3_.5) | copy-start | bytes 589828
  23.9 10.9 %collective-permute-start.2 = (bf16[128,1536]{1,0:T(8,128)(2,1)}, bf16[128,1536]{1,0:T(8,128)(2,1)S(1)}, u32[]{:S(2)}, u32[]{:S(2)}) collective-permute-start(bf16[128,1536]{1,0:T(8,128)(2,1)} %refs_3_.4), channel_id=1, source_target_pairs={{1,2},{2,1},{5,6},{6,5},{9,10},{10,9},{13,14},{14,13},{17,18},{18,... | collective-permute-start | bytes 1179656 | tf_op jit(solution)/shard_map/ppermute | solution.py:334
  24.6 11.3 %collective-permute-start.3 = (bf16[128,1536]{1,0:T(8,128)(2,1)S(1)}, bf16[128,1536]{1,0:T(8,128)(2,1)S(1)}, u32[]{:S(2)}, u32[]{:S(2)}) collective-permute-start(bf16[128,1536]{1,0:T(8,128)(2,1)S(1)} %collective-permute-done.refs_2_.refs_5_), channel_id=1, source_target_pairs={{2,3},{1,0},{6,7},{5,4},{10,11},{9,8},{14,15},{13,12},{18,19},{17,... | collective-permute-start | bytes 1179656 | tf_op jit(solution)/shard_map/ppermute | solution.py:335
  25.9 6.9 %collective-permute-start.6 = (bf16[128,768]{1,0:T(8,128)(2,1)S(1)}, bf16[128,768]{1,0:T(8,128)(2,1)S(1)}, u32[]{:S(2)}, u32[]{:S(2)}) collective-permute-start(bf16[128,768]{1,0:T(8,128)(2,1)S(1)} %get-tuple-element.25.refs_8_.refs_5_.refs_4_), channel_id=1, source_target_pairs={{0,24},{4,28},{8,16},{12,20},{16,8},{20,12},{24,0},{28,4},{1,25},{... | collective-permute-start | bytes 589832 | tf_op jit(solution)/shard_map/ppermute | solution.py:291
  28.4 6.4 %collective-permute-start.5 = (bf16[128,768]{1,0:T(8,128)(2,1)S(1)}, bf16[128,768]{1,0:T(8,128)(2,1)S(1)}, u32[]{:S(2)}, u32[]{:S(2)}) collective-permute-start(bf16[128,768]{1,0:T(8,128)(2,1)S(1)} %get-tuple-element.25.refs_8_.refs_5_.refs_4_), channel_id=1, source_target_pairs={{0,16},{4,20},{8,24},{12,28},{16,0},{20,4},{24,8},{28,12},{1,17},{... | collective-permute-start | bytes 589832 | tf_op jit(solution)/shard_map/ppermute | solution.py:291
  28.9 5.9 %collective-permute-start.4 = (bf16[128,768]{1,0:T(8,128)(2,1)S(1)}, bf16[128,768]{1,0:T(8,128)(2,1)S(1)}, u32[]{:S(2)}, u32[]{:S(2)}) collective-permute-start(bf16[128,768]{1,0:T(8,128)(2,1)S(1)} %get-tuple-element.25.refs_8_.refs_5_.refs_4_), channel_id=1, source_target_pairs={{0,8},{4,12},{8,0},{12,4},{16,24},{20,28},{24,16},{28,20},{1,9},{5... | collective-permute-start | bytes 589832 | tf_op jit(solution)/shard_map/ppermute | solution.py:291
  38.6 18.8 %collective-permute-start.11 = (bf16[4,128,768]{2,1,0:T(8,128)(2,1)S(1)}, bf16[4,128,768]{2,1,0:T(8,128)(2,1)S(1)}, u32[]{:S(2)}, u32[]{:S(2)}) collective-permute-start(bf16[4,128,768]{2,1,0:T(8,128)(2,1)S(1)} %get-tuple-element.35), channel_id=1, source_target_pairs={{0,4},{4,0},{8,12},{12,8},{16,20},{20,16},{24,28},{28,24},{1,5},{5... | collective-permute-start | bytes 2359304 | tf_op jit(solution)/shard_map/ppermute | solution.py:291
  38.6 13.5 %collective-permute-start.7 = (bf16[128,768]{1,0:T(8,128)(2,1)S(1)}, bf16[128,768]{1,0:T(8,128)(2,1)S(1)}, u32[]{:S(2)}, u32[]{:S(2)}) collective-permute-start(bf16[128,768]{1,0:T(8,128)(2,1)S(1)} %get-tuple-element.31.refs_8_), channel_id=1, source_target_pairs={{0,8},{4,12},{8,0},{12,4},{16,24},{20,28},{24,16},{28,20},{1,9},{5... | collective-permute-start | bytes 589832 | tf_op jit(solution)/shard_map/ppermute | solution.py:291
  40.2 15.4 %collective-permute-start.8 = (bf16[128,768]{1,0:T(8,128)(2,1)S(1)}, bf16[128,768]{1,0:T(8,128)(2,1)S(1)}, u32[]{:S(2)}, u32[]{:S(2)}) collective-permute-start(bf16[128,768]{1,0:T(8,128)(2,1)S(1)} %get-tuple-element.32.refs_10_), channel_id=1, source_target_pairs={{0,16},{4,20},{8,24},{12,28},{16,0},{20,4},{24,8},{28,12},{1,17},{... | collective-permute-start | bytes 589832 | tf_op jit(solution)/shard_map/ppermute | solution.py:291
  41.7 13.9 %collective-permute-start.9 = (bf16[128,768]{1,0:T(8,128)(2,1)S(1)}, bf16[128,768]{1,0:T(8,128)(2,1)S(1)}, u32[]{:S(2)}, u32[]{:S(2)}) collective-permute-start(bf16[128,768]{1,0:T(8,128)(2,1)S(1)} %get-tuple-element.33.refs_12_), channel_id=1, source_target_pairs={{0,24},{4,28},{8,16},{12,20},{16,8},{20,12},{24,0},{28,4},{1,25},{... | collective-permute-start | bytes 589832 | tf_op jit(solution)/shard_map/ppermute | solution.py:291
  42.2 15.2 %collective-permute-start.10 = (bf16[128,768]{1,0:T(8,128)(2,1)S(1)}, bf16[128,768]{1,0:T(8,128)(2,1)S(1)}, u32[]{:S(2)}, u32[]{:S(2)}) collective-permute-start(bf16[128,768]{1,0:T(8,128)(2,1)S(1)} %get-tuple-element.34.refs_13_), channel_id=1, source_target_pairs={{0,28},{4,24},{8,20},{12,16},{16,12},{20,8},{24,4},{28,0},{1,29},{... | collective-permute-start | bytes 589832 | tf_op jit(solution)/shard_map/ppermute | solution.py:291
  43.8 3.7 %copy-start = (bf16[6144,768]{1,0:T(8,128)(2,1)S(1)}, bf16[6144,768]{1,0:T(8,128)(2,1)}, u32[]{:S(2)}) copy-start(bf16[6144,768]{1,0:T(8,128)(2,1)} %refs_1_.1) | copy-start | bytes 28311556
  52.1 10.6 %copy-start.6 = (bf16[128,768]{1,0:T(8,128)(2,1)S(1)}, bf16[128,768]{1,0:T(8,128)(2,1)}, u32[]{:S(2)}) copy-start(bf16[128,768]{1,0:T(8,128)(2,1)} %get-tuple-element.22.refs_9_) | copy-start | bytes 589828
  52.1 6.4 %collective-permute-start.12 = (bf16[128,768]{1,0:T(8,128)(2,1)S(1)}, bf16[128,768]{1,0:T(8,128)(2,1)S(1)}, u32[]{:S(2)}, u32[]{:S(2)}) collective-permute-start(bf16[128,768]{1,0:T(8,128)(2,1)S(1)} %get-tuple-element.41.refs_7_), channel_id=1, source_target_pairs={{0,4},{4,0},{8,12},{12,8},{16,20},{20,16},{24,28},{28,24},{1,5},{5... | collective-permute-start | bytes 589832 | tf_op jit(solution)/shard_map/ppermute | solution.py:291
  55.6 5.6 %collective-permute-start.13 = (bf16[128,768]{1,0:T(8,128)(2,1)S(1)}, bf16[128,768]{1,0:T(8,128)(2,1)S(1)}, u32[]{:S(2)}, u32[]{:S(2)}) collective-permute-start(bf16[128,768]{1,0:T(8,128)(2,1)S(1)} %get-tuple-element.42.refs_9_), channel_id=1, source_target_pairs={{0,12},{4,8},{8,4},{12,0},{16,28},{20,24},{24,20},{28,16},{1,13},{... | collective-permute-start | bytes 589832 | tf_op jit(solution)/shard_map/ppermute | solution.py:291
  55.6 7.2 %collective-permute-start.14 = (bf16[128,768]{1,0:T(8,128)(2,1)S(1)}, bf16[128,768]{1,0:T(8,128)(2,1)S(1)}, u32[]{:S(2)}, u32[]{:S(2)}) collective-permute-start(bf16[128,768]{1,0:T(8,128)(2,1)S(1)} %get-tuple-element.43.refs_11_), channel_id=1, source_target_pairs={{0,20},{4,16},{8,28},{12,24},{16,4},{20,0},{24,12},{28,8},{1,21},{... | collective-permute-start | bytes 589832 | tf_op jit(solution)/shard_map/ppermute | solution.py:291

commit v4 on v3

--- a/solution.py
+++ b/solution.py
@@ -9,7 +9,7 @@
 
 HD = 128
 HEADER = 8
-LATE = (1, 3, 5)
+LATE = (3,5)
 
 
 def normalize(rows, norm_gain):
@@ -337,7 +337,7 @@
 
     block = shape((rows, half))
     stats = call(
-        stats_kernel, "partial_stats", shape((rows, 128), jnp.float32), [WHOLE] * 3, WHOLE,
+        stats_kernel, "partial_stats", shape((rows, 128), jnp.float32), [WHOLE] * 3, WHOLE, after=(value_weight,),
     )(middle, first_one, passed)
     *normed, packed = call(
         norm_kernel, "norm_rows", (block,) * 8 + (shape((4,) + flat),),
@@ -345,17 +345,19 @@
         (pltpu.VMEM((4, rows, columns), jnp.bfloat16), pltpu.SemaphoreType.DMA((4,))),
     )(info, stats, gain, patches, one, two, near, far, *chip_values)
 
+    mate_values = across(packed, 1)
+    mate_rows = across(normed[1], 1)
     query_grad, key_grad = call(
         backward_kernel, "attention_backward", (shape(flat), shape(flat)),
         [SMEM] + [WHOLE] * 13, (WHOLE,) * 2, (pltpu.VMEM(flat, jnp.float32),),
+        after=(mate_values, mate_rows),
     )(info, value_weight, queries, key_vectors, cotangent, weights, *normed)
-    mate_values = across(packed, 1)
 
     held = lax.optimization_barrier([normed[offset] for offset in LATE] + [query_grad])
     sent = list(normed)
     for offset, part in zip(LATE, held):
         sent[offset] = part
-    moved = [sent[0]] + [across(sent[offset], offset) for offset in range(1, 8)]
+    moved = [sent[0], mate_rows] + [across(sent[offset], offset) for offset in range(2, 8)]
     early = [offset for offset in range(8) if offset not in LATE]
     late = [offset for offset in range(8) if offset not in early]
 

time: 65.2 us -> 62 us (0.951)
  waiting for transfers between devices: 21.1 us -> 19.2 us
  starting transfers between devices: 22.9 us -> 21.7 us
    ppermute x11, waiting for transfers between devices: 11.5 us -> 9.67 us  [across(): return lax.ppermute(rows, 'dp', [(i, i ^ distance) for i in range(8)])]
    ppermute x11, starting transfers between devices: 11.5 us -> 10.4 us  [across(): return lax.ppermute(rows, 'dp', [(i, i ^ distance) for i in range(8)])]
    unnamed x14 -> x16, local copies, waits for them, and re-layouts: 5.56 us -> 5.56 us
  transfers between devices with their start and end apart: 16 -> 16, of which waited for: 9 -> 8; matrix products, arithmetic and copies ran while one was open for 2% -> 2% of each run, Pallas kernels for 13% -> 14%
where the time goes in v4:
time: 62 us; the launch traced here: 61.5 us
  starting transfers between devices  21.7 us (35%)
  waiting for transfers between devices  19.2 us (31%)
  Pallas kernels  12.8 us (21%)
  local copies, waits for them, and re-layouts  7.09 us (11%)
  between operations  0.73 us (1%)
    pallas_call x7, Pallas kernels, call(): return lambda *args: made(*args, *after)  12.8 us
    ppermute x11, starting transfers between devices, across(): return lax.ppermute(rows, 'dp', [(i, i ^ distance) for i in range(8)])  10.4 us
    ppermute x11, waiting for transfers between devices, across(): return lax.ppermute(rows, 'dp', [(i, i ^ distance) for i in range(8)])  9.67 us
    unnamed x16, local copies, waits for them, and re-layouts  5.56 us
    all_to_all x1, waiting for transfers between devices, fast_body(): lax.all_to_all(head_cotangent.reshape(8, slots // 8, width), 'dp', split_...  3.93 us
    all_to_all x1, starting transfers between devices, fast_body(): lax.all_to_all(head_cotangent.reshape(8, slots // 8, width), 'dp', split_...  3.72 us
    ppermute x1, starting transfers between devices, fast_body(): one = lax.ppermute(patches, 'mp', [(0, 1), (1, 0), (2, 3), (3, 2)])  3.09 us
    ppermute x1, starting transfers between devices, fast_body(): two = lax.ppermute(patches, 'mp', [(0, 2), (2, 0), (1, 3), (3, 1)])  2.59 us
  transfers between devices with their start and end apart: 16, of which 8 were waited for; matrix products, arithmetic and copies ran while one was open for 2% of the time, Pallas kernels for 14%

profile of v4, /device:TPU:0, one launch (start us, length us, event | category | flops | bytes accessed | tf_op | source)
XLA Modules:
  0.0 61.5 jit_solution(15508147623617130184)
XLA Ops:
  0.6 0.0 copy-start.2
  0.6 3.1 %collective-permute-start.1 = (bf16[128,1536]{1,0:T(8,128)(2,1)}, bf16[128,1536]{1,0:T(8,128)(2,1)S(1)}, u32[]{:S(2)}, u32[]{:S(2)}) collective-permute-start(bf16[128,1536]{1,0:T(8,128)(2,1)} %refs_3_.6), channel_id=1, source_target_pairs={{0,1},{1,0},{2,3},{3,2},{4,5},{5,4},{6,7},{7,6},{8,9},{9,8},{10,11... | collective-permute-start | bytes 1179656 | tf_op jit(solution)/shard_map/ppermute | solution.py:323
  3.7 2.6 %collective-permute-start = (bf16[128,1536]{1,0:T(8,128)(2,1)}, bf16[128,1536]{1,0:T(8,128)(2,1)S(1)}, u32[]{:S(2)}, u32[]{:S(2)}) collective-permute-start(bf16[128,1536]{1,0:T(8,128)(2,1)} %refs_3_.6), channel_id=1, source_target_pairs={{0,2},{2,0},{1,3},{3,1},{4,6},{6,4},{5,7},{7,5},{8,10},{10,8},{9,1... | collective-permute-start | bytes 1179656 | tf_op jit(solution)/shard_map/ppermute | solution.py:322
  6.3 3.7 %all-to-all-start = ((bf16[8,32,768]{2,1,0:T(8,128)(2,1)}), bf16[8,32,768]{2,1,0:T(8,128)(2,1)S(1)}, u32[]{:S(2)}, u32[]{:S(2)}) async-start(bf16[8,32,768]{2,1,0:T(8,128)(2,1)} %bitcast.10), calls=%async_computation | async-start | bytes 786432 | tf_op jit(solution)/shard_map/all_to_all | solution.py:319
  10.0 0.7 %reshape.17.refs_1_ = f32[8,768]{1,0:T(8,128)S(1)} reshape(f32[6144]{0:T(1024)} %param.9) | data formatting | bytes 49152 | tf_op jit(solution)/shard_map/reshape | solution.py:328
  10.8 0.7 %dynamic-slice_bitcast_fusion = (s32[8]{0:T(128)S(1)}, s32[8]{0:T(128)S(1)}) fusion(s32[8,8]{1,0:T(8,128)} %param.15, s32[]{:T(128)S(6)} %select_n.18, s32[8,8]{1,0:T(8,128)} %param.14), kind=kLoop, calls=%fused_computation | loop fusion | bytes 132 | tf_op jit(solution)/shard_map/jit(dynamic_index_in_dim)/squeeze | solution.py:315
  11.5 0.1 concatenate.3.refs_0_
  11.6 0.0 copy-start.3
  11.6 0.9 %copy-done.3 = bf16[128,768]{1,0:T(8,128)(2,1)S(1)} copy-done((bf16[128,768]{1,0:T(8,128)(2,1)S(1)}, bf16[128,768]{1,0:T(8,128)(2,1)}, u32[]{:S(2)}) %copy-start.3) | copy-done | bytes 196632
  12.5 0.0 copy-start.5
  12.5 0.9 %copy-done.5 = bf16[128,768]{1,0:T(8,128)(2,1)S(1)} copy-done((bf16[128,768]{1,0:T(8,128)(2,1)S(1)}, bf16[128,768]{1,0:T(8,128)(2,1)}, u32[]{:S(2)}) %copy-start.5) | copy-done | bytes 196632
  13.4 1.0 %attention_weights.1 = (f32[6,128,128]{2,1,0:T(8,128)S(1)}, f32[8,768]{1,0:T(8,128)S(1)}) custom-call(s32[24]{0:T(128)S(1)} %concatenate.3.refs_0_, f32[8,768]{1,0:T(8,128)S(1)} %reshape.17.refs_1_, bf16[128,768]{1,0:T(8,128)(2,1)S(1)} %copy-done.3, bf16[128,768]{1,0:T(8,128)(2,1)S(1)} %copy-done.5), custom_call_target="tpu_custom_call" | custom-call | flops 1 | bytes 1 | tf_op jit(solution)/shard_map/attention_weights/pallas_call | solution.py:287
  14.5 3.9 %all-to-all-done = bf16[8,32,768]{2,1,0:T(8,128)(2,1)S(1)} async-done(((bf16[8,32,768]{2,1,0:T(8,128)(2,1)}), bf16[8,32,768]{2,1,0:T(8,128)(2,1)S(1)}, u32[]{:S(2)}, u32[]{:S(2)}) %all-to-all-start) | async-done | bytes 393248 | tf_op jit(solution)/shard_map/all_to_all | solution.py:319
  18.4 1.0 %value_rows.1 = (bf16[128,768]{1,0:T(8,128)(2,1)S(1)}, bf16[128,768]{1,0:T(8,128)(2,1)S(1)}) custom-call(s32[24]{0:T(128)S(1)} %concatenate.3.refs_0_, bf16[256,768]{1,0:T(8,128)(2,1)S(1)} %bitcast.9, f32[6,128,128]{2,1,0:T(8,128)S(1)} %get-tuple-element.23.refs_2_.refs_5_), custom_call_target="tpu_custom_call" | custom-call | flops 1 | bytes 1 | tf_op jit(solution)/shard_map/value_rows/pallas_call | solution.py:287
  19.4 2.0 %collective-permute-done.1.refs_1_.refs_4_ = bf16[128,1536]{1,0:T(8,128)(2,1)S(1)} collective-permute-done((bf16[128,1536]{1,0:T(8,128)(2,1)}, bf16[128,1536]{1,0:T(8,128)(2,1)S(1)}, u32[]{:S(2)}, u32[]{:S(2)}) %collective-permute-start.1) | collective-permute-done | bytes 393248 | tf_op jit(solution)/shard_map/ppermute | solution.py:323
  21.4 2.6 %collective-permute-done.refs_2_.refs_5_ = bf16[128,1536]{1,0:T(8,128)(2,1)S(1)} collective-permute-done((bf16[128,1536]{1,0:T(8,128)(2,1)}, bf16[128,1536]{1,0:T(8,128)(2,1)S(1)}, u32[]{:S(2)}, u32[]{:S(2)}) %collective-permute-start) | collective-permute-done | bytes 393248 | tf_op jit(solution)/shard_map/ppermute | solution.py:322
  23.9 0.7 %collective-permute-start.2 = (bf16[128,1536]{1,0:T(8,128)(2,1)}, bf16[128,1536]{1,0:T(8,128)(2,1)S(1)}, u32[]{:S(2)}, u32[]{:S(2)}) collective-permute-start(bf16[128,1536]{1,0:T(8,128)(2,1)} %refs_3_.6), channel_id=1, source_target_pairs={{1,2},{2,1},{5,6},{6,5},{9,10},{10,9},{13,14},{14,13},{17,18},{18,... | collective-permute-start | bytes 1179656 | tf_op jit(solution)/shard_map/ppermute | solution.py:334
  24.6 1.3 %collective-permute-start.3 = (bf16[128,1536]{1,0:T(8,128)(2,1)S(1)}, bf16[128,1536]{1,0:T(8,128)(2,1)S(1)}, u32[]{:S(2)}, u32[]{:S(2)}) collective-permute-start(bf16[128,1536]{1,0:T(8,128)(2,1)S(1)} %collective-permute-done.refs_2_.refs_5_), channel_id=1, source_target_pairs={{2,3},{1,0},{6,7},{5,4},{10,11},{9,8},{14,15},{13,12},{18,19},{17,... | collective-permute-start | bytes 1179656 | tf_op jit(solution)/shard_map/ppermute | solution.py:335
  25.9 2.5 %collective-permute-start.6 = (bf16[128,768]{1,0:T(8,128)(2,1)S(1)}, bf16[128,768]{1,0:T(8,128)(2,1)S(1)}, u32[]{:S(2)}, u32[]{:S(2)}) collective-permute-start(bf16[128,768]{1,0:T(8,128)(2,1)S(1)} %get-tuple-element.24.refs_8_.refs_6_.refs_3_), channel_id=1, source_target_pairs={{0,24},{4,28},{8,16},{12,20},{16,8},{20,12},{24,0},{28,4},{1,25},{... | collective-permute-start | bytes 589832 | tf_op jit(solution)/shard_map/ppermute | solution.py:291
  28.4 0.5 collective-permute-start.5
  28.9 0.5 collective-permute-start.4
  29.4 0.0 copy-done.2
  29.4 0.0 copy-start
  29.4 3.7 %copy-done = bf16[6144,768]{1,0:T(8,128)(2,1)S(1)} copy-done((bf16[6144,768]{1,0:T(8,128)(2,1)S(1)}, bf16[6144,768]{1,0:T(8,128)(2,1)}, u32[]{:S(2)}) %copy-start) | copy-done | bytes 9437208
  33.1 0.0 copy-start.1
  33.1 0.6 %partial_stats.1.refs_1_ = f32[128,128]{1,0:T(8,128)S(1)} custom-call(bf16[128,1536]{1,0:T(8,128)(2,1)S(1)} %copy-done.2, bf16[128,1536]{1,0:T(8,128)(2,1)S(1)} %collective-permute-done.1.refs_1_.refs_4_, bf16[128,1536]{1,0:T(8,128)(2,1)S(1)} %collective-permute-done.refs_2_.refs_5_, bf16[6144,768]{1,0:T(8,128)(2,1)S(1)} %copy-done), custom_call_target="tpu_custom_call" | custom-call | flops 1 | bytes 1 | tf_op jit(solution)/shard_map/partial_stats/pallas_call | solution.py:287
  33.8 0.0 copy-start.4
  33.8 0.0 copy-start.6
  33.8 0.0 collective-permute-done.6.refs_11_.refs_9_.refs_6_
  33.8 1.0 %collective-permute-done.5.refs_10_.refs_8_.refs_5_ = bf16[128,768]{1,0:T(8,128)(2,1)S(1)} collective-permute-done((bf16[128,768]{1,0:T(8,128)(2,1)S(1)}, bf16[128,768]{1,0:T(8,128)(2,1)S(1)}, u32[]{:S(2)}, u32[]{:S(2)}) %collective-permute-start.5) | collective-permute-done | bytes 196640 | tf_op jit(solution)/shard_map/ppermute | solution.py:291
  34.8 0.0 collective-permute-done.4.refs_9_.refs_7_.refs_4_
  34.8 0.0 collective-permute-done.2.refs_6_
  34.8 1.1 %collective-permute-done.3.refs_7_ = bf16[128,1536]{1,0:T(8,128)(2,1)S(1)} collective-permute-done((bf16[128,1536]{1,0:T(8,128)(2,1)S(1)}, bf16[128,1536]{1,0:T(8,128)(2,1)S(1)}, u32[]{:S(2)}, u32[]{:S(2)}) %collective-permute-start.3) | collective-permute-done | bytes 393248 | tf_op jit(solution)/shard_map/ppermute | solution.py:335
  35.9 2.7 %norm_rows.1 = (bf16[128,768]{1,0:T(8,128)(2,1)S(1)}, bf16[128,768]{1,0:T(8,128)(2,1)S(1)}, bf16[128,768]{1,0:T(8,128)(2,1)S(1)}, bf16[128,768]{1,0:T(8,128)(2,1...) custom-call(s32[24]{0:T(128)S(1)} %concatenate.3.refs_0_, ...), custom_call_target="tpu_custom_call" | custom-call | flops 1 | bytes 1 | tf_op jit(solution)/shard_map/norm_rows/pallas_call | solution.py:287
  38.6 0.1 collective-permute-start.12
  38.6 0.5 collective-permute-start.7
  39.1 1.5 %collective-permute-start.8 = (bf16[128,768]{1,0:T(8,128)(2,1)S(1)}, bf16[128,768]{1,0:T(8,128)(2,1)S(1)}, u32[]{:S(2)}, u32[]{:S(2)}) collective-permute-start(bf16[128,768]{1,0:T(8,128)(2,1)S(1)} %get-tuple-element.31.refs_8_), channel_id=1, source_target_pairs={{0,8},{4,12},{8,0},{12,4},{16,24},{20,28},{24,16},{28,20},{1,9},{5... | collective-permute-start | bytes 589832 | tf_op jit(solution)/shard_map/ppermute | solution.py:291
  40.6 1.5 %collective-permute-start.9 = (bf16[128,768]{1,0:T(8,128)(2,1)S(1)}, bf16[128,768]{1,0:T(8,128)(2,1)S(1)}, u32[]{:S(2)}, u32[]{:S(2)}) collective-permute-start(bf16[128,768]{1,0:T(8,128)(2,1)S(1)} %get-tuple-element.32.refs_10_), channel_id=1, source_target_pairs={{0,16},{4,20},{8,24},{12,28},{16,0},{20,4},{24,8},{28,12},{1,17},{... | collective-permute-start | bytes 589832 | tf_op jit(solution)/shard_map/ppermute | solution.py:291
  42.1 0.5 collective-permute-start.10
  42.6 0.0 collective-permute-done.7.refs_1_.refs_15_
  42.6 1.3 %collective-permute-start.11 = (bf16[128,768]{1,0:T(8,128)(2,1)S(1)}, bf16[128,768]{1,0:T(8,128)(2,1)S(1)}, u32[]{:S(2)}, u32[]{:S(2)}) collective-permute-start(bf16[128,768]{1,0:T(8,128)(2,1)S(1)} %get-tuple-element.34.refs_13_), channel_id=1, source_target_pairs={{0,28},{4,24},{8,20},{12,16},{16,12},{20,8},{24,4},{28,0},{1,29},{... | collective-permute-start | bytes 589832 | tf_op jit(solution)/shard_map/ppermute | solution.py:291
  43.9 0.0 collective-permute-done.12.refs_10_.refs_14_.refs_7_
  43.9 0.0 copy-done.1
  43.9 0.0 copy-done.4
  43.9 0.0 copy-done.6
  43.9 4.6 %attention_backward.1 = (bf16[128,768]{1,0:T(8,128)(2,1)}, bf16[128,768]{1,0:T(8,128)(2,1)}) custom-call(s32[24]{0:T(128)S(1)} %concatenate.3.refs_0_, bf16[6144,768]{1,0:T(8,128)(2,1)S(1)} %copy-done.1, bf16[128,768]{1,0:T(8,128)(2,1)S(1)} %copy-done.4, bf16[128,768]{1,0:T(8,128)(2,1)S(1)} %copy-done.6, bf16[128,768]{1,0:T(8,128)(2,1)S(1)} %get-tuple-element.38.refs_4_, ...), custom_call_target="tpu_custom_call" | custom-call | flops 1 | bytes 1 | tf_op jit(solution)/shard_map/attention_backward/pallas_call | solution.py:287
  48.6 0.0 copy-start.7
  48.6 1.4 %collective-permute-start.13 = (bf16[128,768]{1,0:T(8,128)(2,1)S(1)}, bf16[128,768]{1,0:T(8,128)(2,1)S(1)}, u32[]{:S(2)}, u32[]{:S(2)}) collective-permute-start(bf16[128,768]{1,0:T(8,128)(2,1)S(1)} %get-tuple-element.40.refs_9_), channel_id=1, source_target_pairs={{0,12},{4,8},{8,4},{12,0},{16,28},{20,24},{24,20},{28,16},{1,13},{... | collective-permute-start | bytes 589832 | tf_op jit(solution)/shard_map/ppermute | solution.py:291
  50.0 0.0 collective-permute-done.8.refs_2_
  50.0 0.0 collective-permute-start.14
  50.0 5.8 %collective-permute-done.9.refs_3_ = bf16[128,768]{1,0:T(8,128)(2,1)S(1)} collective-permute-done((bf16[128,768]{1,0:T(8,128)(2,1)S(1)}, bf16[128,768]{1,0:T(8,128)(2,1)S(1)}, u32[]{:S(2)}, u32[]{:S(2)}) %collective-permute-start.9) | collective-permute-done | bytes 196640 | tf_op jit(solution)/shard_map/ppermute | solution.py:291
  55.8 0.0 collective-permute-done.10.refs_4_
  55.8 0.0 collective-permute-done.11.refs_5_
  55.8 1.1 %gradient_first.1.refs_0_ = f32[768,768]{1,0:T(8,128)S(1)} custom-call(bf16[128,768]{1,0:T(8,128)(2,1)S(1)} %get-tuple-element.29.refs_0_.refs_6_, bf16[128,768]{1,0:T(8,128)(2,1)S(1)} %collective-permute-done.7.refs_1_.refs_15_, bf16[128,768]{1,0:T(8,128)(2,1)S(1)} %collective-permute-done.8.refs_2_, bf16[128,768]{1,0:T(8,128)(2,1)S(1)} %collective-permute-done.9.refs_3_, ...), custom_call_target="tpu_custom_call" | custom-call | flops 1 | bytes 1 | tf_op jit(solution)/shard_map/gradient_first/pallas_call | solution.py:287
  56.9 0.9 %collective-permute-done.13.refs_1_ = bf16[128,768]{1,0:T(8,128)(2,1)S(1)} collective-permute-done((bf16[128,768]{1,0:T(8,128)(2,1)S(1)}, bf16[128,768]{1,0:T(8,128)(2,1)S(1)}, u32[]{:S(2)}, u32[]{:S(2)}) %collective-permute-start.13) | collective-permute-done | bytes 196640 | tf_op jit(solution)/shard_map/ppermute | solution.py:291
  57.8 2.0 %collective-permute-done.14.refs_2_ = bf16[128,768]{1,0:T(8,128)(2,1)S(1)} collective-permute-done((bf16[128,768]{1,0:T(8,128)(2,1)S(1)}, bf16[128,768]{1,0:T(8,128)(2,1)S(1)}, u32[]{:S(2)}, u32[]{:S(2)}) %collective-permute-start.14) | collective-permute-done | bytes 196640 | tf_op jit(solution)/shard_map/ppermute | solution.py:291
  59.8 0.0 copy-done.7
  59.8 1.7 %gradient_last.1 = f32[768,768]{1,0:T(8,128)} custom-call(f32[768,768]{1,0:T(8,128)S(1)} %gradient_first.1.refs_0_, bf16[128,768]{1,0:T(8,128)(2,1)S(1)} %collective-permute-done.13.refs_1_, bf16[128,768]{1,0:T(8,128)(2,1)S(1)} %collective-permute-done.14.refs_2_, bf16[128,768]{1,0:T(8,128)(2,1)S(1)} %get-tuple-element.24.refs_8_.refs_6_.refs_3_, ...), custom_call_target="tpu_custom_call" | custom-call | flops 1 | bytes 1 | tf_op jit(solution)/shard_map/gradient_last/pallas_call | solution.py:287
  (1 shorter events, 0.0 us)
Async XLA Ops:
  0.6 28.8 %copy-start.2 = (bf16[128,1536]{1,0:T(8,128)(2,1)S(1)}, bf16[128,1536]{1,0:T(8,128)(2,1)}, u32[]{:S(2)}) copy-start(bf16[128,1536]{1,0:T(8,128)(2,1)} %refs_3_.6) | copy-start | bytes 1179652
  0.6 20.7 %collective-permute-start.1 = (bf16[128,1536]{1,0:T(8,128)(2,1)}, bf16[128,1536]{1,0:T(8,128)(2,1)S(1)}, u32[]{:S(2)}, u32[]{:S(2)}) collective-permute-start(bf16[128,1536]{1,0:T(8,128)(2,1)} %refs_3_.6), channel_id=1, source_target_pairs={{0,1},{1,0},{2,3},{3,2},{4,5},{5,4},{6,7},{7,6},{8,9},{9,8},{10,11... | collective-permute-start | bytes 1179656 | tf_op jit(solution)/shard_map/ppermute | solution.py:323
  3.7 20.2 %collective-permute-start = (bf16[128,1536]{1,0:T(8,128)(2,1)}, bf16[128,1536]{1,0:T(8,128)(2,1)S(1)}, u32[]{:S(2)}, u32[]{:S(2)}) collective-permute-start(bf16[128,1536]{1,0:T(8,128)(2,1)} %refs_3_.6), channel_id=1, source_target_pairs={{0,2},{2,0},{1,3},{3,1},{4,6},{6,4},{5,7},{7,5},{8,10},{10,8},{9,1... | collective-permute-start | bytes 1179656 | tf_op jit(solution)/shard_map/ppermute | solution.py:322
  6.3 12.1 %all-to-all-start = ((bf16[8,32,768]{2,1,0:T(8,128)(2,1)}), bf16[8,32,768]{2,1,0:T(8,128)(2,1)S(1)}, u32[]{:S(2)}, u32[]{:S(2)}) async-start(bf16[8,32,768]{2,1,0:T(8,128)(2,1)} %bitcast.10), calls=%async_computation | async-start | bytes 786432 | tf_op jit(solution)/shard_map/all_to_all | solution.py:319
  11.6 0.9 %copy-start.3 = (bf16[128,768]{1,0:T(8,128)(2,1)S(1)}, bf16[128,768]{1,0:T(8,128)(2,1)}, u32[]{:S(2)}) copy-start(bf16[128,768]{1,0:T(8,128)(2,1)} %refs_2_.3) | copy-start | bytes 589828
  12.5 0.9 %copy-start.5 = (bf16[128,768]{1,0:T(8,128)(2,1)S(1)}, bf16[128,768]{1,0:T(8,128)(2,1)}, u32[]{:S(2)}) copy-start(bf16[128,768]{1,0:T(8,128)(2,1)} %refs_3_.7) | copy-start | bytes 589828
  23.9 10.9 %collective-permute-start.2 = (bf16[128,1536]{1,0:T(8,128)(2,1)}, bf16[128,1536]{1,0:T(8,128)(2,1)S(1)}, u32[]{:S(2)}, u32[]{:S(2)}) collective-permute-start(bf16[128,1536]{1,0:T(8,128)(2,1)} %refs_3_.6), channel_id=1, source_target_pairs={{1,2},{2,1},{5,6},{6,5},{9,10},{10,9},{13,14},{14,13},{17,18},{18,... | collective-permute-start | bytes 1179656 | tf_op jit(solution)/shard_map/ppermute | solution.py:334
  24.6 11.3 %collective-permute-start.3 = (bf16[128,1536]{1,0:T(8,128)(2,1)S(1)}, bf16[128,1536]{1,0:T(8,128)(2,1)S(1)}, u32[]{:S(2)}, u32[]{:S(2)}) collective-permute-start(bf16[128,1536]{1,0:T(8,128)(2,1)S(1)} %collective-permute-done.refs_2_.refs_5_), channel_id=1, source_target_pairs={{2,3},{1,0},{6,7},{5,4},{10,11},{9,8},{14,15},{13,12},{18,19},{17,... | collective-permute-start | bytes 1179656 | tf_op jit(solution)/shard_map/ppermute | solution.py:335
  25.9 7.9 %collective-permute-start.6 = (bf16[128,768]{1,0:T(8,128)(2,1)S(1)}, bf16[128,768]{1,0:T(8,128)(2,1)S(1)}, u32[]{:S(2)}, u32[]{:S(2)}) collective-permute-start(bf16[128,768]{1,0:T(8,128)(2,1)S(1)} %get-tuple-element.24.refs_8_.refs_6_.refs_3_), channel_id=1, source_target_pairs={{0,24},{4,28},{8,16},{12,20},{16,8},{20,12},{24,0},{28,4},{1,25},{... | collective-permute-start | bytes 589832 | tf_op jit(solution)/shard_map/ppermute | solution.py:291
  28.4 6.4 %collective-permute-start.5 = (bf16[128,768]{1,0:T(8,128)(2,1)S(1)}, bf16[128,768]{1,0:T(8,128)(2,1)S(1)}, u32[]{:S(2)}, u32[]{:S(2)}) collective-permute-start(bf16[128,768]{1,0:T(8,128)(2,1)S(1)} %get-tuple-element.24.refs_8_.refs_6_.refs_3_), channel_id=1, source_target_pairs={{0,16},{4,20},{8,24},{12,28},{16,0},{20,4},{24,8},{28,12},{1,17},{... | collective-permute-start | bytes 589832 | tf_op jit(solution)/shard_map/ppermute | solution.py:291
  28.9 5.9 %collective-permute-start.4 = (bf16[128,768]{1,0:T(8,128)(2,1)S(1)}, bf16[128,768]{1,0:T(8,128)(2,1)S(1)}, u32[]{:S(2)}, u32[]{:S(2)}) collective-permute-start(bf16[128,768]{1,0:T(8,128)(2,1)S(1)} %get-tuple-element.24.refs_8_.refs_6_.refs_3_), channel_id=1, source_target_pairs={{0,8},{4,12},{8,0},{12,4},{16,24},{20,28},{24,16},{28,20},{1,9},{5... | collective-permute-start | bytes 589832 | tf_op jit(solution)/shard_map/ppermute | solution.py:291
  29.4 3.7 %copy-start = (bf16[6144,768]{1,0:T(8,128)(2,1)S(1)}, bf16[6144,768]{1,0:T(8,128)(2,1)}, u32[]{:S(2)}) copy-start(bf16[6144,768]{1,0:T(8,128)(2,1)} %refs_1_.1) | copy-start | bytes 28311556
  33.1 10.8 %copy-start.1 = (bf16[6144,768]{1,0:T(8,128)(2,1)S(1)}, bf16[6144,768]{1,0:T(8,128)(2,1)}, u32[]{:S(2)}) copy-start(bf16[6144,768]{1,0:T(8,128)(2,1)} %refs_1_.1) | copy-start | bytes 28311556
  33.8 10.2 %copy-start.4 = (bf16[128,768]{1,0:T(8,128)(2,1)S(1)}, bf16[128,768]{1,0:T(8,128)(2,1)}, u32[]{:S(2)}) copy-start(bf16[128,768]{1,0:T(8,128)(2,1)} %refs_2_.3) | copy-start | bytes 589828
  33.8 10.2 %copy-start.6 = (bf16[128,768]{1,0:T(8,128)(2,1)S(1)}, bf16[128,768]{1,0:T(8,128)(2,1)}, u32[]{:S(2)}) copy-start(bf16[128,768]{1,0:T(8,128)(2,1)} %refs_3_.7) | copy-start | bytes 589828
  38.6 5.4 %collective-permute-start.12 = (bf16[4,128,768]{2,1,0:T(8,128)(2,1)S(1)}, bf16[4,128,768]{2,1,0:T(8,128)(2,1)S(1)}, u32[]{:S(2)}, u32[]{:S(2)}) collective-permute-start(bf16[4,128,768]{2,1,0:T(8,128)(2,1)S(1)} %get-tuple-element.35), channel_id=1, source_target_pairs={{0,4},{4,0},{8,12},{12,8},{16,20},{20,16},{24,28},{28,24},{1,5},{5... | collective-permute-start | bytes 2359304 | tf_op jit(solution)/shard_map/ppermute | solution.py:291
  38.6 4.0 %collective-permute-start.7 = (bf16[128,768]{1,0:T(8,128)(2,1)S(1)}, bf16[128,768]{1,0:T(8,128)(2,1)S(1)}, u32[]{:S(2)}, u32[]{:S(2)}) collective-permute-start(bf16[128,768]{1,0:T(8,128)(2,1)S(1)} %get-tuple-element.30.refs_7_), channel_id=1, source_target_pairs={{0,4},{4,0},{8,12},{12,8},{16,20},{20,16},{24,28},{28,24},{1,5},{5... | collective-permute-start | bytes 589832 | tf_op jit(solution)/shard_map/ppermute | solution.py:291
  39.1 10.8 %collective-permute-start.8 = (bf16[128,768]{1,0:T(8,128)(2,1)S(1)}, bf16[128,768]{1,0:T(8,128)(2,1)S(1)}, u32[]{:S(2)}, u32[]{:S(2)}) collective-permute-start(bf16[128,768]{1,0:T(8,128)(2,1)S(1)} %get-tuple-element.31.refs_8_), channel_id=1, source_target_pairs={{0,8},{4,12},{8,0},{12,4},{16,24},{20,28},{24,16},{28,20},{1,9},{5... | collective-permute-start | bytes 589832 | tf_op jit(solution)/shard_map/ppermute | solution.py:291
  40.6 15.2 %collective-permute-start.9 = (bf16[128,768]{1,0:T(8,128)(2,1)S(1)}, bf16[128,768]{1,0:T(8,128)(2,1)S(1)}, u32[]{:S(2)}, u32[]{:S(2)}) collective-permute-start(bf16[128,768]{1,0:T(8,128)(2,1)S(1)} %get-tuple-element.32.refs_10_), channel_id=1, source_target_pairs={{0,16},{4,20},{8,24},{12,28},{16,0},{20,4},{24,8},{28,12},{1,17},{... | collective-permute-start | bytes 589832 | tf_op jit(solution)/shard_map/ppermute | solution.py:291
  42.1 13.7 %collective-permute-start.10 = (bf16[128,768]{1,0:T(8,128)(2,1)S(1)}, bf16[128,768]{1,0:T(8,128)(2,1)S(1)}, u32[]{:S(2)}, u32[]{:S(2)}) collective-permute-start(bf16[128,768]{1,0:T(8,128)(2,1)S(1)} %get-tuple-element.33.refs_12_), channel_id=1, source_target_pairs={{0,24},{4,28},{8,16},{12,20},{16,8},{20,12},{24,0},{28,4},{1,25},{... | collective-permute-start | bytes 589832 | tf_op jit(solution)/shard_map/ppermute | solution.py:291
  42.6 13.2 %collective-permute-start.11 = (bf16[128,768]{1,0:T(8,128)(2,1)S(1)}, bf16[128,768]{1,0:T(8,128)(2,1)S(1)}, u32[]{:S(2)}, u32[]{:S(2)}) collective-permute-start(bf16[128,768]{1,0:T(8,128)(2,1)S(1)} %get-tuple-element.34.refs_13_), channel_id=1, source_target_pairs={{0,28},{4,24},{8,20},{12,16},{16,12},{20,8},{24,4},{28,0},{1,29},{... | collective-permute-start | bytes 589832 | tf_op jit(solution)/shard_map/ppermute | solution.py:291
  48.6 11.2 %copy-start.7 = (bf16[128,768]{1,0:T(8,128)(2,1)S(1)}, bf16[128,768]{1,0:T(8,128)(2,1)}, u32[]{:S(2)}) copy-start(bf16[128,768]{1,0:T(8,128)(2,1)} %get-tuple-element.21.refs_8_) | copy-start | bytes 589828
  48.6 9.3 %collective-permute-start.13 = (bf16[128,768]{1,0:T(8,128)(2,1)S(1)}, bf16[128,768]{1,0:T(8,128)(2,1)S(1)}, u32[]{:S(2)}, u32[]{:S(2)}) collective-permute-start(bf16[128,768]{1,0:T(8,128)(2,1)S(1)} %get-tuple-element.40.refs_9_), channel_id=1, source_target_pairs={{0,12},{4,8},{8,4},{12,0},{16,28},{20,24},{24,20},{28,16},{1,13},{... | collective-permute-start | bytes 589832 | tf_op jit(solution)/shard_map/ppermute | solution.py:291
  50.0 9.8 %collective-permute-start.14 = (bf16[128,768]{1,0:T(8,128)(2,1)S(1)}, bf16[128,768]{1,0:T(8,128)(2,1)S(1)}, u32[]{:S(2)}, u32[]{:S(2)}) collective-permute-start(bf16[128,768]{1,0:T(8,128)(2,1)S(1)} %get-tuple-element.41.refs_11_), channel_id=1, source_target_pairs={{0,20},{4,16},{8,28},{12,24},{16,4},{20,0},{24,12},{28,8},{1,21},{... | collective-permute-start | bytes 589832 | tf_op jit(solution)/shard_map/ppermute | solution.py:291

commit v5 on v4

--- a/solution.py
+++ b/solution.py
@@ -9,7 +9,10 @@
 
 HD = 128
 HEADER = 8
-LATE = (3,5)
+FIRST = (0,6,7,2,4,1)
+LAST = (16,17,3,5)
+LATE = (16,17,3,5)
+HALVED = (6, 7)
 
 
 def normalize(rows, norm_gain):
@@ -144,7 +147,9 @@
     return mean, jnp.sum(centred * centred, axis=-1, keepdims=True)
 
 
-def stats_kernel(own, one, two, stats_ref):
+def stats_kernel(info, own, one, two, stats_ref, arranged):
+    for index, ref in enumerate((own, one, two)):
+        arranged[index ^ info[2]] = ref[...]
     rows = own.shape[0]
     lane = lax.broadcasted_iota(jnp.int32, (rows, 128), 1)
     table = jnp.zeros((rows, 128), jnp.float32)
@@ -155,61 +160,61 @@
     stats_ref[...] = table
 
 
-def norm_kernel(info, stats_ref, gain_ref, own, one, two, near, far, *rest):
-    values, outs, (packed_ref, source, sems) = rest[:4], rest[4:12], rest[12:]
+def norm_kernel(info, stats_ref, gain_ref, arranged, near, far, *rest):
+    outs, halves, last_ref = rest[:8], rest[8:-1], rest[-1]
     device, layer = 2 * info[0] + info[1], info[2]
-    outer = (layer == 0) | (layer == 3)
     rows, half = outs[0].shape
-
-    def copy(index, ref):
-        return pltpu.make_async_copy(ref, source.at[index], sems.at[index])
-
-    @pl.when(outer)
-    def _():
-        copy(3, far).start()
-
-    @pl.when(jnp.logical_not(outer))
-    def _():
-        copy(3, near).start()
-
-    for index, ref in enumerate((own, one, two)):
-        copy(index, ref).start()
-    for index, ref in enumerate(values):
-        packed_ref[index] = ref[...]
-    copy(3, far).wait()
+    last = near[...].astype(jnp.float32) + far[...].astype(jnp.float32)
+    last_ref[...] = last.astype(jnp.bfloat16)
     columns = 8 * half
-    last_mean, last_spread = spread_of(source[3].astype(jnp.float32))
+    last_mean, last_spread = spread_of(last)
     table = stats_ref[...]
     means = [table[:, index:index + 1] for index in range(3)] + [last_mean]
     mean = sum(means) * 0.25
     shift = sum((part - mean) * (part - mean) for part in means) * (2 * half)
     spread = table[:, 3:4] + table[:, 4:5] + table[:, 5:6] + last_spread + shift
     rstd = lax.rsqrt(spread * (1.0 / columns) + 1e-06)
-    for index, ref in enumerate((own, one, two)):
-        copy(index, ref).wait()
-
     for offset, out in enumerate(outs):
         block = device ^ offset
         start = pl.multiple_of((block % 2) * half, half)
-        values = source[(block // 2) ^ layer, :, pl.ds(start, half)]
+        origin = block // 2
+        values = jnp.where(
+            (origin ^ layer) == 3, last_ref[:, pl.ds(start, half)], arranged[origin, :, pl.ds(start, half)]
+        )
         gain = gain_ref[pl.ds(block, 1), :]
         out[...] = ((values.astype(jnp.float32) - mean) * rstd * gain).astype(jnp.bfloat16)
-
-
-def backward_kernel(info, weight_ref, query_ref, key_ref, cot_ref, weights_ref, *refs):
-    normed, (query_out, key_out, total) = refs[:8], refs[8:]
+    first = pl.multiple_of((layer % 2) * (rows // 2), rows // 2)
+    for offset, ref in zip(HALVED, halves):
+        ref[...] = outs[offset][pl.ds(first, rows // 2), :]
+
+
+def pack_kernel(*refs):
+    for index, ref in enumerate(refs[:4]):
+        refs[4][index] = ref[...]
+
+
+def project_kernel(info, weight_ref, *refs):
+    normed, (value_ref, total) = refs[:8], refs[8:]
     device = 2 * info[0] + info[1]
     half = normed[0].shape[1]
     for offset, ref in enumerate(normed):
         start = pl.multiple_of((device ^ offset) * half, half)
         part = jnp.dot(ref[...], weight_ref[pl.ds(start, half), :], preferred_element_type=jnp.float32)
-        total[...] = total[...] + part if offset else part
+        if offset == 0:
+            total[...] = part
+        elif offset < 7:
+            total[...] += part
+        else:
+            value_ref[...] = (total[...] + part).astype(jnp.bfloat16)
+
+
+def backward_kernel(value_ref, query_ref, key_ref, cot_ref, weights_ref, query_out, key_out):
     scale = HD ** (-0.5)
     for head in range(query_ref.shape[1] // HD):
         columns = slice(head * HD, (head + 1) * HD)
         weights = weights_ref[head]
         prob_grad = lax.dot_general(
-            cot_ref[:, columns], total[:, columns].astype(jnp.bfloat16), (((1,), (1,)), ((), ())),
+            cot_ref[:, columns], value_ref[:, columns], (((1,), (1,)), ((), ())),
             preferred_element_type=jnp.float32,
         )
         centre = jnp.sum(weights * prob_grad, axis=-1, keepdims=True)
@@ -225,32 +230,42 @@
         ).astype(jnp.bfloat16)
 
 
-def joined(offsets, normed, chip_values, mate_values):
-    right = [mate_values[offset // 2] if offset % 2 else chip_values[offset // 2][...] for offset in offsets]
-    return jnp.concatenate([ref[...] for ref in normed], axis=0), jnp.concatenate(right, axis=0)
-
-
-def gradient_first_kernel(offsets, *refs):
-    count = len(offsets)
-    left, right = joined(offsets, refs[:count], refs[count:count + 4], refs[count + 4])
-    refs[count + 5][...] = lax.dot_general(
+def joined(info, names, refs):
+    refs = list(refs)
+    chip_values, mate_values = refs[-5:-1], refs[-1]
+    left, right = [], []
+    for name in names:
+        offset = name % 10
+        values = mate_values.at[offset // 2] if offset % 2 else chip_values[offset // 2]
+        left.append(refs.pop(0)[...])
+        if offset in HALVED:
+            rows = left[-1].shape[0]
+            side = (info[2] + name // 10) % 2
+            right.append(values[pl.ds(pl.multiple_of(side * rows, rows), rows), :])
+        else:
+            right.append(values[...])
+    return jnp.concatenate(left, axis=0), jnp.concatenate(right, axis=0)
+
+
+def gradient_first_kernel(names, info, *refs):
+    left, right = joined(info, names, refs[:-1])
+    refs[-1][...] = lax.dot_general(
         left, right, (((0,), (0,)), ((), ())), preferred_element_type=jnp.float32
     )
 
 
-def gradient_last_kernel(offsets, before, *refs):
-    count = len(offsets)
-    left, right = joined(offsets, refs[:count], refs[count:count + 4], refs[count + 4])
-    out_ref, ready, done = refs[count + 5:]
-    blocks, _, columns = ready.shape
+def gradient_last_kernel(names, info, before, *refs):
+    left, right = joined(info, names, refs[:-3])
+    out_ref, ready, done = refs[-3:]
+    blocks, rows, _ = ready.shape
     copies = []
     for block in range(blocks):
-        part = slice(block * columns, (block + 1) * columns)
-        ready[block] = before[:, part] + lax.dot_general(
-            left, right[:, part], (((0,), (0,)), ((), ())), preferred_element_type=jnp.float32
+        part = slice(block * rows, (block + 1) * rows)
+        ready[block] = before[part, :] + lax.dot_general(
+            left[:, part], right, (((0,), (0,)), ((), ())), preferred_element_type=jnp.float32
         )
         copies.append(
-            pltpu.make_async_copy(ready.at[block], out_ref.at[:, pl.ds(block * columns, columns)], done.at[block])
+            pltpu.make_async_copy(ready.at[block], out_ref.at[pl.ds(block * rows, rows)], done.at[block])
         )
         copies[-1].start()
     for copy in copies:
@@ -336,41 +351,58 @@
     chip_values = [value_rows] + [across(value_rows, distance) for distance in (2, 4, 6)]
 
     block = shape((rows, half))
-    stats = call(
-        stats_kernel, "partial_stats", shape((rows, 128), jnp.float32), [WHOLE] * 3, WHOLE, after=(value_weight,),
-    )(middle, first_one, passed)
-    *normed, packed = call(
-        norm_kernel, "norm_rows", (block,) * 8 + (shape((4,) + flat),),
-        [SMEM, WHOLE, WHOLE] + [ANY] * 5 + [WHOLE] * 4, (WHOLE,) * 9,
-        (pltpu.VMEM((4, rows, columns), jnp.bfloat16), pltpu.SemaphoreType.DMA((4,))),
-    )(info, stats, gain, patches, one, two, near, far, *chip_values)
+    stats, arranged = call(
+        stats_kernel, "partial_stats", (shape((rows, 128), jnp.float32), shape((4, rows, columns))),
+        [SMEM] + [WHOLE] * 3, (WHOLE, WHOLE), after=(value_weight,),
+    )(info, middle, first_one, passed)
+    *normed, = call(
+        norm_kernel, "norm_rows", (block,) * 8 + (shape((rows // 2, half)),) * len(HALVED),
+        [SMEM] + [WHOLE] * 5, (WHOLE,) * (8 + len(HALVED)), (pltpu.VMEM((rows, columns), jnp.bfloat16),),
+    )(info, stats, gain, arranged, near, far)
+    normed, halves = normed[:8], normed[8:]
+    packed = call(pack_kernel, "pack_values", shape((4,) + flat), [WHOLE] * 4, WHOLE, after=(normed[1],))(*chip_values)
 
     mate_values = across(packed, 1)
     mate_rows = across(normed[1], 1)
+    values = call(
+        project_kernel, "project_values", shape(flat), [SMEM] + [WHOLE] * 9, WHOLE, (pltpu.VMEM(flat, jnp.float32),),
+        after=(mate_values, mate_rows),
+    )(info, value_weight, *normed)
     query_grad, key_grad = call(
-        backward_kernel, "attention_backward", (shape(flat), shape(flat)),
-        [SMEM] + [WHOLE] * 13, (WHOLE,) * 2, (pltpu.VMEM(flat, jnp.float32),),
-        after=(mate_values, mate_rows),
-    )(info, value_weight, queries, key_vectors, cotangent, weights, *normed)
-
-    held = lax.optimization_barrier([normed[offset] for offset in LATE] + [query_grad])
-    sent = list(normed)
-    for offset, part in zip(LATE, held):
-        sent[offset] = part
-    moved = [sent[0], mate_rows] + [across(sent[offset], offset) for offset in range(2, 8)]
-    early = [offset for offset in range(8) if offset not in LATE]
-    late = [offset for offset in range(8) if offset not in early]
+        backward_kernel, "attention_backward", (shape(flat), shape(flat)), [WHOLE] * 5, (WHOLE,) * 2,
+    )(values, queries, key_vectors, cotangent, weights)
+
+    moved = {0: normed[0], 1: mate_rows}
+    sources = {offset: normed[offset] for offset in range(2, 8)} | dict(zip(HALVED, halves))
+    for offset in range(2, 8):
+        if offset not in LATE:
+            moved[offset] = across(sources[offset], offset)
+    held = [sources[name] if name < 10 else moved[name % 10] for name in LATE]
+    held = lax.optimization_barrier(held + [values])
+    for name, part in zip(LATE, held):
+        if name < 10:
+            moved[name] = across(part, name)
+        else:
+            moved[name] = lax.ppermute(part, "mp", [(0, 1), (1, 0), (2, 3), (3, 2)])
+    for offset in HALVED:
+        if offset + 10 not in moved:
+            moved[offset + 10] = lax.ppermute(moved[offset], "mp", [(0, 1), (1, 0), (2, 3), (3, 2)])
+
+    def arrived(names):
+        return [moved[name] for name in names] + chip_values + [mate_values]
 
     grad = shape((half, width), jnp.float32)
+    parts = arrived(FIRST)
     partial = call(
-        functools.partial(gradient_first_kernel, early), "gradient_first", grad, [WHOLE] * (len(early) + 5), WHOLE
-    )(*[moved[offset] for offset in early], *chip_values, mate_values)
-    blocks = width // 256
+        functools.partial(gradient_first_kernel, FIRST), "gradient_first", grad, [SMEM] + [WHOLE] * len(parts), WHOLE
+    )(info, *parts)
+    parts = arrived(LAST)
+    blocks = half // 256
     weight_grad = call(
-        functools.partial(gradient_last_kernel, late), "gradient_last", grad, [WHOLE] * (len(late) + 6), ANY,
-        (pltpu.VMEM((blocks, half, 256), jnp.float32), pltpu.SemaphoreType.DMA((blocks,))),
+        functools.partial(gradient_last_kernel, LAST), "gradient_last", grad, [SMEM] + [WHOLE] * (len(parts) + 1), ANY,
+        (pltpu.VMEM((blocks, 256, width), jnp.float32), pltpu.SemaphoreType.DMA((blocks,))),
         after=(query_grad,),
-    )(partial, *[moved[offset] for offset in late], *chip_values, mate_values)
+    )(info, partial, *parts)
     return weight_grad, query_grad, key_grad
 
 

time: 62 us -> 58.6 us (0.945)
  waiting for transfers between devices: 19.2 us -> 14.4 us
  starting transfers between devices: 21.7 us -> 23.7 us
    ppermute x11, waiting for transfers between devices: 9.67 us -> 3.23 us  [across(): return lax.ppermute(rows, 'dp', [(i, i ^ distance) for i in range(8)])]
    ppermute x1, waiting for transfers between devices: 1.97 us -> 0.19 us  [fast_body(): one = lax.ppermute(patches, 'mp', [(0, 1), (1, 0), (2, 3), (3, 2)])]
    ppermute x1, waiting for transfers between devices: 1.07 us -> 2.71 us  [fast_body(): far = lax.ppermute(passed, 'mp', [(2, 3), (1, 0)])]
    ppermute x0 -> x2, starting transfers between devices: none -> 1.61 us  [fast_body(): moved[name] = lax.ppermute(part, 'mp', [(0, 1), (1, 0), (2, 3), (3, 2)])]
    ppermute x1, starting transfers between devices: 2.59 us -> 4.1 us  [fast_body(): two = lax.ppermute(patches, 'mp', [(0, 2), (2, 0), (1, 3), (3, 1)])]
    ppermute x1, starting transfers between devices: 3.09 us -> 1.58 us  [fast_body(): one = lax.ppermute(patches, 'mp', [(0, 1), (1, 0), (2, 3), (3, 2)])]
    ppermute x0 -> x2, waiting for transfers between devices: none -> 1.08 us  [fast_body(): moved[name] = lax.ppermute(part, 'mp', [(0, 1), (1, 0), (2, 3), (3, 2)])]
    ppermute x1, waiting for transfers between devices: 2.56 us -> 3.22 us  [fast_body(): two = lax.ppermute(patches, 'mp', [(0, 2), (2, 0), (1, 3), (3, 1)])]
  transfers between devices with their start and end apart: 16 -> 18, of which waited for: 8 -> 7; matrix products, arithmetic and copies ran while one was open for 2% -> 3% of each run, Pallas kernels for 14% -> 17%
where the time goes in v5:
time: 58.6 us; the launch traced here: 58.2 us
  starting transfers between devices  23.7 us (40%)
  waiting for transfers between devices  14.4 us (25%)
  Pallas kernels  12.3 us (21%)
  local copies, waits for them, and re-layouts  7.09 us (12%)
  between operations  0.79 us (1%)
    pallas_call x9, Pallas kernels, call(): return lambda *args: made(*args, *after)  12.3 us
    ppermute x11, starting transfers between devices, across(): return lax.ppermute(rows, 'dp', [(i, i ^ distance) for i in range(8)])  10.7 us
    unnamed x16, local copies, waits for them, and re-layouts  5.56 us
    ppermute x1, starting transfers between devices, fast_body(): two = lax.ppermute(patches, 'mp', [(0, 2), (2, 0), (1, 3), (3, 1)])  4.1 us
    all_to_all x1, waiting for transfers between devices, fast_body(): lax.all_to_all(head_cotangent.reshape(8, slots // 8, width), 'dp', split_...  3.93 us
    all_to_all x1, starting transfers between devices, fast_body(): lax.all_to_all(head_cotangent.reshape(8, slots // 8, width), 'dp', split_...  3.72 us
    ppermute x11, waiting for transfers between devices, across(): return lax.ppermute(rows, 'dp', [(i, i ^ distance) for i in range(8)])  3.23 us
    ppermute x1, waiting for transfers between devices, fast_body(): two = lax.ppermute(patches, 'mp', [(0, 2), (2, 0), (1, 3), (3, 1)])  3.22 us
  transfers between devices with their start and end apart: 18, of which 7 were waited for; matrix products, arithmetic and copies ran while one was open for 3% of the time, Pallas kernels for 17%

profile of v5, /device:TPU:0, one launch (start us, length us, event | category | flops | bytes accessed | tf_op | source)
XLA Modules:
  0.0 58.2 jit_solution(11348850647370106043)
XLA Ops:
  0.6 0.0 copy-start.6
  0.6 4.1 %collective-permute-start = (bf16[128,1536]{1,0:T(8,128)(2,1)}, bf16[128,1536]{1,0:T(8,128)(2,1)S(1)}, u32[]{:S(2)}, u32[]{:S(2)}) collective-permute-start(bf16[128,1536]{1,0:T(8,128)(2,1)} %refs_1_.2), channel_id=1, source_target_pairs={{0,2},{2,0},{1,3},{3,1},{4,6},{6,4},{5,7},{7,5},{8,10},{10,8},{9,1... | collective-permute-start | bytes 1179656 | tf_op jit(solution)/shard_map/ppermute | solution.py:337
  4.7 1.6 %collective-permute-start.1 = (bf16[128,1536]{1,0:T(8,128)(2,1)}, bf16[128,1536]{1,0:T(8,128)(2,1)S(1)}, u32[]{:S(2)}, u32[]{:S(2)}) collective-permute-start(bf16[128,1536]{1,0:T(8,128)(2,1)} %refs_1_.2), channel_id=1, source_target_pairs={{0,1},{1,0},{2,3},{3,2},{4,5},{5,4},{6,7},{7,6},{8,9},{9,8},{10,11... | collective-permute-start | bytes 1179656 | tf_op jit(solution)/shard_map/ppermute | solution.py:338
  6.3 3.7 %all-to-all-start = ((bf16[8,32,768]{2,1,0:T(8,128)(2,1)}), bf16[8,32,768]{2,1,0:T(8,128)(2,1)S(1)}, u32[]{:S(2)}, u32[]{:S(2)}) async-start(bf16[8,32,768]{2,1,0:T(8,128)(2,1)} %bitcast.10), calls=%async_computation | async-start | bytes 786432 | tf_op jit(solution)/shard_map/all_to_all | solution.py:334
  10.0 0.7 %reshape.17.refs_1_ = f32[8,768]{1,0:T(8,128)S(1)} reshape(f32[6144]{0:T(1024)} %param.9) | data formatting | bytes 49152 | tf_op jit(solution)/shard_map/reshape | solution.py:343
  10.8 0.7 %dynamic-slice_bitcast_fusion = (s32[8]{0:T(128)S(1)}, s32[8]{0:T(128)S(1)}) fusion(s32[8,8]{1,0:T(8,128)} %param.15, s32[]{:T(128)S(6)} %select_n.18, s32[8,8]{1,0:T(8,128)} %param.14), kind=kLoop, calls=%fused_computation | loop fusion | bytes 132 | tf_op jit(solution)/shard_map/jit(dynamic_index_in_dim)/squeeze | solution.py:330
  11.5 0.1 concatenate.3.refs_0_
  11.6 0.0 copy-start.2
  11.6 0.9 %copy-done.2 = bf16[128,768]{1,0:T(8,128)(2,1)S(1)} copy-done((bf16[128,768]{1,0:T(8,128)(2,1)S(1)}, bf16[128,768]{1,0:T(8,128)(2,1)}, u32[]{:S(2)}) %copy-start.2) | copy-done | bytes 196632
  12.5 0.0 copy-start.4
  12.5 0.9 %copy-done.4 = bf16[128,768]{1,0:T(8,128)(2,1)S(1)} copy-done((bf16[128,768]{1,0:T(8,128)(2,1)S(1)}, bf16[128,768]{1,0:T(8,128)(2,1)}, u32[]{:S(2)}) %copy-start.4) | copy-done | bytes 196632
  13.4 1.0 %attention_weights.1 = (f32[6,128,128]{2,1,0:T(8,128)S(1)}, f32[8,768]{1,0:T(8,128)S(1)}) custom-call(s32[24]{0:T(128)S(1)} %concatenate.3.refs_0_, f32[8,768]{1,0:T(8,128)S(1)} %reshape.17.refs_1_, bf16[128,768]{1,0:T(8,128)(2,1)S(1)} %copy-done.2, bf16[128,768]{1,0:T(8,128)(2,1)S(1)} %copy-done.4), custom_call_target="tpu_custom_call" | custom-call | flops 1 | bytes 1 | tf_op jit(solution)/shard_map/attention_weights/pallas_call | solution.py:302
  14.5 3.9 %all-to-all-done = bf16[8,32,768]{2,1,0:T(8,128)(2,1)S(1)} async-done(((bf16[8,32,768]{2,1,0:T(8,128)(2,1)}), bf16[8,32,768]{2,1,0:T(8,128)(2,1)S(1)}, u32[]{:S(2)}, u32[]{:S(2)}) %all-to-all-start) | async-done | bytes 393248 | tf_op jit(solution)/shard_map/all_to_all | solution.py:334
  18.4 1.0 %value_rows.1 = (bf16[128,768]{1,0:T(8,128)(2,1)S(1)}, bf16[128,768]{1,0:T(8,128)(2,1)S(1)}) custom-call(s32[24]{0:T(128)S(1)} %concatenate.3.refs_0_, bf16[256,768]{1,0:T(8,128)(2,1)S(1)} %bitcast.9, f32[6,128,128]{2,1,0:T(8,128)S(1)} %get-tuple-element.28.refs_2_.refs_4_), custom_call_target="tpu_custom_call" | custom-call | flops 1 | bytes 1 | tf_op jit(solution)/shard_map/value_rows/pallas_call | solution.py:302
  19.4 3.2 %collective-permute-done.refs_3_ = bf16[128,1536]{1,0:T(8,128)(2,1)S(1)} collective-permute-done((bf16[128,1536]{1,0:T(8,128)(2,1)}, bf16[128,1536]{1,0:T(8,128)(2,1)S(1)}, u32[]{:S(2)}, u32[]{:S(2)}) %collective-permute-start) | collective-permute-done | bytes 393248 | tf_op jit(solution)/shard_map/ppermute | solution.py:337
  22.6 0.2 collective-permute-done.1.refs_2_
  22.8 0.7 %collective-permute-start.2 = (bf16[128,1536]{1,0:T(8,128)(2,1)}, bf16[128,1536]{1,0:T(8,128)(2,1)S(1)}, u32[]{:S(2)}, u32[]{:S(2)}) collective-permute-start(bf16[128,1536]{1,0:T(8,128)(2,1)} %refs_1_.2), channel_id=1, source_target_pairs={{1,2},{2,1},{5,6},{6,5},{9,10},{10,9},{13,14},{14,13},{17,18},{18,... | collective-permute-start | bytes 1179656 | tf_op jit(solution)/shard_map/ppermute | solution.py:349
  23.5 1.3 %collective-permute-start.3 = (bf16[128,1536]{1,0:T(8,128)(2,1)S(1)}, bf16[128,1536]{1,0:T(8,128)(2,1)S(1)}, u32[]{:S(2)}, u32[]{:S(2)}) collective-permute-start(bf16[128,1536]{1,0:T(8,128)(2,1)S(1)} %collective-permute-done.refs_3_), channel_id=1, source_target_pairs={{2,3},{1,0},{6,7},{5,4},{10,11},{9,8},{14,15},{13,12},{18,19},{17,... | collective-permute-start | bytes 1179656 | tf_op jit(solution)/shard_map/ppermute | solution.py:350
  24.8 2.6 %collective-permute-start.11 = (bf16[128,768]{1,0:T(8,128)(2,1)S(1)}, bf16[128,768]{1,0:T(8,128)(2,1)S(1)}, u32[]{:S(2)}, u32[]{:S(2)}) collective-permute-start(bf16[128,768]{1,0:T(8,128)(2,1)S(1)} %get-tuple-element.29.refs_0_.refs_7_.refs_6_), channel_id=1, source_target_pairs={{0,24},{4,28},{8,16},{12,20},{16,8},{20,12},{24,0},{28,4},{1,25},{... | collective-permute-start | bytes 589832 | tf_op jit(solution)/shard_map/ppermute | solution.py:306
  27.3 0.5 collective-permute-start.10
  27.8 0.5 collective-permute-start.9
  28.3 0.0 copy-done.6
  28.3 0.0 copy-start
  28.3 3.7 %copy-done = bf16[6144,768]{1,0:T(8,128)(2,1)S(1)} copy-done((bf16[6144,768]{1,0:T(8,128)(2,1)S(1)}, bf16[6144,768]{1,0:T(8,128)(2,1)}, u32[]{:S(2)}) %copy-start) | copy-done | bytes 9437208
  32.0 0.0 copy-start.1
  32.0 1.2 %partial_stats.1 = (f32[128,128]{1,0:T(8,128)S(1)}, bf16[4,128,1536]{2,1,0:T(8,128)(2,1)S(1)}) custom-call(s32[24]{0:T(128)S(1)} %concatenate.3.refs_0_, bf16[128,1536]{1,0:T(8,128)(2,1)S(1)} %copy-done.6, bf16[128,1536]{1,0:T(8,128)(2,1)S(1)} %collective-permute-done.1.refs_2_, bf16[128,1536]{1,0:T(8,128)(2,1)S(1)} %collective-permute-done.refs_3_, ...), custom_call_target="tpu_custom_call" | custom-call | flops 1 | bytes 1 | tf_op jit(solution)/shard_map/partial_stats/pallas_call | solution.py:302
  33.2 0.0 collective-permute-done.2.refs_4_
  33.2 2.7 %collective-permute-done.3.refs_5_ = bf16[128,1536]{1,0:T(8,128)(2,1)S(1)} collective-permute-done((bf16[128,1536]{1,0:T(8,128)(2,1)S(1)}, bf16[128,1536]{1,0:T(8,128)(2,1)S(1)}, u32[]{:S(2)}, u32[]{:S(2)}) %collective-permute-start.3) | collective-permute-done | bytes 393248 | tf_op jit(solution)/shard_map/ppermute | solution.py:350
  35.9 1.7 %norm_rows.1 = (bf16[128,768]{1,0:T(8,128)(2,1)S(1)}, bf16[128,768]{1,0:T(8,128)(2,1)S(1)}, bf16[128,768]{1,0:T(8,128)(2,1)S(1)}, bf16[128,768]{1,0:T(8,128)(2,1...) custom-call(s32[24]{0:T(128)S(1)} %concatenate.3.refs_0_, ...), custom_call_target="tpu_custom_call" | custom-call | flops 1 | bytes 1 | tf_op jit(solution)/shard_map/norm_rows/pallas_call | solution.py:302
  37.6 0.0 collective-permute-done.11.refs_3_.refs_10_.refs_9_
  37.6 0.0 collective-permute-done.10.refs_2_.refs_9_.refs_8_
  37.6 0.0 collective-permute-done.9.refs_1_.refs_8_.refs_7_
  37.6 0.1 pack_values.1
  37.7 0.1 collective-permute-start.12
  37.8 0.5 collective-permute-start.8
  38.3 2.4 %collective-permute-start.4 = (bf16[64,768]{1,0:T(8,128)(2,1)S(1)}, bf16[64,768]{1,0:T(8,128)(2,1)S(1)}, u32[]{:S(2)}, u32[]{:S(2)}) collective-permute-start(bf16[64,768]{1,0:T(8,128)(2,1)S(1)} %get-tuple-element.37), channel_id=1, source_target_pairs={{0,24},{4,28},{8,16},{12,20},{16,8},{20,12},{24,0},{28,4},{1,25},{... | collective-permute-start | bytes 294920 | tf_op jit(solution)/shard_map/ppermute | solution.py:306
  40.7 0.0 collective-permute-start.5
  40.7 1.4 %collective-permute-start.6 = (bf16[128,768]{1,0:T(8,128)(2,1)S(1)}, bf16[128,768]{1,0:T(8,128)(2,1)S(1)}, u32[]{:S(2)}, u32[]{:S(2)}) collective-permute-start(bf16[128,768]{1,0:T(8,128)(2,1)S(1)} %get-tuple-element.39.refs_4_), channel_id=1, source_target_pairs={{0,8},{4,12},{8,0},{12,4},{16,24},{20,28},{24,16},{28,20},{1,9},{5... | collective-permute-start | bytes 589832 | tf_op jit(solution)/shard_map/ppermute | solution.py:306
  42.1 0.0 collective-permute-done.8.refs_6_.refs_11_
  42.1 1.5 %collective-permute-start.7 = (bf16[128,768]{1,0:T(8,128)(2,1)S(1)}, bf16[128,768]{1,0:T(8,128)(2,1)S(1)}, u32[]{:S(2)}, u32[]{:S(2)}) collective-permute-start(bf16[128,768]{1,0:T(8,128)(2,1)S(1)} %get-tuple-element.40.refs_6_), channel_id=1, source_target_pairs={{0,16},{4,20},{8,24},{12,28},{16,0},{20,4},{24,8},{28,12},{1,17},{... | collective-permute-start | bytes 589832 | tf_op jit(solution)/shard_map/ppermute | solution.py:306
  43.6 0.0 collective-permute-done.12.refs_11_.refs_10_
  43.6 0.0 copy-done.1
  43.6 0.0 copy-start.3
  43.6 0.0 copy-start.5
  43.6 2.0 %project_values.1.refs_0_ = bf16[128,768]{1,0:T(8,128)(2,1)S(1)} custom-call(s32[24]{0:T(128)S(1)} %concatenate.3.refs_0_, bf16[6144,768]{1,0:T(8,128)(2,1)S(1)} %copy-done.1, bf16[128,768]{1,0:T(8,128)(2,1)S(1)} %get-tuple-element.36.refs_1_.refs_2_, bf16[128,768]{1,0:T(8,128)(2,1)S(1)} %get-tuple-element.41.refs_4_.refs_3_, ...), custom_call_target="tpu_custom_call" | custom-call | flops 1 | bytes 1 | tf_op jit(solution)/shard_map/project_values/pallas_call | solution.py:302
  45.6 0.0 collective-permute-done.4.refs_2_
  45.6 1.2 %collective-permute-done.5.refs_3_ = bf16[64,768]{1,0:T(8,128)(2,1)S(1)} collective-permute-done((bf16[64,768]{1,0:T(8,128)(2,1)S(1)}, bf16[64,768]{1,0:T(8,128)(2,1)S(1)}, u32[]{:S(2)}, u32[]{:S(2)}) %collective-permute-start.5) | collective-permute-done | bytes 98336 | tf_op jit(solution)/shard_map/ppermute | solution.py:306
  46.8 0.5 collective-permute-start.15
  47.3 0.7 %collective-permute-start.16 = (bf16[128,768]{1,0:T(8,128)(2,1)S(1)}, bf16[128,768]{1,0:T(8,128)(2,1)S(1)}, u32[]{:S(2)}, u32[]{:S(2)}) collective-permute-start(bf16[128,768]{1,0:T(8,128)(2,1)S(1)} %get-tuple-element.49.refs_7_), channel_id=1, source_target_pairs={{0,20},{4,16},{8,28},{12,24},{16,4},{20,0},{24,12},{28,8},{1,21},{... | collective-permute-start | bytes 589832 | tf_op jit(solution)/shard_map/ppermute | solution.py:306
  48.0 0.7 %collective-permute-start.13 = (bf16[64,768]{1,0:T(8,128)(2,1)S(1)}, bf16[64,768]{1,0:T(8,128)(2,1)S(1)}, u32[]{:S(2)}, u32[]{:S(2)}) collective-permute-start(bf16[64,768]{1,0:T(8,128)(2,1)S(1)} %collective-permute-done.4.refs_2_), channel_id=1, source_target_pairs={{0,1},{1,0},{2,3},{3,2},{4,5},{5,4},{6,7},{7,6},{8,9},{9,8},{10,11... | collective-permute-start | bytes 294920 | tf_op jit(solution)/shard_map/ppermute | solution.py:386
  48.7 2.0 %collective-permute-done.6.refs_4_ = bf16[128,768]{1,0:T(8,128)(2,1)S(1)} collective-permute-done((bf16[128,768]{1,0:T(8,128)(2,1)S(1)}, bf16[128,768]{1,0:T(8,128)(2,1)S(1)}, u32[]{:S(2)}, u32[]{:S(2)}) %collective-permute-start.6) | collective-permute-done | bytes 196640 | tf_op jit(solution)/shard_map/ppermute | solution.py:306
  50.7 0.9 %collective-permute-start.14 = (bf16[64,768]{1,0:T(8,128)(2,1)S(1)}, bf16[64,768]{1,0:T(8,128)(2,1)S(1)}, u32[]{:S(2)}, u32[]{:S(2)}) collective-permute-start(bf16[64,768]{1,0:T(8,128)(2,1)S(1)} %collective-permute-done.5.refs_3_), channel_id=1, source_target_pairs={{0,1},{1,0},{2,3},{3,2},{4,5},{5,4},{6,7},{7,6},{8,9},{9,8},{10,11... | collective-permute-start | bytes 294920 | tf_op jit(solution)/shard_map/ppermute | solution.py:386
  51.6 0.0 copy-done.3
  51.6 0.0 copy-done.5
  51.6 1.4 %attention_backward.1 = (bf16[128,768]{1,0:T(8,128)(2,1)}, bf16[128,768]{1,0:T(8,128)(2,1)}) custom-call(bf16[128,768]{1,0:T(8,128)(2,1)S(1)} %project_values.1.refs_0_, bf16[128,768]{1,0:T(8,128)(2,1)S(1)} %copy-done.3, bf16[128,768]{1,0:T(8,128)(2,1)S(1)} %copy-done.5, bf16[128,768]{1,0:T(8,128)(2,1)S(1)} %get-tuple-element.50.refs_3_, ...), custom_call_target="tpu_custom_call" | custom-call | flops 1 | bytes 1 | tf_op jit(solution)/shard_map/attention_backward/pallas_call | solution.py:302
  53.0 0.0 copy-start.7
  53.0 0.0 collective-permute-done.7.refs_5_
  53.0 1.7 %gradient_first.1.refs_1_ = f32[768,768]{1,0:T(8,128)S(1)} custom-call(s32[24]{0:T(128)S(1)} %concatenate.3.refs_0_, bf16[128,768]{1,0:T(8,128)(2,1)S(1)} %get-tuple-element.36.refs_1_.refs_2_, bf16[64,768]{1,0:T(8,128)(2,1)S(1)} %collective-permute-done.4.refs_2_, bf16[64,768]{1,0:T(8,128)(2,1)S(1)} %collective-permute-done.5.refs_3_, ...), custom_call_target="tpu_custom_call" | custom-call | flops 1 | bytes 1 | tf_op jit(solution)/shard_map/gradient_first/pallas_call | solution.py:302
  54.7 0.0 collective-permute-done.13.refs_2_
  54.7 1.1 %collective-permute-done.14.refs_3_ = bf16[64,768]{1,0:T(8,128)(2,1)S(1)} collective-permute-done((bf16[64,768]{1,0:T(8,128)(2,1)S(1)}, bf16[64,768]{1,0:T(8,128)(2,1)S(1)}, u32[]{:S(2)}, u32[]{:S(2)}) %collective-permute-start.14) | collective-permute-done | bytes 98336 | tf_op jit(solution)/shard_map/ppermute | solution.py:386
  55.8 0.0 collective-permute-done.15.refs_4_
  55.8 0.0 collective-permute-done.16.refs_5_
  55.8 0.0 copy-done.7
  55.8 2.4 %gradient_last.1 = f32[768,768]{1,0:T(8,128)} custom-call(s32[24]{0:T(128)S(1)} %concatenate.3.refs_0_, f32[768,768]{1,0:T(8,128)S(1)} %gradient_first.1.refs_1_, bf16[64,768]{1,0:T(8,128)(2,1)S(1)} %collective-permute-done.13.refs_2_, bf16[64,768]{1,0:T(8,128)(2,1)S(1)} %collective-permute-done.14.refs_3_, ...), custom_call_target="tpu_custom_call" | custom-call | flops 1 | bytes 1 | tf_op jit(solution)/shard_map/gradient_last/pallas_call | solution.py:302
  (1 shorter events, 0.0 us)
Async XLA Ops:
  0.6 27.7 %copy-start.6 = (bf16[128,1536]{1,0:T(8,128)(2,1)S(1)}, bf16[128,1536]{1,0:T(8,128)(2,1)}, u32[]{:S(2)}) copy-start(bf16[128,1536]{1,0:T(8,128)(2,1)} %refs_1_.2) | copy-start | bytes 1179652
  0.6 22.0 %collective-permute-start = (bf16[128,1536]{1,0:T(8,128)(2,1)}, bf16[128,1536]{1,0:T(8,128)(2,1)S(1)}, u32[]{:S(2)}, u32[]{:S(2)}) collective-permute-start(bf16[128,1536]{1,0:T(8,128)(2,1)} %refs_1_.2), channel_id=1, source_target_pairs={{0,2},{2,0},{1,3},{3,1},{4,6},{6,4},{5,7},{7,5},{8,10},{10,8},{9,1... | collective-permute-start | bytes 1179656 | tf_op jit(solution)/shard_map/ppermute | solution.py:337
  4.7 18.0 %collective-permute-start.1 = (bf16[128,1536]{1,0:T(8,128)(2,1)}, bf16[128,1536]{1,0:T(8,128)(2,1)S(1)}, u32[]{:S(2)}, u32[]{:S(2)}) collective-permute-start(bf16[128,1536]{1,0:T(8,128)(2,1)} %refs_1_.2), channel_id=1, source_target_pairs={{0,1},{1,0},{2,3},{3,2},{4,5},{5,4},{6,7},{7,6},{8,9},{9,8},{10,11... | collective-permute-start | bytes 1179656 | tf_op jit(solution)/shard_map/ppermute | solution.py:338
  6.3 12.1 %all-to-all-start = ((bf16[8,32,768]{2,1,0:T(8,128)(2,1)}), bf16[8,32,768]{2,1,0:T(8,128)(2,1)S(1)}, u32[]{:S(2)}, u32[]{:S(2)}) async-start(bf16[8,32,768]{2,1,0:T(8,128)(2,1)} %bitcast.10), calls=%async_computation | async-start | bytes 786432 | tf_op jit(solution)/shard_map/all_to_all | solution.py:334
  11.6 0.9 %copy-start.2 = (bf16[128,768]{1,0:T(8,128)(2,1)S(1)}, bf16[128,768]{1,0:T(8,128)(2,1)}, u32[]{:S(2)}) copy-start(bf16[128,768]{1,0:T(8,128)(2,1)} %refs_1_.4) | copy-start | bytes 589828
  12.5 0.9 %copy-start.4 = (bf16[128,768]{1,0:T(8,128)(2,1)S(1)}, bf16[128,768]{1,0:T(8,128)(2,1)}, u32[]{:S(2)}) copy-start(bf16[128,768]{1,0:T(8,128)(2,1)} %refs_2_.3) | copy-start | bytes 589828
  22.8 10.4 %collective-permute-start.2 = (bf16[128,1536]{1,0:T(8,128)(2,1)}, bf16[128,1536]{1,0:T(8,128)(2,1)S(1)}, u32[]{:S(2)}, u32[]{:S(2)}) collective-permute-start(bf16[128,1536]{1,0:T(8,128)(2,1)} %refs_1_.2), channel_id=1, source_target_pairs={{1,2},{2,1},{5,6},{6,5},{9,10},{10,9},{13,14},{14,13},{17,18},{18,... | collective-permute-start | bytes 1179656 | tf_op jit(solution)/shard_map/ppermute | solution.py:349
  23.5 12.4 %collective-permute-start.3 = (bf16[128,1536]{1,0:T(8,128)(2,1)S(1)}, bf16[128,1536]{1,0:T(8,128)(2,1)S(1)}, u32[]{:S(2)}, u32[]{:S(2)}) collective-permute-start(bf16[128,1536]{1,0:T(8,128)(2,1)S(1)} %collective-permute-done.refs_3_), channel_id=1, source_target_pairs={{2,3},{1,0},{6,7},{5,4},{10,11},{9,8},{14,15},{13,12},{18,19},{17,... | collective-permute-start | bytes 1179656 | tf_op jit(solution)/shard_map/ppermute | solution.py:350
  24.8 12.8 %collective-permute-start.11 = (bf16[128,768]{1,0:T(8,128)(2,1)S(1)}, bf16[128,768]{1,0:T(8,128)(2,1)S(1)}, u32[]{:S(2)}, u32[]{:S(2)}) collective-permute-start(bf16[128,768]{1,0:T(8,128)(2,1)S(1)} %get-tuple-element.29.refs_0_.refs_7_.refs_6_), channel_id=1, source_target_pairs={{0,24},{4,28},{8,16},{12,20},{16,8},{20,12},{24,0},{28,4},{1,25},{... | collective-permute-start | bytes 589832 | tf_op jit(solution)/shard_map/ppermute | solution.py:306
  27.3 10.3 %collective-permute-start.10 = (bf16[128,768]{1,0:T(8,128)(2,1)S(1)}, bf16[128,768]{1,0:T(8,128)(2,1)S(1)}, u32[]{:S(2)}, u32[]{:S(2)}) collective-permute-start(bf16[128,768]{1,0:T(8,128)(2,1)S(1)} %get-tuple-element.29.refs_0_.refs_7_.refs_6_), channel_id=1, source_target_pairs={{0,16},{4,20},{8,24},{12,28},{16,0},{20,4},{24,8},{28,12},{1,17},{... | collective-permute-start | bytes 589832 | tf_op jit(solution)/shard_map/ppermute | solution.py:306
  27.8 9.8 %collective-permute-start.9 = (bf16[128,768]{1,0:T(8,128)(2,1)S(1)}, bf16[128,768]{1,0:T(8,128)(2,1)S(1)}, u32[]{:S(2)}, u32[]{:S(2)}) collective-permute-start(bf16[128,768]{1,0:T(8,128)(2,1)S(1)} %get-tuple-element.29.refs_0_.refs_7_.refs_6_), channel_id=1, source_target_pairs={{0,8},{4,12},{8,0},{12,4},{16,24},{20,28},{24,16},{28,20},{1,9},{5... | collective-permute-start | bytes 589832 | tf_op jit(solution)/shard_map/ppermute | solution.py:306
  28.3 3.7 %copy-start = (bf16[6144,768]{1,0:T(8,128)(2,1)S(1)}, bf16[6144,768]{1,0:T(8,128)(2,1)}, u32[]{:S(2)}) copy-start(bf16[6144,768]{1,0:T(8,128)(2,1)} %refs_1_.3) | copy-start | bytes 28311556
  32.0 11.6 %copy-start.1 = (bf16[6144,768]{1,0:T(8,128)(2,1)S(1)}, bf16[6144,768]{1,0:T(8,128)(2,1)}, u32[]{:S(2)}) copy-start(bf16[6144,768]{1,0:T(8,128)(2,1)} %refs_1_.3) | copy-start | bytes 28311556
  37.7 5.9 %collective-permute-start.12 = (bf16[4,128,768]{2,1,0:T(8,128)(2,1)S(1)}, bf16[4,128,768]{2,1,0:T(8,128)(2,1)S(1)}, u32[]{:S(2)}, u32[]{:S(2)}) collective-permute-start(bf16[4,128,768]{2,1,0:T(8,128)(2,1)S(1)} %pack_values.1), channel_id=1, source_target_pairs={{0,4},{4,0},{8,12},{12,8},{16,20},{20,16},{24,28},{28,24},{1,5},{5... | collective-permute-start | bytes 2359304 | tf_op jit(solution)/shard_map/ppermute | solution.py:306
  37.8 4.3 %collective-permute-start.8 = (bf16[128,768]{1,0:T(8,128)(2,1)S(1)}, bf16[128,768]{1,0:T(8,128)(2,1)S(1)}, u32[]{:S(2)}, u32[]{:S(2)}) collective-permute-start(bf16[128,768]{1,0:T(8,128)(2,1)S(1)} %get-tuple-element.41.refs_4_.refs_3_), channel_id=1, source_target_pairs={{0,4},{4,0},{8,12},{12,8},{16,20},{20,16},{24,28},{28,24},{1,5},{5... | collective-permute-start | bytes 589832 | tf_op jit(solution)/shard_map/ppermute | solution.py:306
  38.3 7.3 %collective-permute-start.4 = (bf16[64,768]{1,0:T(8,128)(2,1)S(1)}, bf16[64,768]{1,0:T(8,128)(2,1)S(1)}, u32[]{:S(2)}, u32[]{:S(2)}) collective-permute-start(bf16[64,768]{1,0:T(8,128)(2,1)S(1)} %get-tuple-element.37), channel_id=1, source_target_pairs={{0,24},{4,28},{8,16},{12,20},{16,8},{20,12},{24,0},{28,4},{1,25},{... | collective-permute-start | bytes 294920 | tf_op jit(solution)/shard_map/ppermute | solution.py:306
  40.7 6.1 %collective-permute-start.5 = (bf16[64,768]{1,0:T(8,128)(2,1)S(1)}, bf16[64,768]{1,0:T(8,128)(2,1)S(1)}, u32[]{:S(2)}, u32[]{:S(2)}) collective-permute-start(bf16[64,768]{1,0:T(8,128)(2,1)S(1)} %get-tuple-element.38), channel_id=1, source_target_pairs={{0,28},{4,24},{8,20},{12,16},{16,12},{20,8},{24,4},{28,0},{1,29},{... | collective-permute-start | bytes 294920 | tf_op jit(solution)/shard_map/ppermute | solution.py:306
  40.7 10.0 %collective-permute-start.6 = (bf16[128,768]{1,0:T(8,128)(2,1)S(1)}, bf16[128,768]{1,0:T(8,128)(2,1)S(1)}, u32[]{:S(2)}, u32[]{:S(2)}) collective-permute-start(bf16[128,768]{1,0:T(8,128)(2,1)S(1)} %get-tuple-element.39.refs_4_), channel_id=1, source_target_pairs={{0,8},{4,12},{8,0},{12,4},{16,24},{20,28},{24,16},{28,20},{1,9},{5... | collective-permute-start | bytes 589832 | tf_op jit(solution)/shard_map/ppermute | solution.py:306
  42.1 10.9 %collective-permute-start.7 = (bf16[128,768]{1,0:T(8,128)(2,1)S(1)}, bf16[128,768]{1,0:T(8,128)(2,1)S(1)}, u32[]{:S(2)}, u32[]{:S(2)}) collective-permute-start(bf16[128,768]{1,0:T(8,128)(2,1)S(1)} %get-tuple-element.40.refs_6_), channel_id=1, source_target_pairs={{0,16},{4,20},{8,24},{12,28},{16,0},{20,4},{24,8},{28,12},{1,17},{... | collective-permute-start | bytes 589832 | tf_op jit(solution)/shard_map/ppermute | solution.py:306
  43.6 8.0 %copy-start.3 = (bf16[128,768]{1,0:T(8,128)(2,1)S(1)}, bf16[128,768]{1,0:T(8,128)(2,1)}, u32[]{:S(2)}) copy-start(bf16[128,768]{1,0:T(8,128)(2,1)} %refs_1_.4) | copy-start | bytes 589828
  43.6 8.0 %copy-start.5 = (bf16[128,768]{1,0:T(8,128)(2,1)S(1)}, bf16[128,768]{1,0:T(8,128)(2,1)}, u32[]{:S(2)}) copy-start(bf16[128,768]{1,0:T(8,128)(2,1)} %refs_2_.3) | copy-start | bytes 589828
  46.8 9.0 %collective-permute-start.15 = (bf16[128,768]{1,0:T(8,128)(2,1)S(1)}, bf16[128,768]{1,0:T(8,128)(2,1)S(1)}, u32[]{:S(2)}, u32[]{:S(2)}) collective-permute-start(bf16[128,768]{1,0:T(8,128)(2,1)S(1)} %get-tuple-element.48.refs_5_), channel_id=1, source_target_pairs={{0,12},{4,8},{8,4},{12,0},{16,28},{20,24},{24,20},{28,16},{1,13},{... | collective-permute-start | bytes 589832 | tf_op jit(solution)/shard_map/ppermute | solution.py:306
  47.3 8.5 %collective-permute-start.16 = (bf16[128,768]{1,0:T(8,128)(2,1)S(1)}, bf16[128,768]{1,0:T(8,128)(2,1)S(1)}, u32[]{:S(2)}, u32[]{:S(2)}) collective-permute-start(bf16[128,768]{1,0:T(8,128)(2,1)S(1)} %get-tuple-element.49.refs_7_), channel_id=1, source_target_pairs={{0,20},{4,16},{8,28},{12,24},{16,4},{20,0},{24,12},{28,8},{1,21},{... | collective-permute-start | bytes 589832 | tf_op jit(solution)/shard_map/ppermute | solution.py:306
  48.0 6.7 %collective-permute-start.13 = (bf16[64,768]{1,0:T(8,128)(2,1)S(1)}, bf16[64,768]{1,0:T(8,128)(2,1)S(1)}, u32[]{:S(2)}, u32[]{:S(2)}) collective-permute-start(bf16[64,768]{1,0:T(8,128)(2,1)S(1)} %collective-permute-done.4.refs_2_), channel_id=1, source_target_pairs={{0,1},{1,0},{2,3},{3,2},{4,5},{5,4},{6,7},{7,6},{8,9},{9,8},{10,11... | collective-permute-start | bytes 294920 | tf_op jit(solution)/shard_map/ppermute | solution.py:386
  50.7 5.1 %collective-permute-start.14 = (bf16[64,768]{1,0:T(8,128)(2,1)S(1)}, bf16[64,768]{1,0:T(8,128)(2,1)S(1)}, u32[]{:S(2)}, u32[]{:S(2)}) collective-permute-start(bf16[64,768]{1,0:T(8,128)(2,1)S(1)} %collective-permute-done.5.refs_3_), channel_id=1, source_target_pairs={{0,1},{1,0},{2,3},{3,2},{4,5},{5,4},{6,7},{7,6},{8,9},{9,8},{10,11... | collective-permute-start | bytes 294920 | tf_op jit(solution)/shard_map/ppermute | solution.py:386
  53.0 2.8 %copy-start.7 = (bf16[128,768]{1,0:T(8,128)(2,1)S(1)}, bf16[128,768]{1,0:T(8,128)(2,1)}, u32[]{:S(2)}) copy-start(bf16[128,768]{1,0:T(8,128)(2,1)} %get-tuple-element.26.refs_11_) | copy-start | bytes 589828

commit v6 on v5

--- a/solution.py
+++ b/solution.py
@@ -10,9 +10,10 @@
 HD = 128
 HEADER = 8
 FIRST = (0,6,7,2,4,1)
-LAST = (16,17,3,5)
-LATE = (16,17,3,5)
+LAST = (20,3,5)
+LATE = (20,3,5)
 HALVED = (6, 7)
+SWAPPED = 20
 
 
 def normalize(rows, norm_gain):
@@ -147,7 +148,7 @@
     return mean, jnp.sum(centred * centred, axis=-1, keepdims=True)
 
 
-def stats_kernel(info, own, one, two, stats_ref, arranged):
+def stats_kernel(info, own, two, one, stats_ref, arranged):
     for index, ref in enumerate((own, one, two)):
         arranged[index ^ info[2]] = ref[...]
     rows = own.shape[0]
@@ -189,8 +190,8 @@
 
 
 def pack_kernel(*refs):
-    for index, ref in enumerate(refs[:4]):
-        refs[4][index] = ref[...]
+    for index, ref in enumerate(refs[:-1]):
+        refs[-1][index] = ref[...]
 
 
 def project_kernel(info, weight_ref, *refs):
@@ -234,16 +235,21 @@
     refs = list(refs)
     chip_values, mate_values = refs[-5:-1], refs[-1]
     left, right = [], []
+
+    def rows_of(offset, swapped=None):
+        values = mate_values.at[offset // 2] if offset % 2 else chip_values[offset // 2]
+        if swapped is None:
+            return values[...]
+        rows = values.shape[0] // 2
+        side = (info[2] + swapped) % 2
+        return values[pl.ds(pl.multiple_of(side * rows, rows), rows), :]
+
     for name in names:
-        offset = name % 10
-        values = mate_values.at[offset // 2] if offset % 2 else chip_values[offset // 2]
         left.append(refs.pop(0)[...])
-        if offset in HALVED:
-            rows = left[-1].shape[0]
-            side = (info[2] + name // 10) % 2
-            right.append(values[pl.ds(pl.multiple_of(side * rows, rows), rows), :])
+        if name == SWAPPED:
+            right.extend(rows_of(offset, 1) for offset in HALVED)
         else:
-            right.append(values[...])
+            right.append(rows_of(name, 0 if name in HALVED else None))
     return jnp.concatenate(left, axis=0), jnp.concatenate(right, axis=0)
 
 
@@ -354,7 +360,7 @@
     stats, arranged = call(
         stats_kernel, "partial_stats", (shape((rows, 128), jnp.float32), shape((4, rows, columns))),
         [SMEM] + [WHOLE] * 3, (WHOLE, WHOLE), after=(value_weight,),
-    )(info, middle, first_one, passed)
+    )(info, middle, passed, first_one)
     *normed, = call(
         norm_kernel, "norm_rows", (block,) * 8 + (shape((rows // 2, half)),) * len(HALVED),
         [SMEM] + [WHOLE] * 5, (WHOLE,) * (8 + len(HALVED)), (pltpu.VMEM((rows, columns), jnp.bfloat16),),
@@ -377,16 +383,16 @@
     for offset in range(2, 8):
         if offset not in LATE:
             moved[offset] = across(sources[offset], offset)
-    held = [sources[name] if name < 10 else moved[name % 10] for name in LATE]
-    held = lax.optimization_barrier(held + [values])
+    swapped = call(pack_kernel, "pack_halves", shape((2, rows // 2, half)), [WHOLE] * 2, WHOLE, after=(values,))(
+        *[moved[offset] for offset in HALVED]
+    )
+    sources[SWAPPED] = swapped.reshape(rows, half)
+    held = lax.optimization_barrier([sources[name] for name in LATE] + [values])
     for name, part in zip(LATE, held):
-        if name < 10:
+        if name == SWAPPED:
+            moved[name] = lax.ppermute(part, "mp", [(0, 1), (1, 0), (2, 3), (3, 2)])
+        else:
             moved[name] = across(part, name)
-        else:
-            moved[name] = lax.ppermute(part, "mp", [(0, 1), (1, 0), (2, 3), (3, 2)])
-    for offset in HALVED:
-        if offset + 10 not in moved:
-            moved[offset + 10] = lax.ppermute(moved[offset], "mp", [(0, 1), (1, 0), (2, 3), (3, 2)])
 
     def arrived(names):
         return [moved[name] for name in names] + chip_values + [mate_values]

time: 58.6 us -> 58 us (0.990)
  starting transfers between devices: 23.7 us -> 22.8 us
    ppermute x2 -> x1, starting transfers between devices: 1.61 us -> 0.62 us  [fast_body(): moved[name] = lax.ppermute(part, 'mp', [(0, 1), (1, 0), (2, 3), (3, 2)])]
    pallas_call x9 -> x10, Pallas kernels: 12.3 us -> 12.3 us  [call(): return lambda *args: made(*args, *after)]
  transfers between devices with their start and end apart: 18 -> 17, of which waited for: 7 -> 10; matrix products, arithmetic and copies ran while one was open for 3% -> 3% of each run, Pallas kernels for 17% -> 17%
where the time goes in v6:
time: 58 us; the launch traced here: 57.6 us
  starting transfers between devices  22.8 us (39%)
  waiting for transfers between devices  14.7 us (25%)
  Pallas kernels  12.3 us (21%)
  local copies, waits for them, and re-layouts  7.09 us (12%)
  between operations  0.78 us (1%)
    pallas_call x10, Pallas kernels, call(): return lambda *args: made(*args, *after)  12.3 us
    ppermute x11, starting transfers between devices, across(): return lax.ppermute(rows, 'dp', [(i, i ^ distance) for i in range(8)])  10.8 us
    unnamed x16, local copies, waits for them, and re-layouts  5.56 us
    ppermute x1, starting transfers between devices, fast_body(): two = lax.ppermute(patches, 'mp', [(0, 2), (2, 0), (1, 3), (3, 1)])  4.1 us
    all_to_all x1, waiting for transfers between devices, fast_body(): lax.all_to_all(head_cotangent.reshape(8, slots // 8, width), 'dp', split_...  3.93 us
    all_to_all x1, starting transfers between devices, fast_body(): lax.all_to_all(head_cotangent.reshape(8, slots // 8, width), 'dp', split_...  3.72 us
    ppermute x11, waiting for transfers between devices, across(): return lax.ppermute(rows, 'dp', [(i, i ^ distance) for i in range(8)])  3.5 us
    ppermute x1, waiting for transfers between devices, fast_body(): two = lax.ppermute(patches, 'mp', [(0, 2), (2, 0), (1, 3), (3, 1)])  3.22 us
  transfers between devices with their start and end apart: 17, of which 10 were waited for; matrix products, arithmetic and copies ran while one was open for 3% of the time, Pallas kernels for 17%

profile of v6, /device:TPU:0, one launch (start us, length us, event | category | flops | bytes accessed | tf_op | source)
XLA Modules:
  0.0 57.6 jit_solution(6576781607286544251)
XLA Ops:
  0.6 0.0 copy-start.6
  0.6 4.1 %collective-permute-start = (bf16[128,1536]{1,0:T(8,128)(2,1)}, bf16[128,1536]{1,0:T(8,128)(2,1)S(1)}, u32[]{:S(2)}, u32[]{:S(2)}) collective-permute-start(bf16[128,1536]{1,0:T(8,128)(2,1)} %refs_1_.2), channel_id=1, source_target_pairs={{0,2},{2,0},{1,3},{3,1},{4,6},{6,4},{5,7},{7,5},{8,10},{10,8},{9,1... | collective-permute-start | bytes 1179656 | tf_op jit(solution)/shard_map/ppermute | solution.py:343
  4.7 1.6 %collective-permute-start.1 = (bf16[128,1536]{1,0:T(8,128)(2,1)}, bf16[128,1536]{1,0:T(8,128)(2,1)S(1)}, u32[]{:S(2)}, u32[]{:S(2)}) collective-permute-start(bf16[128,1536]{1,0:T(8,128)(2,1)} %refs_1_.2), channel_id=1, source_target_pairs={{0,1},{1,0},{2,3},{3,2},{4,5},{5,4},{6,7},{7,6},{8,9},{9,8},{10,11... | collective-permute-start | bytes 1179656 | tf_op jit(solution)/shard_map/ppermute | solution.py:344
  6.3 3.7 %all-to-all-start = ((bf16[8,32,768]{2,1,0:T(8,128)(2,1)}), bf16[8,32,768]{2,1,0:T(8,128)(2,1)S(1)}, u32[]{:S(2)}, u32[]{:S(2)}) async-start(bf16[8,32,768]{2,1,0:T(8,128)(2,1)} %bitcast.12), calls=%async_computation | async-start | bytes 786432 | tf_op jit(solution)/shard_map/all_to_all | solution.py:340
  10.0 0.7 %reshape.20.refs_1_ = f32[8,768]{1,0:T(8,128)S(1)} reshape(f32[6144]{0:T(1024)} %param.9) | data formatting | bytes 49152 | tf_op jit(solution)/shard_map/reshape | solution.py:349
  10.8 0.7 %dynamic-slice_bitcast_fusion = (s32[8]{0:T(128)S(1)}, s32[8]{0:T(128)S(1)}) fusion(s32[8,8]{1,0:T(8,128)} %param.15, s32[]{:T(128)S(6)} %select_n.18, s32[8,8]{1,0:T(8,128)} %param.14), kind=kLoop, calls=%fused_computation | loop fusion | bytes 132 | tf_op jit(solution)/shard_map/jit(dynamic_index_in_dim)/squeeze | solution.py:336
  11.5 0.1 concatenate.3.refs_0_
  11.6 0.0 copy-start.2
  11.6 0.9 %copy-done.2 = bf16[128,768]{1,0:T(8,128)(2,1)S(1)} copy-done((bf16[128,768]{1,0:T(8,128)(2,1)S(1)}, bf16[128,768]{1,0:T(8,128)(2,1)}, u32[]{:S(2)}) %copy-start.2) | copy-done | bytes 196632
  12.5 0.0 copy-start.4
  12.5 0.9 %copy-done.4 = bf16[128,768]{1,0:T(8,128)(2,1)S(1)} copy-done((bf16[128,768]{1,0:T(8,128)(2,1)S(1)}, bf16[128,768]{1,0:T(8,128)(2,1)}, u32[]{:S(2)}) %copy-start.4) | copy-done | bytes 196632
  13.4 1.0 %attention_weights.1 = (f32[6,128,128]{2,1,0:T(8,128)S(1)}, f32[8,768]{1,0:T(8,128)S(1)}) custom-call(s32[24]{0:T(128)S(1)} %concatenate.3.refs_0_, f32[8,768]{1,0:T(8,128)S(1)} %reshape.20.refs_1_, bf16[128,768]{1,0:T(8,128)(2,1)S(1)} %copy-done.2, bf16[128,768]{1,0:T(8,128)(2,1)S(1)} %copy-done.4), custom_call_target="tpu_custom_call" | custom-call | flops 1 | bytes 1 | tf_op jit(solution)/shard_map/attention_weights/pallas_call | solution.py:308
  14.5 3.9 %all-to-all-done = bf16[8,32,768]{2,1,0:T(8,128)(2,1)S(1)} async-done(((bf16[8,32,768]{2,1,0:T(8,128)(2,1)}), bf16[8,32,768]{2,1,0:T(8,128)(2,1)S(1)}, u32[]{:S(2)}, u32[]{:S(2)}) %all-to-all-start) | async-done | bytes 393248 | tf_op jit(solution)/shard_map/all_to_all | solution.py:340
  18.4 1.0 %value_rows.1 = (bf16[128,768]{1,0:T(8,128)(2,1)S(1)}, bf16[128,768]{1,0:T(8,128)(2,1)S(1)}) custom-call(s32[24]{0:T(128)S(1)} %concatenate.3.refs_0_, bf16[256,768]{1,0:T(8,128)(2,1)S(1)} %bitcast.10, f32[6,128,128]{2,1,0:T(8,128)S(1)} %get-tuple-element.27.refs_2_.refs_4_), custom_call_target="tpu_custom_call" | custom-call | flops 1 | bytes 1 | tf_op jit(solution)/shard_map/value_rows/pallas_call | solution.py:308
  19.4 3.2 %collective-permute-done.refs_2_ = bf16[128,1536]{1,0:T(8,128)(2,1)S(1)} collective-permute-done((bf16[128,1536]{1,0:T(8,128)(2,1)}, bf16[128,1536]{1,0:T(8,128)(2,1)S(1)}, u32[]{:S(2)}, u32[]{:S(2)}) %collective-permute-start) | collective-permute-done | bytes 393248 | tf_op jit(solution)/shard_map/ppermute | solution.py:343
  22.6 0.2 collective-permute-done.1.refs_3_
  22.8 0.7 %collective-permute-start.2 = (bf16[128,1536]{1,0:T(8,128)(2,1)}, bf16[128,1536]{1,0:T(8,128)(2,1)S(1)}, u32[]{:S(2)}, u32[]{:S(2)}) collective-permute-start(bf16[128,1536]{1,0:T(8,128)(2,1)} %refs_1_.2), channel_id=1, source_target_pairs={{1,2},{2,1},{5,6},{6,5},{9,10},{10,9},{13,14},{14,13},{17,18},{18,... | collective-permute-start | bytes 1179656 | tf_op jit(solution)/shard_map/ppermute | solution.py:355
  23.5 1.3 %collective-permute-start.3 = (bf16[128,1536]{1,0:T(8,128)(2,1)S(1)}, bf16[128,1536]{1,0:T(8,128)(2,1)S(1)}, u32[]{:S(2)}, u32[]{:S(2)}) collective-permute-start(bf16[128,1536]{1,0:T(8,128)(2,1)S(1)} %collective-permute-done.refs_2_), channel_id=1, source_target_pairs={{2,3},{1,0},{6,7},{5,4},{10,11},{9,8},{14,15},{13,12},{18,19},{17,... | collective-permute-start | bytes 1179656 | tf_op jit(solution)/shard_map/ppermute | solution.py:356
  24.8 2.6 %collective-permute-start.11 = (bf16[128,768]{1,0:T(8,128)(2,1)S(1)}, bf16[128,768]{1,0:T(8,128)(2,1)S(1)}, u32[]{:S(2)}, u32[]{:S(2)}) collective-permute-start(bf16[128,768]{1,0:T(8,128)(2,1)S(1)} %get-tuple-element.28.refs_0_.refs_7_.refs_5_), channel_id=1, source_target_pairs={{0,24},{4,28},{8,16},{12,20},{16,8},{20,12},{24,0},{28,4},{1,25},{... | collective-permute-start | bytes 589832 | tf_op jit(solution)/shard_map/ppermute | solution.py:312
  27.3 0.5 collective-permute-start.10
  27.8 0.5 collective-permute-start.9
  28.3 0.0 copy-done.6
  28.3 0.0 copy-start
  28.3 3.7 %copy-done = bf16[6144,768]{1,0:T(8,128)(2,1)S(1)} copy-done((bf16[6144,768]{1,0:T(8,128)(2,1)S(1)}, bf16[6144,768]{1,0:T(8,128)(2,1)}, u32[]{:S(2)}) %copy-start) | copy-done | bytes 9437208
  32.0 0.0 copy-start.1
  32.0 1.2 %partial_stats.1 = (f32[128,128]{1,0:T(8,128)S(1)}, bf16[4,128,1536]{2,1,0:T(8,128)(2,1)S(1)}) custom-call(s32[24]{0:T(128)S(1)} %concatenate.3.refs_0_, bf16[128,1536]{1,0:T(8,128)(2,1)S(1)} %copy-done.6, bf16[128,1536]{1,0:T(8,128)(2,1)S(1)} %collective-permute-done.refs_2_, bf16[128,1536]{1,0:T(8,128)(2,1)S(1)} %collective-permute-done.1.refs_3_, ...), custom_call_target="tpu_custom_call" | custom-call | flops 1 | bytes 1 | tf_op jit(solution)/shard_map/partial_stats/pallas_call | solution.py:308
  33.2 0.0 collective-permute-done.2.refs_4_
  33.2 2.7 %collective-permute-done.3.refs_5_ = bf16[128,1536]{1,0:T(8,128)(2,1)S(1)} collective-permute-done((bf16[128,1536]{1,0:T(8,128)(2,1)S(1)}, bf16[128,1536]{1,0:T(8,128)(2,1)S(1)}, u32[]{:S(2)}, u32[]{:S(2)}) %collective-permute-start.3) | collective-permute-done | bytes 393248 | tf_op jit(solution)/shard_map/ppermute | solution.py:356
  35.9 1.7 %norm_rows.1 = (bf16[128,768]{1,0:T(8,128)(2,1)S(1)}, bf16[128,768]{1,0:T(8,128)(2,1)S(1)}, bf16[128,768]{1,0:T(8,128)(2,1)S(1)}, bf16[128,768]{1,0:T(8,128)(2,1...) custom-call(s32[24]{0:T(128)S(1)} %concatenate.3.refs_0_, ...), custom_call_target="tpu_custom_call" | custom-call | flops 1 | bytes 1 | tf_op jit(solution)/shard_map/norm_rows/pallas_call | solution.py:308
  37.6 0.0 collective-permute-done.11.refs_3_.refs_10_.refs_8_
  37.6 0.0 collective-permute-done.10.refs_2_.refs_9_.refs_7_
  37.6 0.0 collective-permute-done.9.refs_1_.refs_8_.refs_6_
  37.6 0.1 pack_values.1
  37.7 0.1 collective-permute-start.12
  37.8 0.5 collective-permute-start.8
  38.3 2.4 %collective-permute-start.4 = (bf16[64,768]{1,0:T(8,128)(2,1)S(1)}, bf16[64,768]{1,0:T(8,128)(2,1)S(1)}, u32[]{:S(2)}, u32[]{:S(2)}) collective-permute-start(bf16[64,768]{1,0:T(8,128)(2,1)S(1)} %get-tuple-element.36), channel_id=1, source_target_pairs={{0,24},{4,28},{8,16},{12,20},{16,8},{20,12},{24,0},{28,4},{1,25},{... | collective-permute-start | bytes 294920 | tf_op jit(solution)/shard_map/ppermute | solution.py:312
  40.7 0.0 collective-permute-start.5
  40.7 1.4 %collective-permute-start.6 = (bf16[128,768]{1,0:T(8,128)(2,1)S(1)}, bf16[128,768]{1,0:T(8,128)(2,1)S(1)}, u32[]{:S(2)}, u32[]{:S(2)}) collective-permute-start(bf16[128,768]{1,0:T(8,128)(2,1)S(1)} %get-tuple-element.38.refs_4_), channel_id=1, source_target_pairs={{0,8},{4,12},{8,0},{12,4},{16,24},{20,28},{24,16},{28,20},{1,9},{5... | collective-permute-start | bytes 589832 | tf_op jit(solution)/shard_map/ppermute | solution.py:312
  42.1 0.0 collective-permute-done.8.refs_6_.refs_11_
  42.1 1.5 %collective-permute-start.7 = (bf16[128,768]{1,0:T(8,128)(2,1)S(1)}, bf16[128,768]{1,0:T(8,128)(2,1)S(1)}, u32[]{:S(2)}, u32[]{:S(2)}) collective-permute-start(bf16[128,768]{1,0:T(8,128)(2,1)S(1)} %get-tuple-element.39.refs_6_), channel_id=1, source_target_pairs={{0,16},{4,20},{8,24},{12,28},{16,0},{20,4},{24,8},{28,12},{1,17},{... | collective-permute-start | bytes 589832 | tf_op jit(solution)/shard_map/ppermute | solution.py:312
  43.6 0.0 collective-permute-done.12.refs_11_.refs_10_.refs_9_
  43.6 0.0 copy-done.1
  43.6 0.0 copy-start.3
  43.6 0.0 copy-start.5
  43.6 2.0 %project_values.1.refs_2_.refs_0_ = bf16[128,768]{1,0:T(8,128)(2,1)S(1)} custom-call(s32[24]{0:T(128)S(1)} %concatenate.3.refs_0_, bf16[6144,768]{1,0:T(8,128)(2,1)S(1)} %copy-done.1, bf16[128,768]{1,0:T(8,128)(2,1)S(1)} %get-tuple-element.35.refs_1_.refs_2_, bf16[128,768]{1,0:T(8,128)(2,1)S(1)} %get-tuple-element.40.refs_4_.refs_3_, ...), custom_call_target="tpu_custom_call" | custom-call | flops 1 | bytes 1 | tf_op jit(solution)/shard_map/project_values/pallas_call | solution.py:308
  45.6 0.0 collective-permute-done.4.refs_2_.refs_0_
  45.6 1.2 %collective-permute-done.5.refs_3_.refs_1_ = bf16[64,768]{1,0:T(8,128)(2,1)S(1)} collective-permute-done((bf16[64,768]{1,0:T(8,128)(2,1)S(1)}, bf16[64,768]{1,0:T(8,128)(2,1)S(1)}, u32[]{:S(2)}, u32[]{:S(2)}) %collective-permute-start.5) | collective-permute-done | bytes 98336 | tf_op jit(solution)/shard_map/ppermute | solution.py:312
  46.8 0.6 %collective-permute-start.13 = (bf16[128,768]{1,0:T(8,128)(2,1)S(1)}, bf16[128,768]{1,0:T(8,128)(2,1)S(1)}, u32[]{:S(2)}, u32[]{:S(2)}) collective-permute-start(bf16[128,768]{1,0:T(8,128)(2,1)S(1)} %bitcast.11), channel_id=1, source_target_pairs={{0,1},{1,0},{2,3},{3,2},{4,5},{5,4},{6,7},{7,6},{8,9},{9,8},{10,11... | collective-permute-start | bytes 589832 | tf_op jit(solution)/shard_map/ppermute | solution.py:393
  47.4 0.9 %collective-permute-start.14 = (bf16[128,768]{1,0:T(8,128)(2,1)S(1)}, bf16[128,768]{1,0:T(8,128)(2,1)S(1)}, u32[]{:S(2)}, u32[]{:S(2)}) collective-permute-start(bf16[128,768]{1,0:T(8,128)(2,1)S(1)} %get-tuple-element.46.refs_5_), channel_id=1, source_target_pairs={{0,12},{4,8},{8,4},{12,0},{16,28},{20,24},{24,20},{28,16},{1,13},{... | collective-permute-start | bytes 589832 | tf_op jit(solution)/shard_map/ppermute | solution.py:312
  48.3 0.4 collective-permute-start.15
  48.7 0.0 copy-done.3
  48.8 0.0 copy-done.5
  48.8 1.4 %attention_backward.1 = (bf16[128,768]{1,0:T(8,128)(2,1)}, bf16[128,768]{1,0:T(8,128)(2,1)}) custom-call(bf16[128,768]{1,0:T(8,128)(2,1)S(1)} %project_values.1.refs_2_.refs_0_, bf16[128,768]{1,0:T(8,128)(2,1)S(1)} %copy-done.3, bf16[128,768]{1,0:T(8,128)(2,1)S(1)} %copy-done.5, bf16[128,768]{1,0:T(8,128)(2,1)S(1)} %get-tuple-element.48.refs_3_, ...), custom_call_target="tpu_custom_call" | custom-call | flops 1 | bytes 1 | tf_op jit(solution)/shard_map/attention_backward/pallas_call | solution.py:308
  50.1 0.0 copy-start.7
  50.1 0.2 collective-permute-done.6.refs_4_
  50.3 0.6 %collective-permute-done.7.refs_5_ = bf16[128,768]{1,0:T(8,128)(2,1)S(1)} collective-permute-done((bf16[128,768]{1,0:T(8,128)(2,1)S(1)}, bf16[128,768]{1,0:T(8,128)(2,1)S(1)}, u32[]{:S(2)}, u32[]{:S(2)}) %collective-permute-start.7) | collective-permute-done | bytes 196640 | tf_op jit(solution)/shard_map/ppermute | solution.py:312
  50.9 1.7 %gradient_first.1.refs_1_ = f32[768,768]{1,0:T(8,128)S(1)} custom-call(s32[24]{0:T(128)S(1)} %concatenate.3.refs_0_, bf16[128,768]{1,0:T(8,128)(2,1)S(1)} %get-tuple-element.35.refs_1_.refs_2_, bf16[64,768]{1,0:T(8,128)(2,1)S(1)} %collective-permute-done.4.refs_2_.refs_0_, bf16[64,768]{1,0:T(8,128)(2,1)S(1)} %collective-permute-done.5.refs_3_.refs_1_, ...), custom_call_target="tpu_custom_call" | custom-call | flops 1 | bytes 1 | tf_op jit(solution)/shard_map/gradient_first/pallas_call | solution.py:308
  52.6 1.1 %collective-permute-done.13.refs_2_ = bf16[128,768]{1,0:T(8,128)(2,1)S(1)} collective-permute-done((bf16[128,768]{1,0:T(8,128)(2,1)S(1)}, bf16[128,768]{1,0:T(8,128)(2,1)S(1)}, u32[]{:S(2)}, u32[]{:S(2)}) %collective-permute-start.13) | collective-permute-done | bytes 196640 | tf_op jit(solution)/shard_map/ppermute | solution.py:393
  53.7 0.9 %collective-permute-done.14.refs_3_ = bf16[128,768]{1,0:T(8,128)(2,1)S(1)} collective-permute-done((bf16[128,768]{1,0:T(8,128)(2,1)S(1)}, bf16[128,768]{1,0:T(8,128)(2,1)S(1)}, u32[]{:S(2)}, u32[]{:S(2)}) %collective-permute-start.14) | collective-permute-done | bytes 196640 | tf_op jit(solution)/shard_map/ppermute | solution.py:312
  54.5 0.7 %collective-permute-done.15.refs_4_ = bf16[128,768]{1,0:T(8,128)(2,1)S(1)} collective-permute-done((bf16[128,768]{1,0:T(8,128)(2,1)S(1)}, bf16[128,768]{1,0:T(8,128)(2,1)S(1)}, u32[]{:S(2)}, u32[]{:S(2)}) %collective-permute-start.15) | collective-permute-done | bytes 196640 | tf_op jit(solution)/shard_map/ppermute | solution.py:312
  55.2 0.0 copy-done.7
  55.2 2.4 %gradient_last.1 = f32[768,768]{1,0:T(8,128)} custom-call(s32[24]{0:T(128)S(1)} %concatenate.3.refs_0_, f32[768,768]{1,0:T(8,128)S(1)} %gradient_first.1.refs_1_, bf16[128,768]{1,0:T(8,128)(2,1)S(1)} %collective-permute-done.13.refs_2_, bf16[128,768]{1,0:T(8,128)(2,1)S(1)} %collective-permute-done.14.refs_3_, ...), custom_call_target="tpu_custom_call" | custom-call | flops 1 | bytes 1 | tf_op jit(solution)/shard_map/gradient_last/pallas_call | solution.py:308
  (2 shorter events, 0.0 us)
Async XLA Ops:
  0.6 27.7 %copy-start.6 = (bf16[128,1536]{1,0:T(8,128)(2,1)S(1)}, bf16[128,1536]{1,0:T(8,128)(2,1)}, u32[]{:S(2)}) copy-start(bf16[128,1536]{1,0:T(8,128)(2,1)} %refs_1_.2) | copy-start | bytes 1179652
  0.6 22.0 %collective-permute-start = (bf16[128,1536]{1,0:T(8,128)(2,1)}, bf16[128,1536]{1,0:T(8,128)(2,1)S(1)}, u32[]{:S(2)}, u32[]{:S(2)}) collective-permute-start(bf16[128,1536]{1,0:T(8,128)(2,1)} %refs_1_.2), channel_id=1, source_target_pairs={{0,2},{2,0},{1,3},{3,1},{4,6},{6,4},{5,7},{7,5},{8,10},{10,8},{9,1... | collective-permute-start | bytes 1179656 | tf_op jit(solution)/shard_map/ppermute | solution.py:343
  4.7 18.0 %collective-permute-start.1 = (bf16[128,1536]{1,0:T(8,128)(2,1)}, bf16[128,1536]{1,0:T(8,128)(2,1)S(1)}, u32[]{:S(2)}, u32[]{:S(2)}) collective-permute-start(bf16[128,1536]{1,0:T(8,128)(2,1)} %refs_1_.2), channel_id=1, source_target_pairs={{0,1},{1,0},{2,3},{3,2},{4,5},{5,4},{6,7},{7,6},{8,9},{9,8},{10,11... | collective-permute-start | bytes 1179656 | tf_op jit(solution)/shard_map/ppermute | solution.py:344
  6.3 12.1 %all-to-all-start = ((bf16[8,32,768]{2,1,0:T(8,128)(2,1)}), bf16[8,32,768]{2,1,0:T(8,128)(2,1)S(1)}, u32[]{:S(2)}, u32[]{:S(2)}) async-start(bf16[8,32,768]{2,1,0:T(8,128)(2,1)} %bitcast.12), calls=%async_computation | async-start | bytes 786432 | tf_op jit(solution)/shard_map/all_to_all | solution.py:340
  11.6 0.9 %copy-start.2 = (bf16[128,768]{1,0:T(8,128)(2,1)S(1)}, bf16[128,768]{1,0:T(8,128)(2,1)}, u32[]{:S(2)}) copy-start(bf16[128,768]{1,0:T(8,128)(2,1)} %refs_1_.4) | copy-start | bytes 589828
  12.5 0.9 %copy-start.4 = (bf16[128,768]{1,0:T(8,128)(2,1)S(1)}, bf16[128,768]{1,0:T(8,128)(2,1)}, u32[]{:S(2)}) copy-start(bf16[128,768]{1,0:T(8,128)(2,1)} %refs_2_.3) | copy-start | bytes 589828
  22.8 10.4 %collective-permute-start.2 = (bf16[128,1536]{1,0:T(8,128)(2,1)}, bf16[128,1536]{1,0:T(8,128)(2,1)S(1)}, u32[]{:S(2)}, u32[]{:S(2)}) collective-permute-start(bf16[128,1536]{1,0:T(8,128)(2,1)} %refs_1_.2), channel_id=1, source_target_pairs={{1,2},{2,1},{5,6},{6,5},{9,10},{10,9},{13,14},{14,13},{17,18},{18,... | collective-permute-start | bytes 1179656 | tf_op jit(solution)/shard_map/ppermute | solution.py:355
  23.5 12.4 %collective-permute-start.3 = (bf16[128,1536]{1,0:T(8,128)(2,1)S(1)}, bf16[128,1536]{1,0:T(8,128)(2,1)S(1)}, u32[]{:S(2)}, u32[]{:S(2)}) collective-permute-start(bf16[128,1536]{1,0:T(8,128)(2,1)S(1)} %collective-permute-done.refs_2_), channel_id=1, source_target_pairs={{2,3},{1,0},{6,7},{5,4},{10,11},{9,8},{14,15},{13,12},{18,19},{17,... | collective-permute-start | bytes 1179656 | tf_op jit(solution)/shard_map/ppermute | solution.py:356
  24.8 12.8 %collective-permute-start.11 = (bf16[128,768]{1,0:T(8,128)(2,1)S(1)}, bf16[128,768]{1,0:T(8,128)(2,1)S(1)}, u32[]{:S(2)}, u32[]{:S(2)}) collective-permute-start(bf16[128,768]{1,0:T(8,128)(2,1)S(1)} %get-tuple-element.28.refs_0_.refs_7_.refs_5_), channel_id=1, source_target_pairs={{0,24},{4,28},{8,16},{12,20},{16,8},{20,12},{24,0},{28,4},{1,25},{... | collective-permute-start | bytes 589832 | tf_op jit(solution)/shard_map/ppermute | solution.py:312
  27.3 10.3 %collective-permute-start.10 = (bf16[128,768]{1,0:T(8,128)(2,1)S(1)}, bf16[128,768]{1,0:T(8,128)(2,1)S(1)}, u32[]{:S(2)}, u32[]{:S(2)}) collective-permute-start(bf16[128,768]{1,0:T(8,128)(2,1)S(1)} %get-tuple-element.28.refs_0_.refs_7_.refs_5_), channel_id=1, source_target_pairs={{0,16},{4,20},{8,24},{12,28},{16,0},{20,4},{24,8},{28,12},{1,17},{... | collective-permute-start | bytes 589832 | tf_op jit(solution)/shard_map/ppermute | solution.py:312
  27.8 9.8 %collective-permute-start.9 = (bf16[128,768]{1,0:T(8,128)(2,1)S(1)}, bf16[128,768]{1,0:T(8,128)(2,1)S(1)}, u32[]{:S(2)}, u32[]{:S(2)}) collective-permute-start(bf16[128,768]{1,0:T(8,128)(2,1)S(1)} %get-tuple-element.28.refs_0_.refs_7_.refs_5_), channel_id=1, source_target_pairs={{0,8},{4,12},{8,0},{12,4},{16,24},{20,28},{24,16},{28,20},{1,9},{5... | collective-permute-start | bytes 589832 | tf_op jit(solution)/shard_map/ppermute | solution.py:312
  28.3 3.7 %copy-start = (bf16[6144,768]{1,0:T(8,128)(2,1)S(1)}, bf16[6144,768]{1,0:T(8,128)(2,1)}, u32[]{:S(2)}) copy-start(bf16[6144,768]{1,0:T(8,128)(2,1)} %refs_1_.3) | copy-start | bytes 28311556
  32.0 11.6 %copy-start.1 = (bf16[6144,768]{1,0:T(8,128)(2,1)S(1)}, bf16[6144,768]{1,0:T(8,128)(2,1)}, u32[]{:S(2)}) copy-start(bf16[6144,768]{1,0:T(8,128)(2,1)} %refs_1_.3) | copy-start | bytes 28311556
  37.7 5.9 %collective-permute-start.12 = (bf16[4,128,768]{2,1,0:T(8,128)(2,1)S(1)}, bf16[4,128,768]{2,1,0:T(8,128)(2,1)S(1)}, u32[]{:S(2)}, u32[]{:S(2)}) collective-permute-start(bf16[4,128,768]{2,1,0:T(8,128)(2,1)S(1)} %pack_values.1), channel_id=1, source_target_pairs={{0,4},{4,0},{8,12},{12,8},{16,20},{20,16},{24,28},{28,24},{1,5},{5... | collective-permute-start | bytes 2359304 | tf_op jit(solution)/shard_map/ppermute | solution.py:312
  37.8 4.3 %collective-permute-start.8 = (bf16[128,768]{1,0:T(8,128)(2,1)S(1)}, bf16[128,768]{1,0:T(8,128)(2,1)S(1)}, u32[]{:S(2)}, u32[]{:S(2)}) collective-permute-start(bf16[128,768]{1,0:T(8,128)(2,1)S(1)} %get-tuple-element.40.refs_4_.refs_3_), channel_id=1, source_target_pairs={{0,4},{4,0},{8,12},{12,8},{16,20},{20,16},{24,28},{28,24},{1,5},{5... | collective-permute-start | bytes 589832 | tf_op jit(solution)/shard_map/ppermute | solution.py:312
  38.3 7.3 %collective-permute-start.4 = (bf16[64,768]{1,0:T(8,128)(2,1)S(1)}, bf16[64,768]{1,0:T(8,128)(2,1)S(1)}, u32[]{:S(2)}, u32[]{:S(2)}) collective-permute-start(bf16[64,768]{1,0:T(8,128)(2,1)S(1)} %get-tuple-element.36), channel_id=1, source_target_pairs={{0,24},{4,28},{8,16},{12,20},{16,8},{20,12},{24,0},{28,4},{1,25},{... | collective-permute-start | bytes 294920 | tf_op jit(solution)/shard_map/ppermute | solution.py:312
  40.7 6.1 %collective-permute-start.5 = (bf16[64,768]{1,0:T(8,128)(2,1)S(1)}, bf16[64,768]{1,0:T(8,128)(2,1)S(1)}, u32[]{:S(2)}, u32[]{:S(2)}) collective-permute-start(bf16[64,768]{1,0:T(8,128)(2,1)S(1)} %get-tuple-element.37), channel_id=1, source_target_pairs={{0,28},{4,24},{8,20},{12,16},{16,12},{20,8},{24,4},{28,0},{1,29},{... | collective-permute-start | bytes 294920 | tf_op jit(solution)/shard_map/ppermute | solution.py:312
  40.7 9.6 %collective-permute-start.6 = (bf16[128,768]{1,0:T(8,128)(2,1)S(1)}, bf16[128,768]{1,0:T(8,128)(2,1)S(1)}, u32[]{:S(2)}, u32[]{:S(2)}) collective-permute-start(bf16[128,768]{1,0:T(8,128)(2,1)S(1)} %get-tuple-element.38.refs_4_), channel_id=1, source_target_pairs={{0,8},{4,12},{8,0},{12,4},{16,24},{20,28},{24,16},{28,20},{1,9},{5... | collective-permute-start | bytes 589832 | tf_op jit(solution)/shard_map/ppermute | solution.py:312
  42.1 8.8 %collective-permute-start.7 = (bf16[128,768]{1,0:T(8,128)(2,1)S(1)}, bf16[128,768]{1,0:T(8,128)(2,1)S(1)}, u32[]{:S(2)}, u32[]{:S(2)}) collective-permute-start(bf16[128,768]{1,0:T(8,128)(2,1)S(1)} %get-tuple-element.39.refs_6_), channel_id=1, source_target_pairs={{0,16},{4,20},{8,24},{12,28},{16,0},{20,4},{24,8},{28,12},{1,17},{... | collective-permute-start | bytes 589832 | tf_op jit(solution)/shard_map/ppermute | solution.py:312
  43.6 5.1 %copy-start.3 = (bf16[128,768]{1,0:T(8,128)(2,1)S(1)}, bf16[128,768]{1,0:T(8,128)(2,1)}, u32[]{:S(2)}) copy-start(bf16[128,768]{1,0:T(8,128)(2,1)} %refs_1_.4) | copy-start | bytes 589828
  43.6 5.1 %copy-start.5 = (bf16[128,768]{1,0:T(8,128)(2,1)S(1)}, bf16[128,768]{1,0:T(8,128)(2,1)}, u32[]{:S(2)}) copy-start(bf16[128,768]{1,0:T(8,128)(2,1)} %refs_2_.3) | copy-start | bytes 589828
  46.8 6.9 %collective-permute-start.13 = (bf16[128,768]{1,0:T(8,128)(2,1)S(1)}, bf16[128,768]{1,0:T(8,128)(2,1)S(1)}, u32[]{:S(2)}, u32[]{:S(2)}) collective-permute-start(bf16[128,768]{1,0:T(8,128)(2,1)S(1)} %bitcast.11), channel_id=1, source_target_pairs={{0,1},{1,0},{2,3},{3,2},{4,5},{5,4},{6,7},{7,6},{8,9},{9,8},{10,11... | collective-permute-start | bytes 589832 | tf_op jit(solution)/shard_map/ppermute | solution.py:393
  47.4 7.1 %collective-permute-start.14 = (bf16[128,768]{1,0:T(8,128)(2,1)S(1)}, bf16[128,768]{1,0:T(8,128)(2,1)S(1)}, u32[]{:S(2)}, u32[]{:S(2)}) collective-permute-start(bf16[128,768]{1,0:T(8,128)(2,1)S(1)} %get-tuple-element.46.refs_5_), channel_id=1, source_target_pairs={{0,12},{4,8},{8,4},{12,0},{16,28},{20,24},{24,20},{28,16},{1,13},{... | collective-permute-start | bytes 589832 | tf_op jit(solution)/shard_map/ppermute | solution.py:312
  48.3 6.9 %collective-permute-start.15 = (bf16[128,768]{1,0:T(8,128)(2,1)S(1)}, bf16[128,768]{1,0:T(8,128)(2,1)S(1)}, u32[]{:S(2)}, u32[]{:S(2)}) collective-permute-start(bf16[128,768]{1,0:T(8,128)(2,1)S(1)} %get-tuple-element.47.refs_7_), channel_id=1, source_target_pairs={{0,20},{4,16},{8,28},{12,24},{16,4},{20,0},{24,12},{28,8},{1,21},{... | collective-permute-start | bytes 589832 | tf_op jit(solution)/shard_map/ppermute | solution.py:312
  50.1 5.1 %copy-start.7 = (bf16[128,768]{1,0:T(8,128)(2,1)S(1)}, bf16[128,768]{1,0:T(8,128)(2,1)}, u32[]{:S(2)}) copy-start(bf16[128,768]{1,0:T(8,128)(2,1)} %get-tuple-element.25.refs_10_) | copy-start | bytes 589828

commit v7 on v6

--- a/solution.py
+++ b/solution.py
@@ -231,10 +231,8 @@
         ).astype(jnp.bfloat16)
 
 
-def joined(info, names, refs):
-    refs = list(refs)
-    chip_values, mate_values = refs[-5:-1], refs[-1]
-    left, right = [], []
+def value_parts(info, names, chip_values, mate_values):
+    parts = []
 
     def rows_of(offset, swapped=None):
         values = mate_values.at[offset // 2] if offset % 2 else chip_values[offset // 2]
@@ -245,30 +243,36 @@
         return values[pl.ds(pl.multiple_of(side * rows, rows), rows), :]
 
     for name in names:
-        left.append(refs.pop(0)[...])
         if name == SWAPPED:
-            right.extend(rows_of(offset, 1) for offset in HALVED)
+            parts.extend(rows_of(offset, 1) for offset in HALVED)
         else:
-            right.append(rows_of(name, 0 if name in HALVED else None))
-    return jnp.concatenate(left, axis=0), jnp.concatenate(right, axis=0)
-
-
-def gradient_first_kernel(names, info, *refs):
-    left, right = joined(info, names, refs[:-1])
-    refs[-1][...] = lax.dot_general(
+            parts.append(rows_of(name, 0 if name in HALVED else None))
+    return parts
+
+
+def gradient_first_kernel(info, *refs):
+    normed, chip_values, mate_values = refs[:-7], refs[-7:-3], refs[-3]
+    sum_ref, right_ref = refs[-2:]
+    row = 0
+    for part in value_parts(info, LAST, chip_values, mate_values):
+        right_ref[row:row + part.shape[0], :] = part
+        row += part.shape[0]
+    left = jnp.concatenate([ref[...] for ref in normed], axis=0)
+    right = jnp.concatenate(value_parts(info, FIRST, chip_values, mate_values), axis=0)
+    sum_ref[...] = lax.dot_general(
         left, right, (((0,), (0,)), ((), ())), preferred_element_type=jnp.float32
     )
 
 
-def gradient_last_kernel(names, info, before, *refs):
-    left, right = joined(info, names, refs[:-3])
-    out_ref, ready, done = refs[-3:]
+def gradient_last_kernel(before, right, *refs):
+    normed, (out_ref, ready, done) = refs[:-3], refs[-3:]
+    left = jnp.concatenate([ref[...] for ref in normed], axis=0)
     blocks, rows, _ = ready.shape
     copies = []
     for block in range(blocks):
         part = slice(block * rows, (block + 1) * rows)
         ready[block] = before[part, :] + lax.dot_general(
-            left[:, part], right, (((0,), (0,)), ((), ())), preferred_element_type=jnp.float32
+            left[:, part], right[...], (((0,), (0,)), ((), ())), preferred_element_type=jnp.float32
         )
         copies.append(
             pltpu.make_async_copy(ready.at[block], out_ref.at[pl.ds(block * rows, rows)], done.at[block])
@@ -394,21 +398,18 @@
         else:
             moved[name] = across(part, name)
 
-    def arrived(names):
-        return [moved[name] for name in names] + chip_values + [mate_values]
-
+    first, last = [moved[name] for name in FIRST], [moved[name] for name in LAST]
     grad = shape((half, width), jnp.float32)
-    parts = arrived(FIRST)
-    partial = call(
-        functools.partial(gradient_first_kernel, FIRST), "gradient_first", grad, [SMEM] + [WHOLE] * len(parts), WHOLE
-    )(info, *parts)
-    parts = arrived(LAST)
+    partial, last_values = call(
+        gradient_first_kernel, "gradient_first", (grad, shape((rows * len(LAST), width))),
+        [SMEM] + [WHOLE] * (len(first) + 5), (WHOLE, WHOLE),
+    )(info, *first, *chip_values, mate_values)
     blocks = half // 256
     weight_grad = call(
-        functools.partial(gradient_last_kernel, LAST), "gradient_last", grad, [SMEM] + [WHOLE] * (len(parts) + 1), ANY,
+        gradient_last_kernel, "gradient_last", grad, [WHOLE] * (len(last) + 2), ANY,
         (pltpu.VMEM((blocks, 256, width), jnp.float32), pltpu.SemaphoreType.DMA((blocks,))),
         after=(query_grad,),
-    )(info, partial, *parts)
+    )(partial, last_values, *last)
     return weight_grad, query_grad, key_grad
 
 

time: 58 us -> 57.5 us (level)
  no operation moved by 1% of the time
where the time goes in v7:
time: 57.5 us; the launch traced here: 57 us
  starting transfers between devices  22.8 us (40%)
  waiting for transfers between devices  14.6 us (25%)
  Pallas kernels  11.8 us (21%)
  local copies, waits for them, and re-layouts  7.09 us (12%)
  between operations  0.78 us (1%)
    pallas_call x10, Pallas kernels, call(): return lambda *args: made(*args, *after)  11.8 us
    ppermute x11, starting transfers between devices, across(): return lax.ppermute(rows, 'dp', [(i, i ^ distance) for i in range(8)])  10.8 us
    unnamed x16, local copies, waits for them, and re-layouts  5.56 us
    ppermute x1, starting transfers between devices, fast_body(): two = lax.ppermute(patches, 'mp', [(0, 2), (2, 0), (1, 3), (3, 1)])  4.1 us
    all_to_all x1, waiting for transfers between devices, fast_body(): lax.all_to_all(head_cotangent.reshape(8, slots // 8, width), 'dp', split_...  3.93 us
    all_to_all x1, starting transfers between devices, fast_body(): lax.all_to_all(head_cotangent.reshape(8, slots // 8, width), 'dp', split_...  3.72 us
    ppermute x11, waiting for transfers between devices, across(): return lax.ppermute(rows, 'dp', [(i, i ^ distance) for i in range(8)])  3.5 us
    ppermute x1, waiting for transfers between devices, fast_body(): two = lax.ppermute(patches, 'mp', [(0, 2), (2, 0), (1, 3), (3, 1)])  3.22 us
  transfers between devices with their start and end apart: 17, of which 10 were waited for; matrix products, arithmetic and copies ran while one was open for 3% of the time, Pallas kernels for 17%

profile of v7, /device:TPU:0, one launch (start us, length us, event | category | flops | bytes accessed | tf_op | source)
XLA Modules:
  0.0 57.0 jit_solution(5925665311594701102)
XLA Ops:
  0.6 0.0 copy-start.6
  0.6 4.1 %collective-permute-start = (bf16[128,1536]{1,0:T(8,128)(2,1)}, bf16[128,1536]{1,0:T(8,128)(2,1)S(1)}, u32[]{:S(2)}, u32[]{:S(2)}) collective-permute-start(bf16[128,1536]{1,0:T(8,128)(2,1)} %refs_1_.2), channel_id=1, source_target_pairs={{0,2},{2,0},{1,3},{3,1},{4,6},{6,4},{5,7},{7,5},{8,10},{10,8},{9,1... | collective-permute-start | bytes 1179656 | tf_op jit(solution)/shard_map/ppermute | solution.py:347
  4.7 1.6 %collective-permute-start.1 = (bf16[128,1536]{1,0:T(8,128)(2,1)}, bf16[128,1536]{1,0:T(8,128)(2,1)S(1)}, u32[]{:S(2)}, u32[]{:S(2)}) collective-permute-start(bf16[128,1536]{1,0:T(8,128)(2,1)} %refs_1_.2), channel_id=1, source_target_pairs={{0,1},{1,0},{2,3},{3,2},{4,5},{5,4},{6,7},{7,6},{8,9},{9,8},{10,11... | collective-permute-start | bytes 1179656 | tf_op jit(solution)/shard_map/ppermute | solution.py:348
  6.3 3.7 %all-to-all-start = ((bf16[8,32,768]{2,1,0:T(8,128)(2,1)}), bf16[8,32,768]{2,1,0:T(8,128)(2,1)S(1)}, u32[]{:S(2)}, u32[]{:S(2)}) async-start(bf16[8,32,768]{2,1,0:T(8,128)(2,1)} %bitcast.12), calls=%async_computation | async-start | bytes 786432 | tf_op jit(solution)/shard_map/all_to_all | solution.py:344
  10.0 0.7 %reshape.20.refs_1_ = f32[8,768]{1,0:T(8,128)S(1)} reshape(f32[6144]{0:T(1024)} %param.9) | data formatting | bytes 49152 | tf_op jit(solution)/shard_map/reshape | solution.py:353
  10.8 0.7 %dynamic-slice_bitcast_fusion = (s32[8]{0:T(128)S(1)}, s32[8]{0:T(128)S(1)}) fusion(s32[8,8]{1,0:T(8,128)} %param.15, s32[]{:T(128)S(6)} %select_n.18, s32[8,8]{1,0:T(8,128)} %param.14), kind=kLoop, calls=%fused_computation | loop fusion | bytes 132 | tf_op jit(solution)/shard_map/jit(dynamic_index_in_dim)/squeeze | solution.py:340
  11.5 0.1 concatenate.3.refs_0_
  11.6 0.0 copy-start.2
  11.6 0.9 %copy-done.2 = bf16[128,768]{1,0:T(8,128)(2,1)S(1)} copy-done((bf16[128,768]{1,0:T(8,128)(2,1)S(1)}, bf16[128,768]{1,0:T(8,128)(2,1)}, u32[]{:S(2)}) %copy-start.2) | copy-done | bytes 196632
  12.5 0.0 copy-start.4
  12.5 0.9 %copy-done.4 = bf16[128,768]{1,0:T(8,128)(2,1)S(1)} copy-done((bf16[128,768]{1,0:T(8,128)(2,1)S(1)}, bf16[128,768]{1,0:T(8,128)(2,1)}, u32[]{:S(2)}) %copy-start.4) | copy-done | bytes 196632
  13.4 1.0 %attention_weights.1 = (f32[6,128,128]{2,1,0:T(8,128)S(1)}, f32[8,768]{1,0:T(8,128)S(1)}) custom-call(s32[24]{0:T(128)S(1)} %concatenate.3.refs_0_, f32[8,768]{1,0:T(8,128)S(1)} %reshape.20.refs_1_, bf16[128,768]{1,0:T(8,128)(2,1)S(1)} %copy-done.2, bf16[128,768]{1,0:T(8,128)(2,1)S(1)} %copy-done.4), custom_call_target="tpu_custom_call" | custom-call | flops 1 | bytes 1 | tf_op jit(solution)/shard_map/attention_weights/pallas_call | solution.py:312
  14.5 3.9 %all-to-all-done = bf16[8,32,768]{2,1,0:T(8,128)(2,1)S(1)} async-done(((bf16[8,32,768]{2,1,0:T(8,128)(2,1)}), bf16[8,32,768]{2,1,0:T(8,128)(2,1)S(1)}, u32[]{:S(2)}, u32[]{:S(2)}) %all-to-all-start) | async-done | bytes 393248 | tf_op jit(solution)/shard_map/all_to_all | solution.py:344
  18.4 1.0 %value_rows.1 = (bf16[128,768]{1,0:T(8,128)(2,1)S(1)}, bf16[128,768]{1,0:T(8,128)(2,1)S(1)}) custom-call(s32[24]{0:T(128)S(1)} %concatenate.3.refs_0_, bf16[256,768]{1,0:T(8,128)(2,1)S(1)} %bitcast.10, f32[6,128,128]{2,1,0:T(8,128)S(1)} %get-tuple-element.29.refs_2_.refs_4_), custom_call_target="tpu_custom_call" | custom-call | flops 1 | bytes 1 | tf_op jit(solution)/shard_map/value_rows/pallas_call | solution.py:312
  19.4 3.2 %collective-permute-done.refs_2_ = bf16[128,1536]{1,0:T(8,128)(2,1)S(1)} collective-permute-done((bf16[128,1536]{1,0:T(8,128)(2,1)}, bf16[128,1536]{1,0:T(8,128)(2,1)S(1)}, u32[]{:S(2)}, u32[]{:S(2)}) %collective-permute-start) | collective-permute-done | bytes 393248 | tf_op jit(solution)/shard_map/ppermute | solution.py:347
  22.6 0.2 collective-permute-done.1.refs_3_
  22.8 0.7 %collective-permute-start.2 = (bf16[128,1536]{1,0:T(8,128)(2,1)}, bf16[128,1536]{1,0:T(8,128)(2,1)S(1)}, u32[]{:S(2)}, u32[]{:S(2)}) collective-permute-start(bf16[128,1536]{1,0:T(8,128)(2,1)} %refs_1_.2), channel_id=1, source_target_pairs={{1,2},{2,1},{5,6},{6,5},{9,10},{10,9},{13,14},{14,13},{17,18},{18,... | collective-permute-start | bytes 1179656 | tf_op jit(solution)/shard_map/ppermute | solution.py:359
  23.5 1.3 %collective-permute-start.3 = (bf16[128,1536]{1,0:T(8,128)(2,1)S(1)}, bf16[128,1536]{1,0:T(8,128)(2,1)S(1)}, u32[]{:S(2)}, u32[]{:S(2)}) collective-permute-start(bf16[128,1536]{1,0:T(8,128)(2,1)S(1)} %collective-permute-done.refs_2_), channel_id=1, source_target_pairs={{2,3},{1,0},{6,7},{5,4},{10,11},{9,8},{14,15},{13,12},{18,19},{17,... | collective-permute-start | bytes 1179656 | tf_op jit(solution)/shard_map/ppermute | solution.py:360
  24.8 2.6 %collective-permute-start.11 = (bf16[128,768]{1,0:T(8,128)(2,1)S(1)}, bf16[128,768]{1,0:T(8,128)(2,1)S(1)}, u32[]{:S(2)}, u32[]{:S(2)}) collective-permute-start(bf16[128,768]{1,0:T(8,128)(2,1)S(1)} %get-tuple-element.30.refs_0_.refs_7_), channel_id=1, source_target_pairs={{0,24},{4,28},{8,16},{12,20},{16,8},{20,12},{24,0},{28,4},{1,25},{... | collective-permute-start | bytes 589832 | tf_op jit(solution)/shard_map/ppermute | solution.py:316
  27.3 0.5 collective-permute-start.10
  27.8 0.5 collective-permute-start.9
  28.3 0.0 copy-done.6
  28.3 0.0 copy-start
  28.3 3.7 %copy-done = bf16[6144,768]{1,0:T(8,128)(2,1)S(1)} copy-done((bf16[6144,768]{1,0:T(8,128)(2,1)S(1)}, bf16[6144,768]{1,0:T(8,128)(2,1)}, u32[]{:S(2)}) %copy-start) | copy-done | bytes 9437208
  32.0 0.0 copy-start.1
  32.0 1.2 %partial_stats.1 = (f32[128,128]{1,0:T(8,128)S(1)}, bf16[4,128,1536]{2,1,0:T(8,128)(2,1)S(1)}) custom-call(s32[24]{0:T(128)S(1)} %concatenate.3.refs_0_, bf16[128,1536]{1,0:T(8,128)(2,1)S(1)} %copy-done.6, bf16[128,1536]{1,0:T(8,128)(2,1)S(1)} %collective-permute-done.refs_2_, bf16[128,1536]{1,0:T(8,128)(2,1)S(1)} %collective-permute-done.1.refs_3_, ...), custom_call_target="tpu_custom_call" | custom-call | flops 1 | bytes 1 | tf_op jit(solution)/shard_map/partial_stats/pallas_call | solution.py:312
  33.2 0.0 collective-permute-done.2.refs_4_
  33.2 2.7 %collective-permute-done.3.refs_5_ = bf16[128,1536]{1,0:T(8,128)(2,1)S(1)} collective-permute-done((bf16[128,1536]{1,0:T(8,128)(2,1)S(1)}, bf16[128,1536]{1,0:T(8,128)(2,1)S(1)}, u32[]{:S(2)}, u32[]{:S(2)}) %collective-permute-start.3) | collective-permute-done | bytes 393248 | tf_op jit(solution)/shard_map/ppermute | solution.py:360
  35.9 1.7 %norm_rows.1 = (bf16[128,768]{1,0:T(8,128)(2,1)S(1)}, bf16[128,768]{1,0:T(8,128)(2,1)S(1)}, bf16[128,768]{1,0:T(8,128)(2,1)S(1)}, bf16[128,768]{1,0:T(8,128)(2,1...) custom-call(s32[24]{0:T(128)S(1)} %concatenate.3.refs_0_, ...), custom_call_target="tpu_custom_call" | custom-call | flops 1 | bytes 1 | tf_op jit(solution)/shard_map/norm_rows/pallas_call | solution.py:312
  37.6 0.0 collective-permute-done.11.refs_3_.refs_10_
  37.6 0.0 collective-permute-done.10.refs_2_.refs_9_
  37.6 0.0 collective-permute-done.9.refs_1_.refs_8_
  37.6 0.1 pack_values.1
  37.7 0.1 collective-permute-start.12
  37.8 0.5 collective-permute-start.8
  38.3 2.4 %collective-permute-start.4 = (bf16[64,768]{1,0:T(8,128)(2,1)S(1)}, bf16[64,768]{1,0:T(8,128)(2,1)S(1)}, u32[]{:S(2)}, u32[]{:S(2)}) collective-permute-start(bf16[64,768]{1,0:T(8,128)(2,1)S(1)} %get-tuple-element.38), channel_id=1, source_target_pairs={{0,24},{4,28},{8,16},{12,20},{16,8},{20,12},{24,0},{28,4},{1,25},{... | collective-permute-start | bytes 294920 | tf_op jit(solution)/shard_map/ppermute | solution.py:316
  40.7 0.0 collective-permute-start.5
  40.7 1.4 %collective-permute-start.6 = (bf16[128,768]{1,0:T(8,128)(2,1)S(1)}, bf16[128,768]{1,0:T(8,128)(2,1)S(1)}, u32[]{:S(2)}, u32[]{:S(2)}) collective-permute-start(bf16[128,768]{1,0:T(8,128)(2,1)S(1)} %get-tuple-element.40.refs_4_), channel_id=1, source_target_pairs={{0,8},{4,12},{8,0},{12,4},{16,24},{20,28},{24,16},{28,20},{1,9},{5... | collective-permute-start | bytes 589832 | tf_op jit(solution)/shard_map/ppermute | solution.py:316
  42.1 0.0 collective-permute-done.8.refs_6_.refs_11_
  42.1 1.5 %collective-permute-start.7 = (bf16[128,768]{1,0:T(8,128)(2,1)S(1)}, bf16[128,768]{1,0:T(8,128)(2,1)S(1)}, u32[]{:S(2)}, u32[]{:S(2)}) collective-permute-start(bf16[128,768]{1,0:T(8,128)(2,1)S(1)} %get-tuple-element.41.refs_6_), channel_id=1, source_target_pairs={{0,16},{4,20},{8,24},{12,28},{16,0},{20,4},{24,8},{28,12},{1,17},{... | collective-permute-start | bytes 589832 | tf_op jit(solution)/shard_map/ppermute | solution.py:316
  43.6 0.0 collective-permute-done.12.refs_11_.refs_10_
  43.6 0.0 copy-done.1
  43.6 0.0 copy-start.3
  43.6 0.0 copy-start.5
  43.6 2.0 %project_values.1.refs_2_.refs_0_ = bf16[128,768]{1,0:T(8,128)(2,1)S(1)} custom-call(s32[24]{0:T(128)S(1)} %concatenate.3.refs_0_, bf16[6144,768]{1,0:T(8,128)(2,1)S(1)} %copy-done.1, bf16[128,768]{1,0:T(8,128)(2,1)S(1)} %get-tuple-element.37.refs_1_.refs_2_, bf16[128,768]{1,0:T(8,128)(2,1)S(1)} %get-tuple-element.42.refs_4_.refs_3_, ...), custom_call_target="tpu_custom_call" | custom-call | flops 1 | bytes 1 | tf_op jit(solution)/shard_map/project_values/pallas_call | solution.py:312
  45.6 0.0 collective-permute-done.4.refs_2_.refs_0_
  45.6 1.2 %collective-permute-done.5.refs_3_.refs_1_ = bf16[64,768]{1,0:T(8,128)(2,1)S(1)} collective-permute-done((bf16[64,768]{1,0:T(8,128)(2,1)S(1)}, bf16[64,768]{1,0:T(8,128)(2,1)S(1)}, u32[]{:S(2)}, u32[]{:S(2)}) %collective-permute-start.5) | collective-permute-done | bytes 98336 | tf_op jit(solution)/shard_map/ppermute | solution.py:316
  46.8 0.6 %collective-permute-start.13 = (bf16[128,768]{1,0:T(8,128)(2,1)S(1)}, bf16[128,768]{1,0:T(8,128)(2,1)S(1)}, u32[]{:S(2)}, u32[]{:S(2)}) collective-permute-start(bf16[128,768]{1,0:T(8,128)(2,1)S(1)} %bitcast.11), channel_id=1, source_target_pairs={{0,1},{1,0},{2,3},{3,2},{4,5},{5,4},{6,7},{7,6},{8,9},{9,8},{10,11... | collective-permute-start | bytes 589832 | tf_op jit(solution)/shard_map/ppermute | solution.py:397
  47.4 0.9 %collective-permute-start.14 = (bf16[128,768]{1,0:T(8,128)(2,1)S(1)}, bf16[128,768]{1,0:T(8,128)(2,1)S(1)}, u32[]{:S(2)}, u32[]{:S(2)}) collective-permute-start(bf16[128,768]{1,0:T(8,128)(2,1)S(1)} %get-tuple-element.50.refs_5_), channel_id=1, source_target_pairs={{0,12},{4,8},{8,4},{12,0},{16,28},{20,24},{24,20},{28,16},{1,13},{... | collective-permute-start | bytes 589832 | tf_op jit(solution)/shard_map/ppermute | solution.py:316
  48.3 0.4 collective-permute-start.15
  48.7 0.0 copy-done.3
  48.7 0.0 copy-done.5
  48.8 1.4 %attention_backward.1 = (bf16[128,768]{1,0:T(8,128)(2,1)}, bf16[128,768]{1,0:T(8,128)(2,1)}) custom-call(bf16[128,768]{1,0:T(8,128)(2,1)S(1)} %project_values.1.refs_2_.refs_0_, bf16[128,768]{1,0:T(8,128)(2,1)S(1)} %copy-done.3, bf16[128,768]{1,0:T(8,128)(2,1)S(1)} %copy-done.5, bf16[128,768]{1,0:T(8,128)(2,1)S(1)} %get-tuple-element.52.refs_3_, ...), custom_call_target="tpu_custom_call" | custom-call | flops 1 | bytes 1 | tf_op jit(solution)/shard_map/attention_backward/pallas_call | solution.py:312
  50.1 0.0 copy-start.7
  50.1 0.2 collective-permute-done.6.refs_4_
  50.3 0.6 %collective-permute-done.7.refs_5_ = bf16[128,768]{1,0:T(8,128)(2,1)S(1)} collective-permute-done((bf16[128,768]{1,0:T(8,128)(2,1)S(1)}, bf16[128,768]{1,0:T(8,128)(2,1)S(1)}, u32[]{:S(2)}, u32[]{:S(2)}) %collective-permute-start.7) | collective-permute-done | bytes 196640 | tf_op jit(solution)/shard_map/ppermute | solution.py:316
  50.9 1.7 %gradient_first.1 = (f32[768,768]{1,0:T(8,128)S(1)}, bf16[384,768]{1,0:T(8,128)(2,1)S(1)}) custom-call(s32[24]{0:T(128)S(1)} %concatenate.3.refs_0_, bf16[128,768]{1,0:T(8,128)(2,1)S(1)} %get-tuple-element.37.refs_1_.refs_2_, bf16[64,768]{1,0:T(8,128)(2,1)S(1)} %collective-permute-done.4.refs_2_.refs_0_, ...), custom_call_target="tpu_custom_call" | custom-call | flops 1 | bytes 1 | tf_op jit(solution)/shard_map/gradient_first/pallas_call | solution.py:312
  52.6 1.1 %collective-permute-done.13.refs_2_ = bf16[128,768]{1,0:T(8,128)(2,1)S(1)} collective-permute-done((bf16[128,768]{1,0:T(8,128)(2,1)S(1)}, bf16[128,768]{1,0:T(8,128)(2,1)S(1)}, u32[]{:S(2)}, u32[]{:S(2)}) %collective-permute-start.13) | collective-permute-done | bytes 196640 | tf_op jit(solution)/shard_map/ppermute | solution.py:397
  53.7 0.9 %collective-permute-done.14.refs_3_ = bf16[128,768]{1,0:T(8,128)(2,1)S(1)} collective-permute-done((bf16[128,768]{1,0:T(8,128)(2,1)S(1)}, bf16[128,768]{1,0:T(8,128)(2,1)S(1)}, u32[]{:S(2)}, u32[]{:S(2)}) %collective-permute-start.14) | collective-permute-done | bytes 196640 | tf_op jit(solution)/shard_map/ppermute | solution.py:316
  54.5 0.7 %collective-permute-done.15.refs_4_ = bf16[128,768]{1,0:T(8,128)(2,1)S(1)} collective-permute-done((bf16[128,768]{1,0:T(8,128)(2,1)S(1)}, bf16[128,768]{1,0:T(8,128)(2,1)S(1)}, u32[]{:S(2)}, u32[]{:S(2)}) %collective-permute-start.15) | collective-permute-done | bytes 196640 | tf_op jit(solution)/shard_map/ppermute | solution.py:316
  55.2 0.0 copy-done.7
  55.2 1.8 %gradient_last.1 = f32[768,768]{1,0:T(8,128)} custom-call(f32[768,768]{1,0:T(8,128)S(1)} %get-tuple-element.43.refs_0_, bf16[384,768]{1,0:T(8,128)(2,1)S(1)} %get-tuple-element.44.refs_1_, bf16[128,768]{1,0:T(8,128)(2,1)S(1)} %collective-permute-done.13.refs_2_, bf16[128,768]{1,0:T(8,128)(2,1)S(1)} %collective-permute-done.14.refs_3_, ...), custom_call_target="tpu_custom_call" | custom-call | flops 1 | bytes 1 | tf_op jit(solution)/shard_map/gradient_last/pallas_call | solution.py:312
  (2 shorter events, 0.0 us)
Async XLA Ops:
  0.6 27.7 %copy-start.6 = (bf16[128,1536]{1,0:T(8,128)(2,1)S(1)}, bf16[128,1536]{1,0:T(8,128)(2,1)}, u32[]{:S(2)}) copy-start(bf16[128,1536]{1,0:T(8,128)(2,1)} %refs_1_.2) | copy-start | bytes 1179652
  0.6 22.0 %collective-permute-start = (bf16[128,1536]{1,0:T(8,128)(2,1)}, bf16[128,1536]{1,0:T(8,128)(2,1)S(1)}, u32[]{:S(2)}, u32[]{:S(2)}) collective-permute-start(bf16[128,1536]{1,0:T(8,128)(2,1)} %refs_1_.2), channel_id=1, source_target_pairs={{0,2},{2,0},{1,3},{3,1},{4,6},{6,4},{5,7},{7,5},{8,10},{10,8},{9,1... | collective-permute-start | bytes 1179656 | tf_op jit(solution)/shard_map/ppermute | solution.py:347
  4.7 18.0 %collective-permute-start.1 = (bf16[128,1536]{1,0:T(8,128)(2,1)}, bf16[128,1536]{1,0:T(8,128)(2,1)S(1)}, u32[]{:S(2)}, u32[]{:S(2)}) collective-permute-start(bf16[128,1536]{1,0:T(8,128)(2,1)} %refs_1_.2), channel_id=1, source_target_pairs={{0,1},{1,0},{2,3},{3,2},{4,5},{5,4},{6,7},{7,6},{8,9},{9,8},{10,11... | collective-permute-start | bytes 1179656 | tf_op jit(solution)/shard_map/ppermute | solution.py:348
  6.3 12.1 %all-to-all-start = ((bf16[8,32,768]{2,1,0:T(8,128)(2,1)}), bf16[8,32,768]{2,1,0:T(8,128)(2,1)S(1)}, u32[]{:S(2)}, u32[]{:S(2)}) async-start(bf16[8,32,768]{2,1,0:T(8,128)(2,1)} %bitcast.12), calls=%async_computation | async-start | bytes 786432 | tf_op jit(solution)/shard_map/all_to_all | solution.py:344
  11.6 0.9 %copy-start.2 = (bf16[128,768]{1,0:T(8,128)(2,1)S(1)}, bf16[128,768]{1,0:T(8,128)(2,1)}, u32[]{:S(2)}) copy-start(bf16[128,768]{1,0:T(8,128)(2,1)} %refs_1_.4) | copy-start | bytes 589828
  12.5 0.9 %copy-start.4 = (bf16[128,768]{1,0:T(8,128)(2,1)S(1)}, bf16[128,768]{1,0:T(8,128)(2,1)}, u32[]{:S(2)}) copy-start(bf16[128,768]{1,0:T(8,128)(2,1)} %refs_2_.3) | copy-start | bytes 589828
  22.8 10.4 %collective-permute-start.2 = (bf16[128,1536]{1,0:T(8,128)(2,1)}, bf16[128,1536]{1,0:T(8,128)(2,1)S(1)}, u32[]{:S(2)}, u32[]{:S(2)}) collective-permute-start(bf16[128,1536]{1,0:T(8,128)(2,1)} %refs_1_.2), channel_id=1, source_target_pairs={{1,2},{2,1},{5,6},{6,5},{9,10},{10,9},{13,14},{14,13},{17,18},{18,... | collective-permute-start | bytes 1179656 | tf_op jit(solution)/shard_map/ppermute | solution.py:359
  23.5 12.4 %collective-permute-start.3 = (bf16[128,1536]{1,0:T(8,128)(2,1)S(1)}, bf16[128,1536]{1,0:T(8,128)(2,1)S(1)}, u32[]{:S(2)}, u32[]{:S(2)}) collective-permute-start(bf16[128,1536]{1,0:T(8,128)(2,1)S(1)} %collective-permute-done.refs_2_), channel_id=1, source_target_pairs={{2,3},{1,0},{6,7},{5,4},{10,11},{9,8},{14,15},{13,12},{18,19},{17,... | collective-permute-start | bytes 1179656 | tf_op jit(solution)/shard_map/ppermute | solution.py:360
  24.8 12.8 %collective-permute-start.11 = (bf16[128,768]{1,0:T(8,128)(2,1)S(1)}, bf16[128,768]{1,0:T(8,128)(2,1)S(1)}, u32[]{:S(2)}, u32[]{:S(2)}) collective-permute-start(bf16[128,768]{1,0:T(8,128)(2,1)S(1)} %get-tuple-element.30.refs_0_.refs_7_), channel_id=1, source_target_pairs={{0,24},{4,28},{8,16},{12,20},{16,8},{20,12},{24,0},{28,4},{1,25},{... | collective-permute-start | bytes 589832 | tf_op jit(solution)/shard_map/ppermute | solution.py:316
  27.3 10.3 %collective-permute-start.10 = (bf16[128,768]{1,0:T(8,128)(2,1)S(1)}, bf16[128,768]{1,0:T(8,128)(2,1)S(1)}, u32[]{:S(2)}, u32[]{:S(2)}) collective-permute-start(bf16[128,768]{1,0:T(8,128)(2,1)S(1)} %get-tuple-element.30.refs_0_.refs_7_), channel_id=1, source_target_pairs={{0,16},{4,20},{8,24},{12,28},{16,0},{20,4},{24,8},{28,12},{1,17},{... | collective-permute-start | bytes 589832 | tf_op jit(solution)/shard_map/ppermute | solution.py:316
  27.8 9.8 %collective-permute-start.9 = (bf16[128,768]{1,0:T(8,128)(2,1)S(1)}, bf16[128,768]{1,0:T(8,128)(2,1)S(1)}, u32[]{:S(2)}, u32[]{:S(2)}) collective-permute-start(bf16[128,768]{1,0:T(8,128)(2,1)S(1)} %get-tuple-element.30.refs_0_.refs_7_), channel_id=1, source_target_pairs={{0,8},{4,12},{8,0},{12,4},{16,24},{20,28},{24,16},{28,20},{1,9},{5... | collective-permute-start | bytes 589832 | tf_op jit(solution)/shard_map/ppermute | solution.py:316
  28.3 3.7 %copy-start = (bf16[6144,768]{1,0:T(8,128)(2,1)S(1)}, bf16[6144,768]{1,0:T(8,128)(2,1)}, u32[]{:S(2)}) copy-start(bf16[6144,768]{1,0:T(8,128)(2,1)} %refs_1_.3) | copy-start | bytes 28311556
  32.0 11.6 %copy-start.1 = (bf16[6144,768]{1,0:T(8,128)(2,1)S(1)}, bf16[6144,768]{1,0:T(8,128)(2,1)}, u32[]{:S(2)}) copy-start(bf16[6144,768]{1,0:T(8,128)(2,1)} %refs_1_.3) | copy-start | bytes 28311556
  37.7 5.9 %collective-permute-start.12 = (bf16[4,128,768]{2,1,0:T(8,128)(2,1)S(1)}, bf16[4,128,768]{2,1,0:T(8,128)(2,1)S(1)}, u32[]{:S(2)}, u32[]{:S(2)}) collective-permute-start(bf16[4,128,768]{2,1,0:T(8,128)(2,1)S(1)} %pack_values.1), channel_id=1, source_target_pairs={{0,4},{4,0},{8,12},{12,8},{16,20},{20,16},{24,28},{28,24},{1,5},{5... | collective-permute-start | bytes 2359304 | tf_op jit(solution)/shard_map/ppermute | solution.py:316
  37.8 4.3 %collective-permute-start.8 = (bf16[128,768]{1,0:T(8,128)(2,1)S(1)}, bf16[128,768]{1,0:T(8,128)(2,1)S(1)}, u32[]{:S(2)}, u32[]{:S(2)}) collective-permute-start(bf16[128,768]{1,0:T(8,128)(2,1)S(1)} %get-tuple-element.42.refs_4_.refs_3_), channel_id=1, source_target_pairs={{0,4},{4,0},{8,12},{12,8},{16,20},{20,16},{24,28},{28,24},{1,5},{5... | collective-permute-start | bytes 589832 | tf_op jit(solution)/shard_map/ppermute | solution.py:316
  38.3 7.3 %collective-permute-start.4 = (bf16[64,768]{1,0:T(8,128)(2,1)S(1)}, bf16[64,768]{1,0:T(8,128)(2,1)S(1)}, u32[]{:S(2)}, u32[]{:S(2)}) collective-permute-start(bf16[64,768]{1,0:T(8,128)(2,1)S(1)} %get-tuple-element.38), channel_id=1, source_target_pairs={{0,24},{4,28},{8,16},{12,20},{16,8},{20,12},{24,0},{28,4},{1,25},{... | collective-permute-start | bytes 294920 | tf_op jit(solution)/shard_map/ppermute | solution.py:316
  40.7 6.1 %collective-permute-start.5 = (bf16[64,768]{1,0:T(8,128)(2,1)S(1)}, bf16[64,768]{1,0:T(8,128)(2,1)S(1)}, u32[]{:S(2)}, u32[]{:S(2)}) collective-permute-start(bf16[64,768]{1,0:T(8,128)(2,1)S(1)} %get-tuple-element.39), channel_id=1, source_target_pairs={{0,28},{4,24},{8,20},{12,16},{16,12},{20,8},{24,4},{28,0},{1,29},{... | collective-permute-start | bytes 294920 | tf_op jit(solution)/shard_map/ppermute | solution.py:316
  40.7 9.6 %collective-permute-start.6 = (bf16[128,768]{1,0:T(8,128)(2,1)S(1)}, bf16[128,768]{1,0:T(8,128)(2,1)S(1)}, u32[]{:S(2)}, u32[]{:S(2)}) collective-permute-start(bf16[128,768]{1,0:T(8,128)(2,1)S(1)} %get-tuple-element.40.refs_4_), channel_id=1, source_target_pairs={{0,8},{4,12},{8,0},{12,4},{16,24},{20,28},{24,16},{28,20},{1,9},{5... | collective-permute-start | bytes 589832 | tf_op jit(solution)/shard_map/ppermute | solution.py:316
  42.1 8.8 %collective-permute-start.7 = (bf16[128,768]{1,0:T(8,128)(2,1)S(1)}, bf16[128,768]{1,0:T(8,128)(2,1)S(1)}, u32[]{:S(2)}, u32[]{:S(2)}) collective-permute-start(bf16[128,768]{1,0:T(8,128)(2,1)S(1)} %get-tuple-element.41.refs_6_), channel_id=1, source_target_pairs={{0,16},{4,20},{8,24},{12,28},{16,0},{20,4},{24,8},{28,12},{1,17},{... | collective-permute-start | bytes 589832 | tf_op jit(solution)/shard_map/ppermute | solution.py:316
  43.6 5.1 %copy-start.3 = (bf16[128,768]{1,0:T(8,128)(2,1)S(1)}, bf16[128,768]{1,0:T(8,128)(2,1)}, u32[]{:S(2)}) copy-start(bf16[128,768]{1,0:T(8,128)(2,1)} %refs_1_.4) | copy-start | bytes 589828
  43.6 5.1 %copy-start.5 = (bf16[128,768]{1,0:T(8,128)(2,1)S(1)}, bf16[128,768]{1,0:T(8,128)(2,1)}, u32[]{:S(2)}) copy-start(bf16[128,768]{1,0:T(8,128)(2,1)} %refs_2_.3) | copy-start | bytes 589828
  46.8 6.9 %collective-permute-start.13 = (bf16[128,768]{1,0:T(8,128)(2,1)S(1)}, bf16[128,768]{1,0:T(8,128)(2,1)S(1)}, u32[]{:S(2)}, u32[]{:S(2)}) collective-permute-start(bf16[128,768]{1,0:T(8,128)(2,1)S(1)} %bitcast.11), channel_id=1, source_target_pairs={{0,1},{1,0},{2,3},{3,2},{4,5},{5,4},{6,7},{7,6},{8,9},{9,8},{10,11... | collective-permute-start | bytes 589832 | tf_op jit(solution)/shard_map/ppermute | solution.py:397
  47.4 7.1 %collective-permute-start.14 = (bf16[128,768]{1,0:T(8,128)(2,1)S(1)}, bf16[128,768]{1,0:T(8,128)(2,1)S(1)}, u32[]{:S(2)}, u32[]{:S(2)}) collective-permute-start(bf16[128,768]{1,0:T(8,128)(2,1)S(1)} %get-tuple-element.50.refs_5_), channel_id=1, source_target_pairs={{0,12},{4,8},{8,4},{12,0},{16,28},{20,24},{24,20},{28,16},{1,13},{... | collective-permute-start | bytes 589832 | tf_op jit(solution)/shard_map/ppermute | solution.py:316
  48.3 6.9 %collective-permute-start.15 = (bf16[128,768]{1,0:T(8,128)(2,1)S(1)}, bf16[128,768]{1,0:T(8,128)(2,1)S(1)}, u32[]{:S(2)}, u32[]{:S(2)}) collective-permute-start(bf16[128,768]{1,0:T(8,128)(2,1)S(1)} %get-tuple-element.51.refs_7_), channel_id=1, source_target_pairs={{0,20},{4,16},{8,28},{12,24},{16,4},{20,0},{24,12},{28,8},{1,21},{... | collective-permute-start | bytes 589832 | tf_op jit(solution)/shard_map/ppermute | solution.py:316
  50.1 5.1 %copy-start.7 = (bf16[128,768]{1,0:T(8,128)(2,1)S(1)}, bf16[128,768]{1,0:T(8,128)(2,1)}, u32[]{:S(2)}) copy-start(bf16[128,768]{1,0:T(8,128)(2,1)} %get-tuple-element.27.refs_5_) | copy-start | bytes 589828

commit v8 on v7

--- a/solution.py
+++ b/solution.py
@@ -355,7 +355,8 @@
         functools.partial(value_kernel, images), "value_rows",
         (shape(flat), shape(flat)), [SMEM, WHOLE, WHOLE], (WHOLE, WHOLE),
     )(info, received, weights)
-    middle, passed, first_one, _ = lax.optimization_barrier((patches, two, one, value_rows))
+    middle, first_one, ready = lax.optimization_barrier((patches, one, value_rows))
+    passed, _ = lax.optimization_barrier((two, ready))
     near = lax.ppermute(middle, "mp", [(1, 2), (2, 1)])
     far = lax.ppermute(passed, "mp", [(2, 3), (1, 0)])
     chip_values = [value_rows] + [across(value_rows, distance) for distance in (2, 4, 6)]

time: 57.5 us -> 56.6 us (0.984)
  waiting for transfers between devices: 14.6 us -> 12.4 us
  starting transfers between devices: 22.8 us -> 24.2 us
    ppermute x1, waiting for transfers between devices: 2.71 us -> 0.61 us  [fast_body(): far = lax.ppermute(passed, 'mp', [(2, 3), (1, 0)])]
    ppermute x1, waiting for transfers between devices: 0.19 us -> 1.97 us  [fast_body(): one = lax.ppermute(patches, 'mp', [(0, 1), (1, 0), (2, 3), (3, 2)])]
    ppermute x1, starting transfers between devices: 0.62 us -> 2.31 us  [fast_body(): moved[name] = lax.ppermute(part, 'mp', [(0, 1), (1, 0), (2, 3), (3, 2)])]
    ppermute x1, starting transfers between devices: 4.1 us -> 2.59 us  [fast_body(): two = lax.ppermute(patches, 'mp', [(0, 2), (2, 0), (1, 3), (3, 1)])]
    ppermute x1, starting transfers between devices: 1.58 us -> 3.09 us  [fast_body(): one = lax.ppermute(patches, 'mp', [(0, 1), (1, 0), (2, 3), (3, 2)])]
    ppermute x1, waiting for transfers between devices: 3.22 us -> 1.87 us  [fast_body(): two = lax.ppermute(patches, 'mp', [(0, 2), (2, 0), (1, 3), (3, 1)])]
  transfers between devices with their start and end apart: 17 -> 17, of which waited for: 10 -> 7; matrix products, arithmetic and copies ran while one was open for 3% -> 3% of each run, Pallas kernels for 17% -> 18%
where the time goes in v8:
time: 56.6 us; the launch traced here: 56.2 us
  starting transfers between devices  24.2 us (43%)
  waiting for transfers between devices  12.4 us (22%)
  Pallas kernels  11.7 us (21%)
  local copies, waits for them, and re-layouts  7.09 us (13%)
  between operations  0.79 us (1%)
    pallas_call x10, Pallas kernels, call(): return lambda *args: made(*args, *after)  11.7 us
    ppermute x11, starting transfers between devices, across(): return lax.ppermute(rows, 'dp', [(i, i ^ distance) for i in range(8)])  10.5 us
    unnamed x16, local copies, waits for them, and re-layouts  5.56 us
    all_to_all x1, waiting for transfers between devices, fast_body(): lax.all_to_all(head_cotangent.reshape(8, slots // 8, width), 'dp', split_...  3.93 us
    all_to_all x1, starting transfers between devices, fast_body(): lax.all_to_all(head_cotangent.reshape(8, slots // 8, width), 'dp', split_...  3.72 us
    ppermute x11, waiting for transfers between devices, across(): return lax.ppermute(rows, 'dp', [(i, i ^ distance) for i in range(8)])  3.27 us
    ppermute x1, starting transfers between devices, fast_body(): one = lax.ppermute(patches, 'mp', [(0, 1), (1, 0), (2, 3), (3, 2)])  3.09 us
    ppermute x1, starting transfers between devices, fast_body(): two = lax.ppermute(patches, 'mp', [(0, 2), (2, 0), (1, 3), (3, 1)])  2.59 us
  transfers between devices with their start and end apart: 17, of which 7 were waited for; matrix products, arithmetic and copies ran while one was open for 3% of the time, Pallas kernels for 18%

profile of v8, /device:TPU:0, one launch (start us, length us, event | category | flops | bytes accessed | tf_op | source)
XLA Modules:
  0.0 56.2 jit_solution(9793970450635218486)
XLA Ops:
  0.6 0.0 copy-start.6
  0.6 3.1 %collective-permute-start = (bf16[128,1536]{1,0:T(8,128)(2,1)}, bf16[128,1536]{1,0:T(8,128)(2,1)S(1)}, u32[]{:S(2)}, u32[]{:S(2)}) collective-permute-start(bf16[128,1536]{1,0:T(8,128)(2,1)} %refs_1_.2), channel_id=1, source_target_pairs={{0,1},{1,0},{2,3},{3,2},{4,5},{5,4},{6,7},{7,6},{8,9},{9,8},{10,11... | collective-permute-start | bytes 1179656 | tf_op jit(solution)/shard_map/ppermute | solution.py:348
  3.7 2.6 %collective-permute-start.1 = (bf16[128,1536]{1,0:T(8,128)(2,1)}, bf16[128,1536]{1,0:T(8,128)(2,1)S(1)}, u32[]{:S(2)}, u32[]{:S(2)}) collective-permute-start(bf16[128,1536]{1,0:T(8,128)(2,1)} %refs_1_.2), channel_id=1, source_target_pairs={{0,2},{2,0},{1,3},{3,1},{4,6},{6,4},{5,7},{7,5},{8,10},{10,8},{9,1... | collective-permute-start | bytes 1179656 | tf_op jit(solution)/shard_map/ppermute | solution.py:347
  6.3 3.7 %all-to-all-start = ((bf16[8,32,768]{2,1,0:T(8,128)(2,1)}), bf16[8,32,768]{2,1,0:T(8,128)(2,1)S(1)}, u32[]{:S(2)}, u32[]{:S(2)}) async-start(bf16[8,32,768]{2,1,0:T(8,128)(2,1)} %bitcast.12), calls=%async_computation | async-start | bytes 786432 | tf_op jit(solution)/shard_map/all_to_all | solution.py:344
  10.0 0.7 %reshape.20.refs_1_ = f32[8,768]{1,0:T(8,128)S(1)} reshape(f32[6144]{0:T(1024)} %param.9) | data formatting | bytes 49152 | tf_op jit(solution)/shard_map/reshape | solution.py:353
  10.8 0.7 %dynamic-slice_bitcast_fusion = (s32[8]{0:T(128)S(1)}, s32[8]{0:T(128)S(1)}) fusion(s32[8,8]{1,0:T(8,128)} %param.15, s32[]{:T(128)S(6)} %select_n.18, s32[8,8]{1,0:T(8,128)} %param.14), kind=kLoop, calls=%fused_computation | loop fusion | bytes 132 | tf_op jit(solution)/shard_map/jit(dynamic_index_in_dim)/squeeze | solution.py:340
  11.5 0.1 concatenate.3.refs_0_
  11.6 0.0 copy-start.2
  11.6 0.9 %copy-done.2 = bf16[128,768]{1,0:T(8,128)(2,1)S(1)} copy-done((bf16[128,768]{1,0:T(8,128)(2,1)S(1)}, bf16[128,768]{1,0:T(8,128)(2,1)}, u32[]{:S(2)}) %copy-start.2) | copy-done | bytes 196632
  12.5 0.0 copy-start.4
  12.5 0.9 %copy-done.4 = bf16[128,768]{1,0:T(8,128)(2,1)S(1)} copy-done((bf16[128,768]{1,0:T(8,128)(2,1)S(1)}, bf16[128,768]{1,0:T(8,128)(2,1)}, u32[]{:S(2)}) %copy-start.4) | copy-done | bytes 196632
  13.4 1.0 %attention_weights.1 = (f32[6,128,128]{2,1,0:T(8,128)S(1)}, f32[8,768]{1,0:T(8,128)S(1)}) custom-call(s32[24]{0:T(128)S(1)} %concatenate.3.refs_0_, f32[8,768]{1,0:T(8,128)S(1)} %reshape.20.refs_1_, bf16[128,768]{1,0:T(8,128)(2,1)S(1)} %copy-done.2, bf16[128,768]{1,0:T(8,128)(2,1)S(1)} %copy-done.4), custom_call_target="tpu_custom_call" | custom-call | flops 1 | bytes 1 | tf_op jit(solution)/shard_map/attention_weights/pallas_call | solution.py:312
  14.5 3.9 %all-to-all-done = bf16[8,32,768]{2,1,0:T(8,128)(2,1)S(1)} async-done(((bf16[8,32,768]{2,1,0:T(8,128)(2,1)}), bf16[8,32,768]{2,1,0:T(8,128)(2,1)S(1)}, u32[]{:S(2)}, u32[]{:S(2)}) %all-to-all-start) | async-done | bytes 393248 | tf_op jit(solution)/shard_map/all_to_all | solution.py:344
  18.4 1.0 %value_rows.1 = (bf16[128,768]{1,0:T(8,128)(2,1)S(1)}, bf16[128,768]{1,0:T(8,128)(2,1)S(1)}) custom-call(s32[24]{0:T(128)S(1)} %concatenate.3.refs_0_, bf16[256,768]{1,0:T(8,128)(2,1)S(1)} %bitcast.10, f32[6,128,128]{2,1,0:T(8,128)S(1)} %get-tuple-element.28.refs_2_.refs_4_), custom_call_target="tpu_custom_call" | custom-call | flops 1 | bytes 1 | tf_op jit(solution)/shard_map/value_rows/pallas_call | solution.py:312
  19.4 2.0 %collective-permute-done.refs_3_ = bf16[128,1536]{1,0:T(8,128)(2,1)S(1)} collective-permute-done((bf16[128,1536]{1,0:T(8,128)(2,1)}, bf16[128,1536]{1,0:T(8,128)(2,1)S(1)}, u32[]{:S(2)}, u32[]{:S(2)}) %collective-permute-start) | collective-permute-done | bytes 393248 | tf_op jit(solution)/shard_map/ppermute | solution.py:348
  21.4 0.7 %collective-permute-start.2 = (bf16[128,1536]{1,0:T(8,128)(2,1)}, bf16[128,1536]{1,0:T(8,128)(2,1)S(1)}, u32[]{:S(2)}, u32[]{:S(2)}) collective-permute-start(bf16[128,1536]{1,0:T(8,128)(2,1)} %refs_1_.2), channel_id=1, source_target_pairs={{1,2},{2,1},{5,6},{6,5},{9,10},{10,9},{13,14},{14,13},{17,18},{18,... | collective-permute-start | bytes 1179656 | tf_op jit(solution)/shard_map/ppermute | solution.py:360
  22.0 1.9 %collective-permute-done.1.refs_2_ = bf16[128,1536]{1,0:T(8,128)(2,1)S(1)} collective-permute-done((bf16[128,1536]{1,0:T(8,128)(2,1)}, bf16[128,1536]{1,0:T(8,128)(2,1)S(1)}, u32[]{:S(2)}, u32[]{:S(2)}) %collective-permute-start.1) | collective-permute-done | bytes 393248 | tf_op jit(solution)/shard_map/ppermute | solution.py:347
  23.9 1.3 %collective-permute-start.3 = (bf16[128,1536]{1,0:T(8,128)(2,1)S(1)}, bf16[128,1536]{1,0:T(8,128)(2,1)S(1)}, u32[]{:S(2)}, u32[]{:S(2)}) collective-permute-start(bf16[128,1536]{1,0:T(8,128)(2,1)S(1)} %collective-permute-done.1.refs_2_), channel_id=1, source_target_pairs={{2,3},{1,0},{6,7},{5,4},{10,11},{9,8},{14,15},{13,12},{18,19},{17,... | collective-permute-start | bytes 1179656 | tf_op jit(solution)/shard_map/ppermute | solution.py:361
  25.2 2.5 %collective-permute-start.11 = (bf16[128,768]{1,0:T(8,128)(2,1)S(1)}, bf16[128,768]{1,0:T(8,128)(2,1)S(1)}, u32[]{:S(2)}, u32[]{:S(2)}) collective-permute-start(bf16[128,768]{1,0:T(8,128)(2,1)S(1)} %get-tuple-element.29.refs_0_.refs_7_), channel_id=1, source_target_pairs={{0,24},{4,28},{8,16},{12,20},{16,8},{20,12},{24,0},{28,4},{1,25},{... | collective-permute-start | bytes 589832 | tf_op jit(solution)/shard_map/ppermute | solution.py:316
  27.7 0.5 collective-permute-start.10
  28.2 0.5 collective-permute-start.9
  28.8 0.0 copy-done.6
  28.8 0.0 copy-start
  28.8 3.7 %copy-done = bf16[6144,768]{1,0:T(8,128)(2,1)S(1)} copy-done((bf16[6144,768]{1,0:T(8,128)(2,1)S(1)}, bf16[6144,768]{1,0:T(8,128)(2,1)}, u32[]{:S(2)}) %copy-start) | copy-done | bytes 9437208
  32.4 0.0 copy-start.1
  32.4 1.2 %partial_stats.1 = (f32[128,128]{1,0:T(8,128)S(1)}, bf16[4,128,1536]{2,1,0:T(8,128)(2,1)S(1)}) custom-call(s32[24]{0:T(128)S(1)} %concatenate.3.refs_0_, bf16[128,1536]{1,0:T(8,128)(2,1)S(1)} %copy-done.6, bf16[128,1536]{1,0:T(8,128)(2,1)S(1)} %collective-permute-done.1.refs_2_, bf16[128,1536]{1,0:T(8,128)(2,1)S(1)} %collective-permute-done.refs_3_, ...), custom_call_target="tpu_custom_call" | custom-call | flops 1 | bytes 1 | tf_op jit(solution)/shard_map/partial_stats/pallas_call | solution.py:312
  33.6 0.0 collective-permute-done.2.refs_4_
  33.6 0.6 %collective-permute-done.3.refs_5_ = bf16[128,1536]{1,0:T(8,128)(2,1)S(1)} collective-permute-done((bf16[128,1536]{1,0:T(8,128)(2,1)S(1)}, bf16[128,1536]{1,0:T(8,128)(2,1)S(1)}, u32[]{:S(2)}, u32[]{:S(2)}) %collective-permute-start.3) | collective-permute-done | bytes 393248 | tf_op jit(solution)/shard_map/ppermute | solution.py:361
  34.2 1.7 %norm_rows.1 = (bf16[128,768]{1,0:T(8,128)(2,1)S(1)}, bf16[128,768]{1,0:T(8,128)(2,1)S(1)}, bf16[128,768]{1,0:T(8,128)(2,1)S(1)}, bf16[128,768]{1,0:T(8,128)(2,1...) custom-call(s32[24]{0:T(128)S(1)} %concatenate.3.refs_0_, ...), custom_call_target="tpu_custom_call" | custom-call | flops 1 | bytes 1 | tf_op jit(solution)/shard_map/norm_rows/pallas_call | solution.py:312
  35.9 0.0 collective-permute-done.11.refs_3_.refs_10_
  35.9 0.0 collective-permute-done.10.refs_2_.refs_9_
  35.9 0.0 collective-permute-done.9.refs_1_.refs_8_
  36.0 0.1 pack_values.1
  36.0 0.1 collective-permute-start.12
  36.1 0.5 collective-permute-start.8
  36.6 2.3 %collective-permute-start.4 = (bf16[64,768]{1,0:T(8,128)(2,1)S(1)}, bf16[64,768]{1,0:T(8,128)(2,1)S(1)}, u32[]{:S(2)}, u32[]{:S(2)}) collective-permute-start(bf16[64,768]{1,0:T(8,128)(2,1)S(1)} %get-tuple-element.36), channel_id=1, source_target_pairs={{0,24},{4,28},{8,16},{12,20},{16,8},{20,12},{24,0},{28,4},{1,25},{... | collective-permute-start | bytes 294920 | tf_op jit(solution)/shard_map/ppermute | solution.py:316
  38.9 0.0 collective-permute-start.5
  38.9 1.3 %collective-permute-start.6 = (bf16[128,768]{1,0:T(8,128)(2,1)S(1)}, bf16[128,768]{1,0:T(8,128)(2,1)S(1)}, u32[]{:S(2)}, u32[]{:S(2)}) collective-permute-start(bf16[128,768]{1,0:T(8,128)(2,1)S(1)} %get-tuple-element.38.refs_4_), channel_id=1, source_target_pairs={{0,8},{4,12},{8,0},{12,4},{16,24},{20,28},{24,16},{28,20},{1,9},{5... | collective-permute-start | bytes 589832 | tf_op jit(solution)/shard_map/ppermute | solution.py:316
  40.3 0.0 collective-permute-done.8.refs_6_.refs_11_
  40.3 1.5 %collective-permute-start.7 = (bf16[128,768]{1,0:T(8,128)(2,1)S(1)}, bf16[128,768]{1,0:T(8,128)(2,1)S(1)}, u32[]{:S(2)}, u32[]{:S(2)}) collective-permute-start(bf16[128,768]{1,0:T(8,128)(2,1)S(1)} %get-tuple-element.39.refs_6_), channel_id=1, source_target_pairs={{0,16},{4,20},{8,24},{12,28},{16,0},{20,4},{24,8},{28,12},{1,17},{... | collective-permute-start | bytes 589832 | tf_op jit(solution)/shard_map/ppermute | solution.py:316
  41.8 0.0 collective-permute-done.12.refs_11_.refs_10_
  41.8 0.0 copy-done.1
  41.8 0.0 copy-start.3
  41.8 0.0 copy-start.5
  41.8 1.9 %project_values.1.refs_2_.refs_0_ = bf16[128,768]{1,0:T(8,128)(2,1)S(1)} custom-call(s32[24]{0:T(128)S(1)} %concatenate.3.refs_0_, bf16[6144,768]{1,0:T(8,128)(2,1)S(1)} %copy-done.1, bf16[128,768]{1,0:T(8,128)(2,1)S(1)} %get-tuple-element.35.refs_1_.refs_2_, bf16[128,768]{1,0:T(8,128)(2,1)S(1)} %get-tuple-element.40.refs_4_.refs_3_, ...), custom_call_target="tpu_custom_call" | custom-call | flops 1 | bytes 1 | tf_op jit(solution)/shard_map/project_values/pallas_call | solution.py:312
  43.7 0.0 collective-permute-done.4.refs_2_.refs_0_
  43.7 1.2 %collective-permute-done.5.refs_3_.refs_1_ = bf16[64,768]{1,0:T(8,128)(2,1)S(1)} collective-permute-done((bf16[64,768]{1,0:T(8,128)(2,1)S(1)}, bf16[64,768]{1,0:T(8,128)(2,1)S(1)}, u32[]{:S(2)}, u32[]{:S(2)}) %collective-permute-start.5) | collective-permute-done | bytes 98336 | tf_op jit(solution)/shard_map/ppermute | solution.py:316
  45.0 2.3 %collective-permute-start.13 = (bf16[128,768]{1,0:T(8,128)(2,1)S(1)}, bf16[128,768]{1,0:T(8,128)(2,1)S(1)}, u32[]{:S(2)}, u32[]{:S(2)}) collective-permute-start(bf16[128,768]{1,0:T(8,128)(2,1)S(1)} %bitcast.11), channel_id=1, source_target_pairs={{0,1},{1,0},{2,3},{3,2},{4,5},{5,4},{6,7},{7,6},{8,9},{9,8},{10,11... | collective-permute-start | bytes 589832 | tf_op jit(solution)/shard_map/ppermute | solution.py:398
  47.3 0.2 collective-permute-start.14
  47.5 1.0 %collective-permute-start.15 = (bf16[128,768]{1,0:T(8,128)(2,1)S(1)}, bf16[128,768]{1,0:T(8,128)(2,1)S(1)}, u32[]{:S(2)}, u32[]{:S(2)}) collective-permute-start(bf16[128,768]{1,0:T(8,128)(2,1)S(1)} %get-tuple-element.49.refs_7_), channel_id=1, source_target_pairs={{0,20},{4,16},{8,28},{12,24},{16,4},{20,0},{24,12},{28,8},{1,21},{... | collective-permute-start | bytes 589832 | tf_op jit(solution)/shard_map/ppermute | solution.py:316
  48.5 0.0 copy-done.3
  48.5 0.0 copy-done.5
  48.5 1.4 %attention_backward.1 = (bf16[128,768]{1,0:T(8,128)(2,1)}, bf16[128,768]{1,0:T(8,128)(2,1)}) custom-call(bf16[128,768]{1,0:T(8,128)(2,1)S(1)} %project_values.1.refs_2_.refs_0_, bf16[128,768]{1,0:T(8,128)(2,1)S(1)} %copy-done.3, bf16[128,768]{1,0:T(8,128)(2,1)S(1)} %copy-done.5, bf16[128,768]{1,0:T(8,128)(2,1)S(1)} %get-tuple-element.50.refs_3_, ...), custom_call_target="tpu_custom_call" | custom-call | flops 1 | bytes 1 | tf_op jit(solution)/shard_map/attention_backward/pallas_call | solution.py:312
  49.9 0.0 copy-start.7
  49.9 0.0 collective-permute-done.6.refs_4_
  49.9 0.0 collective-permute-done.7.refs_5_
  49.9 1.7 %gradient_first.1 = (f32[768,768]{1,0:T(8,128)S(1)}, bf16[384,768]{1,0:T(8,128)(2,1)S(1)}) custom-call(s32[24]{0:T(128)S(1)} %concatenate.3.refs_0_, bf16[128,768]{1,0:T(8,128)(2,1)S(1)} %get-tuple-element.35.refs_1_.refs_2_, bf16[64,768]{1,0:T(8,128)(2,1)S(1)} %collective-permute-done.4.refs_2_.refs_0_, ...), custom_call_target="tpu_custom_call" | custom-call | flops 1 | bytes 1 | tf_op jit(solution)/shard_map/gradient_first/pallas_call | solution.py:312
  51.6 0.8 %collective-permute-done.13.refs_2_ = bf16[128,768]{1,0:T(8,128)(2,1)S(1)} collective-permute-done((bf16[128,768]{1,0:T(8,128)(2,1)S(1)}, bf16[128,768]{1,0:T(8,128)(2,1)S(1)}, u32[]{:S(2)}, u32[]{:S(2)}) %collective-permute-start.13) | collective-permute-done | bytes 196640 | tf_op jit(solution)/shard_map/ppermute | solution.py:398
  52.3 2.0 %collective-permute-done.14.refs_3_ = bf16[128,768]{1,0:T(8,128)(2,1)S(1)} collective-permute-done((bf16[128,768]{1,0:T(8,128)(2,1)S(1)}, bf16[128,768]{1,0:T(8,128)(2,1)S(1)}, u32[]{:S(2)}, u32[]{:S(2)}) %collective-permute-start.14) | collective-permute-done | bytes 196640 | tf_op jit(solution)/shard_map/ppermute | solution.py:316
  54.4 0.0 collective-permute-done.15.refs_4_
  54.4 0.0 copy-done.7
  54.4 1.8 %gradient_last.1 = f32[768,768]{1,0:T(8,128)} custom-call(f32[768,768]{1,0:T(8,128)S(1)} %get-tuple-element.41.refs_0_, bf16[384,768]{1,0:T(8,128)(2,1)S(1)} %get-tuple-element.42.refs_1_, bf16[128,768]{1,0:T(8,128)(2,1)S(1)} %collective-permute-done.13.refs_2_, bf16[128,768]{1,0:T(8,128)(2,1)S(1)} %collective-permute-done.14.refs_3_, ...), custom_call_target="tpu_custom_call" | custom-call | flops 1 | bytes 1 | tf_op jit(solution)/shard_map/gradient_last/pallas_call | solution.py:312
  (2 shorter events, 0.0 us)
Async XLA Ops:
  0.6 28.1 %copy-start.6 = (bf16[128,1536]{1,0:T(8,128)(2,1)S(1)}, bf16[128,1536]{1,0:T(8,128)(2,1)}, u32[]{:S(2)}) copy-start(bf16[128,1536]{1,0:T(8,128)(2,1)} %refs_1_.2) | copy-start | bytes 1179652
  0.6 20.7 %collective-permute-start = (bf16[128,1536]{1,0:T(8,128)(2,1)}, bf16[128,1536]{1,0:T(8,128)(2,1)S(1)}, u32[]{:S(2)}, u32[]{:S(2)}) collective-permute-start(bf16[128,1536]{1,0:T(8,128)(2,1)} %refs_1_.2), channel_id=1, source_target_pairs={{0,1},{1,0},{2,3},{3,2},{4,5},{5,4},{6,7},{7,6},{8,9},{9,8},{10,11... | collective-permute-start | bytes 1179656 | tf_op jit(solution)/shard_map/ppermute | solution.py:348
  3.7 20.2 %collective-permute-start.1 = (bf16[128,1536]{1,0:T(8,128)(2,1)}, bf16[128,1536]{1,0:T(8,128)(2,1)S(1)}, u32[]{:S(2)}, u32[]{:S(2)}) collective-permute-start(bf16[128,1536]{1,0:T(8,128)(2,1)} %refs_1_.2), channel_id=1, source_target_pairs={{0,2},{2,0},{1,3},{3,1},{4,6},{6,4},{5,7},{7,5},{8,10},{10,8},{9,1... | collective-permute-start | bytes 1179656 | tf_op jit(solution)/shard_map/ppermute | solution.py:347
  6.3 12.1 %all-to-all-start = ((bf16[8,32,768]{2,1,0:T(8,128)(2,1)}), bf16[8,32,768]{2,1,0:T(8,128)(2,1)S(1)}, u32[]{:S(2)}, u32[]{:S(2)}) async-start(bf16[8,32,768]{2,1,0:T(8,128)(2,1)} %bitcast.12), calls=%async_computation | async-start | bytes 786432 | tf_op jit(solution)/shard_map/all_to_all | solution.py:344
  11.6 0.9 %copy-start.2 = (bf16[128,768]{1,0:T(8,128)(2,1)S(1)}, bf16[128,768]{1,0:T(8,128)(2,1)}, u32[]{:S(2)}) copy-start(bf16[128,768]{1,0:T(8,128)(2,1)} %refs_1_.4) | copy-start | bytes 589828
  12.5 0.9 %copy-start.4 = (bf16[128,768]{1,0:T(8,128)(2,1)S(1)}, bf16[128,768]{1,0:T(8,128)(2,1)}, u32[]{:S(2)}) copy-start(bf16[128,768]{1,0:T(8,128)(2,1)} %refs_2_.3) | copy-start | bytes 589828
  21.4 12.3 %collective-permute-start.2 = (bf16[128,1536]{1,0:T(8,128)(2,1)}, bf16[128,1536]{1,0:T(8,128)(2,1)S(1)}, u32[]{:S(2)}, u32[]{:S(2)}) collective-permute-start(bf16[128,1536]{1,0:T(8,128)(2,1)} %refs_1_.2), channel_id=1, source_target_pairs={{1,2},{2,1},{5,6},{6,5},{9,10},{10,9},{13,14},{14,13},{17,18},{18,... | collective-permute-start | bytes 1179656 | tf_op jit(solution)/shard_map/ppermute | solution.py:360
  23.9 10.3 %collective-permute-start.3 = (bf16[128,1536]{1,0:T(8,128)(2,1)S(1)}, bf16[128,1536]{1,0:T(8,128)(2,1)S(1)}, u32[]{:S(2)}, u32[]{:S(2)}) collective-permute-start(bf16[128,1536]{1,0:T(8,128)(2,1)S(1)} %collective-permute-done.1.refs_2_), channel_id=1, source_target_pairs={{2,3},{1,0},{6,7},{5,4},{10,11},{9,8},{14,15},{13,12},{18,19},{17,... | collective-permute-start | bytes 1179656 | tf_op jit(solution)/shard_map/ppermute | solution.py:361
  25.2 10.7 %collective-permute-start.11 = (bf16[128,768]{1,0:T(8,128)(2,1)S(1)}, bf16[128,768]{1,0:T(8,128)(2,1)S(1)}, u32[]{:S(2)}, u32[]{:S(2)}) collective-permute-start(bf16[128,768]{1,0:T(8,128)(2,1)S(1)} %get-tuple-element.29.refs_0_.refs_7_), channel_id=1, source_target_pairs={{0,24},{4,28},{8,16},{12,20},{16,8},{20,12},{24,0},{28,4},{1,25},{... | collective-permute-start | bytes 589832 | tf_op jit(solution)/shard_map/ppermute | solution.py:316
  27.7 8.2 %collective-permute-start.10 = (bf16[128,768]{1,0:T(8,128)(2,1)S(1)}, bf16[128,768]{1,0:T(8,128)(2,1)S(1)}, u32[]{:S(2)}, u32[]{:S(2)}) collective-permute-start(bf16[128,768]{1,0:T(8,128)(2,1)S(1)} %get-tuple-element.29.refs_0_.refs_7_), channel_id=1, source_target_pairs={{0,16},{4,20},{8,24},{12,28},{16,0},{20,4},{24,8},{28,12},{1,17},{... | collective-permute-start | bytes 589832 | tf_op jit(solution)/shard_map/ppermute | solution.py:316
  28.2 7.7 %collective-permute-start.9 = (bf16[128,768]{1,0:T(8,128)(2,1)S(1)}, bf16[128,768]{1,0:T(8,128)(2,1)S(1)}, u32[]{:S(2)}, u32[]{:S(2)}) collective-permute-start(bf16[128,768]{1,0:T(8,128)(2,1)S(1)} %get-tuple-element.29.refs_0_.refs_7_), channel_id=1, source_target_pairs={{0,8},{4,12},{8,0},{12,4},{16,24},{20,28},{24,16},{28,20},{1,9},{5... | collective-permute-start | bytes 589832 | tf_op jit(solution)/shard_map/ppermute | solution.py:316
  28.8 3.7 %copy-start = (bf16[6144,768]{1,0:T(8,128)(2,1)S(1)}, bf16[6144,768]{1,0:T(8,128)(2,1)}, u32[]{:S(2)}) copy-start(bf16[6144,768]{1,0:T(8,128)(2,1)} %refs_1_.3) | copy-start | bytes 28311556
  32.4 9.3 %copy-start.1 = (bf16[6144,768]{1,0:T(8,128)(2,1)S(1)}, bf16[6144,768]{1,0:T(8,128)(2,1)}, u32[]{:S(2)}) copy-start(bf16[6144,768]{1,0:T(8,128)(2,1)} %refs_1_.3) | copy-start | bytes 28311556
  36.0 5.8 %collective-permute-start.12 = (bf16[4,128,768]{2,1,0:T(8,128)(2,1)S(1)}, bf16[4,128,768]{2,1,0:T(8,128)(2,1)S(1)}, u32[]{:S(2)}, u32[]{:S(2)}) collective-permute-start(bf16[4,128,768]{2,1,0:T(8,128)(2,1)S(1)} %pack_values.1), channel_id=1, source_target_pairs={{0,4},{4,0},{8,12},{12,8},{16,20},{20,16},{24,28},{28,24},{1,5},{5... | collective-permute-start | bytes 2359304 | tf_op jit(solution)/shard_map/ppermute | solution.py:316
  36.1 4.2 %collective-permute-start.8 = (bf16[128,768]{1,0:T(8,128)(2,1)S(1)}, bf16[128,768]{1,0:T(8,128)(2,1)S(1)}, u32[]{:S(2)}, u32[]{:S(2)}) collective-permute-start(bf16[128,768]{1,0:T(8,128)(2,1)S(1)} %get-tuple-element.40.refs_4_.refs_3_), channel_id=1, source_target_pairs={{0,4},{4,0},{8,12},{12,8},{16,20},{20,16},{24,28},{28,24},{1,5},{5... | collective-permute-start | bytes 589832 | tf_op jit(solution)/shard_map/ppermute | solution.py:316
  36.6 7.2 %collective-permute-start.4 = (bf16[64,768]{1,0:T(8,128)(2,1)S(1)}, bf16[64,768]{1,0:T(8,128)(2,1)S(1)}, u32[]{:S(2)}, u32[]{:S(2)}) collective-permute-start(bf16[64,768]{1,0:T(8,128)(2,1)S(1)} %get-tuple-element.36), channel_id=1, source_target_pairs={{0,24},{4,28},{8,16},{12,20},{16,8},{20,12},{24,0},{28,4},{1,25},{... | collective-permute-start | bytes 294920 | tf_op jit(solution)/shard_map/ppermute | solution.py:316
  38.9 6.1 %collective-permute-start.5 = (bf16[64,768]{1,0:T(8,128)(2,1)S(1)}, bf16[64,768]{1,0:T(8,128)(2,1)S(1)}, u32[]{:S(2)}, u32[]{:S(2)}) collective-permute-start(bf16[64,768]{1,0:T(8,128)(2,1)S(1)} %get-tuple-element.37), channel_id=1, source_target_pairs={{0,28},{4,24},{8,20},{12,16},{16,12},{20,8},{24,4},{28,0},{1,29},{... | collective-permute-start | bytes 294920 | tf_op jit(solution)/shard_map/ppermute | solution.py:316
  38.9 11.0 %collective-permute-start.6 = (bf16[128,768]{1,0:T(8,128)(2,1)S(1)}, bf16[128,768]{1,0:T(8,128)(2,1)S(1)}, u32[]{:S(2)}, u32[]{:S(2)}) collective-permute-start(bf16[128,768]{1,0:T(8,128)(2,1)S(1)} %get-tuple-element.38.refs_4_), channel_id=1, source_target_pairs={{0,8},{4,12},{8,0},{12,4},{16,24},{20,28},{24,16},{28,20},{1,9},{5... | collective-permute-start | bytes 589832 | tf_op jit(solution)/shard_map/ppermute | solution.py:316
  40.3 9.6 %collective-permute-start.7 = (bf16[128,768]{1,0:T(8,128)(2,1)S(1)}, bf16[128,768]{1,0:T(8,128)(2,1)S(1)}, u32[]{:S(2)}, u32[]{:S(2)}) collective-permute-start(bf16[128,768]{1,0:T(8,128)(2,1)S(1)} %get-tuple-element.39.refs_6_), channel_id=1, source_target_pairs={{0,16},{4,20},{8,24},{12,28},{16,0},{20,4},{24,8},{28,12},{1,17},{... | collective-permute-start | bytes 589832 | tf_op jit(solution)/shard_map/ppermute | solution.py:316
  41.8 6.7 %copy-start.3 = (bf16[128,768]{1,0:T(8,128)(2,1)S(1)}, bf16[128,768]{1,0:T(8,128)(2,1)}, u32[]{:S(2)}) copy-start(bf16[128,768]{1,0:T(8,128)(2,1)} %refs_1_.4) | copy-start | bytes 589828
  41.8 6.7 %copy-start.5 = (bf16[128,768]{1,0:T(8,128)(2,1)S(1)}, bf16[128,768]{1,0:T(8,128)(2,1)}, u32[]{:S(2)}) copy-start(bf16[128,768]{1,0:T(8,128)(2,1)} %refs_2_.3) | copy-start | bytes 589828
  45.0 7.4 %collective-permute-start.13 = (bf16[128,768]{1,0:T(8,128)(2,1)S(1)}, bf16[128,768]{1,0:T(8,128)(2,1)S(1)}, u32[]{:S(2)}, u32[]{:S(2)}) collective-permute-start(bf16[128,768]{1,0:T(8,128)(2,1)S(1)} %bitcast.11), channel_id=1, source_target_pairs={{0,1},{1,0},{2,3},{3,2},{4,5},{5,4},{6,7},{7,6},{8,9},{9,8},{10,11... | collective-permute-start | bytes 589832 | tf_op jit(solution)/shard_map/ppermute | solution.py:398
  47.3 7.1 %collective-permute-start.14 = (bf16[128,768]{1,0:T(8,128)(2,1)S(1)}, bf16[128,768]{1,0:T(8,128)(2,1)S(1)}, u32[]{:S(2)}, u32[]{:S(2)}) collective-permute-start(bf16[128,768]{1,0:T(8,128)(2,1)S(1)} %get-tuple-element.48.refs_5_), channel_id=1, source_target_pairs={{0,12},{4,8},{8,4},{12,0},{16,28},{20,24},{24,20},{28,16},{1,13},{... | collective-permute-start | bytes 589832 | tf_op jit(solution)/shard_map/ppermute | solution.py:316
  47.5 6.9 %collective-permute-start.15 = (bf16[128,768]{1,0:T(8,128)(2,1)S(1)}, bf16[128,768]{1,0:T(8,128)(2,1)S(1)}, u32[]{:S(2)}, u32[]{:S(2)}) collective-permute-start(bf16[128,768]{1,0:T(8,128)(2,1)S(1)} %get-tuple-element.49.refs_7_), channel_id=1, source_target_pairs={{0,20},{4,16},{8,28},{12,24},{16,4},{20,0},{24,12},{28,8},{1,21},{... | collective-permute-start | bytes 589832 | tf_op jit(solution)/shard_map/ppermute | solution.py:316
  49.9 4.5 %copy-start.7 = (bf16[128,768]{1,0:T(8,128)(2,1)S(1)}, bf16[128,768]{1,0:T(8,128)(2,1)}, u32[]{:S(2)}) copy-start(bf16[128,768]{1,0:T(8,128)(2,1)} %get-tuple-element.26.refs_5_) | copy-start | bytes 589828

commit v9 on v8

--- a/solution.py
+++ b/solution.py
@@ -11,7 +11,7 @@
 HEADER = 8
 FIRST = (0,6,7,2,4,1)
 LAST = (20,3,5)
-LATE = (20,3,5)
+LATE = (20, 5)
 HALVED = (6, 7)
 SWAPPED = 20
 

time: 56.6 us -> 56.6 us (level)
  waiting for transfers between devices: 12.4 us -> 13 us
  starting transfers between devices: 24.2 us -> 23.6 us
    ppermute x11, waiting for transfers between devices: 3.27 us -> 4.64 us  [across(): return lax.ppermute(rows, 'dp', [(i, i ^ distance) for i in range(8)])]
    ppermute x1, waiting for transfers between devices: 0.76 us -> 0.01 us  [fast_body(): moved[name] = lax.ppermute(part, 'mp', [(0, 1), (1, 0), (2, 3), (3, 2)])]
    ppermute x11, starting transfers between devices: 10.5 us -> 9.91 us  [across(): return lax.ppermute(rows, 'dp', [(i, i ^ distance) for i in range(8)])]
  transfers between devices with their start and end apart: 17 -> 17, of which waited for: 7 -> 8; matrix products, arithmetic and copies ran while one was open for 3% -> 3% of each run, Pallas kernels for 18% -> 18%
where the time goes in v9:
time: 56.6 us; the launch traced here: 56.2 us
  starting transfers between devices  23.6 us (42%)
  waiting for transfers between devices  13 us (23%)
  Pallas kernels  11.7 us (21%)
  local copies, waits for them, and re-layouts  7.09 us (13%)
  between operations  0.78 us (1%)
    pallas_call x10, Pallas kernels, call(): return lambda *args: made(*args, *after)  11.7 us
    ppermute x11, starting transfers between devices, across(): return lax.ppermute(rows, 'dp', [(i, i ^ distance) for i in range(8)])  9.91 us
    unnamed x16, local copies, waits for them, and re-layouts  5.56 us
    ppermute x11, waiting for transfers between devices, across(): return lax.ppermute(rows, 'dp', [(i, i ^ distance) for i in range(8)])  4.64 us
    all_to_all x1, waiting for transfers between devices, fast_body(): lax.all_to_all(head_cotangent.reshape(8, slots // 8, width), 'dp', split_...  3.93 us
    all_to_all x1, starting transfers between devices, fast_body(): lax.all_to_all(head_cotangent.reshape(8, slots // 8, width), 'dp', split_...  3.72 us
    ppermute x1, starting transfers between devices, fast_body(): one = lax.ppermute(patches, 'mp', [(0, 1), (1, 0), (2, 3), (3, 2)])  3.09 us
    ppermute x1, starting transfers between devices, fast_body(): two = lax.ppermute(patches, 'mp', [(0, 2), (2, 0), (1, 3), (3, 1)])  2.59 us
  transfers between devices with their start and end apart: 17, of which 8 were waited for; matrix products, arithmetic and copies ran while one was open for 3% of the time, Pallas kernels for 18%

profile of v9, /device:TPU:0, one launch (start us, length us, event | category | flops | bytes accessed | tf_op | source)
XLA Modules:
  0.0 56.2 jit_solution(1028682681451100352)
XLA Ops:
  0.6 0.0 copy-start.6
  0.6 3.1 %collective-permute-start = (bf16[128,1536]{1,0:T(8,128)(2,1)}, bf16[128,1536]{1,0:T(8,128)(2,1)S(1)}, u32[]{:S(2)}, u32[]{:S(2)}) collective-permute-start(bf16[128,1536]{1,0:T(8,128)(2,1)} %refs_1_.2), channel_id=1, source_target_pairs={{0,1},{1,0},{2,3},{3,2},{4,5},{5,4},{6,7},{7,6},{8,9},{9,8},{10,11... | collective-permute-start | bytes 1179656 | tf_op jit(solution)/shard_map/ppermute | solution.py:348
  3.7 2.6 %collective-permute-start.1 = (bf16[128,1536]{1,0:T(8,128)(2,1)}, bf16[128,1536]{1,0:T(8,128)(2,1)S(1)}, u32[]{:S(2)}, u32[]{:S(2)}) collective-permute-start(bf16[128,1536]{1,0:T(8,128)(2,1)} %refs_1_.2), channel_id=1, source_target_pairs={{0,2},{2,0},{1,3},{3,1},{4,6},{6,4},{5,7},{7,5},{8,10},{10,8},{9,1... | collective-permute-start | bytes 1179656 | tf_op jit(solution)/shard_map/ppermute | solution.py:347
  6.3 3.7 %all-to-all-start = ((bf16[8,32,768]{2,1,0:T(8,128)(2,1)}), bf16[8,32,768]{2,1,0:T(8,128)(2,1)S(1)}, u32[]{:S(2)}, u32[]{:S(2)}) async-start(bf16[8,32,768]{2,1,0:T(8,128)(2,1)} %bitcast.12), calls=%async_computation | async-start | bytes 786432 | tf_op jit(solution)/shard_map/all_to_all | solution.py:344
  10.0 0.7 %reshape.20.refs_1_ = f32[8,768]{1,0:T(8,128)S(1)} reshape(f32[6144]{0:T(1024)} %param.9) | data formatting | bytes 49152 | tf_op jit(solution)/shard_map/reshape | solution.py:353
  10.8 0.7 %dynamic-slice_bitcast_fusion = (s32[8]{0:T(128)S(1)}, s32[8]{0:T(128)S(1)}) fusion(s32[8,8]{1,0:T(8,128)} %param.15, s32[]{:T(128)S(6)} %select_n.18, s32[8,8]{1,0:T(8,128)} %param.14), kind=kLoop, calls=%fused_computation | loop fusion | bytes 132 | tf_op jit(solution)/shard_map/jit(dynamic_index_in_dim)/squeeze | solution.py:340
  11.5 0.1 concatenate.3.refs_0_
  11.6 0.0 copy-start.2
  11.6 0.9 %copy-done.2 = bf16[128,768]{1,0:T(8,128)(2,1)S(1)} copy-done((bf16[128,768]{1,0:T(8,128)(2,1)S(1)}, bf16[128,768]{1,0:T(8,128)(2,1)}, u32[]{:S(2)}) %copy-start.2) | copy-done | bytes 196632
  12.5 0.0 copy-start.4
  12.5 0.9 %copy-done.4 = bf16[128,768]{1,0:T(8,128)(2,1)S(1)} copy-done((bf16[128,768]{1,0:T(8,128)(2,1)S(1)}, bf16[128,768]{1,0:T(8,128)(2,1)}, u32[]{:S(2)}) %copy-start.4) | copy-done | bytes 196632
  13.4 1.0 %attention_weights.1 = (f32[6,128,128]{2,1,0:T(8,128)S(1)}, f32[8,768]{1,0:T(8,128)S(1)}) custom-call(s32[24]{0:T(128)S(1)} %concatenate.3.refs_0_, f32[8,768]{1,0:T(8,128)S(1)} %reshape.20.refs_1_, bf16[128,768]{1,0:T(8,128)(2,1)S(1)} %copy-done.2, bf16[128,768]{1,0:T(8,128)(2,1)S(1)} %copy-done.4), custom_call_target="tpu_custom_call" | custom-call | flops 1 | bytes 1 | tf_op jit(solution)/shard_map/attention_weights/pallas_call | solution.py:312
  14.5 3.9 %all-to-all-done = bf16[8,32,768]{2,1,0:T(8,128)(2,1)S(1)} async-done(((bf16[8,32,768]{2,1,0:T(8,128)(2,1)}), bf16[8,32,768]{2,1,0:T(8,128)(2,1)S(1)}, u32[]{:S(2)}, u32[]{:S(2)}) %all-to-all-start) | async-done | bytes 393248 | tf_op jit(solution)/shard_map/all_to_all | solution.py:344
  18.4 1.0 %value_rows.1 = (bf16[128,768]{1,0:T(8,128)(2,1)S(1)}, bf16[128,768]{1,0:T(8,128)(2,1)S(1)}) custom-call(s32[24]{0:T(128)S(1)} %concatenate.3.refs_0_, bf16[256,768]{1,0:T(8,128)(2,1)S(1)} %bitcast.10, f32[6,128,128]{2,1,0:T(8,128)S(1)} %get-tuple-element.27.refs_2_.refs_4_), custom_call_target="tpu_custom_call" | custom-call | flops 1 | bytes 1 | tf_op jit(solution)/shard_map/value_rows/pallas_call | solution.py:312
  19.4 2.0 %collective-permute-done.refs_3_ = bf16[128,1536]{1,0:T(8,128)(2,1)S(1)} collective-permute-done((bf16[128,1536]{1,0:T(8,128)(2,1)}, bf16[128,1536]{1,0:T(8,128)(2,1)S(1)}, u32[]{:S(2)}, u32[]{:S(2)}) %collective-permute-start) | collective-permute-done | bytes 393248 | tf_op jit(solution)/shard_map/ppermute | solution.py:348
  21.4 0.7 %collective-permute-start.2 = (bf16[128,1536]{1,0:T(8,128)(2,1)}, bf16[128,1536]{1,0:T(8,128)(2,1)S(1)}, u32[]{:S(2)}, u32[]{:S(2)}) collective-permute-start(bf16[128,1536]{1,0:T(8,128)(2,1)} %refs_1_.2), channel_id=1, source_target_pairs={{1,2},{2,1},{5,6},{6,5},{9,10},{10,9},{13,14},{14,13},{17,18},{18,... | collective-permute-start | bytes 1179656 | tf_op jit(solution)/shard_map/ppermute | solution.py:360
  22.0 1.9 %collective-permute-done.1.refs_2_ = bf16[128,1536]{1,0:T(8,128)(2,1)S(1)} collective-permute-done((bf16[128,1536]{1,0:T(8,128)(2,1)}, bf16[128,1536]{1,0:T(8,128)(2,1)S(1)}, u32[]{:S(2)}, u32[]{:S(2)}) %collective-permute-start.1) | collective-permute-done | bytes 393248 | tf_op jit(solution)/shard_map/ppermute | solution.py:347
  23.9 1.3 %collective-permute-start.3 = (bf16[128,1536]{1,0:T(8,128)(2,1)S(1)}, bf16[128,1536]{1,0:T(8,128)(2,1)S(1)}, u32[]{:S(2)}, u32[]{:S(2)}) collective-permute-start(bf16[128,1536]{1,0:T(8,128)(2,1)S(1)} %collective-permute-done.1.refs_2_), channel_id=1, source_target_pairs={{2,3},{1,0},{6,7},{5,4},{10,11},{9,8},{14,15},{13,12},{18,19},{17,... | collective-permute-start | bytes 1179656 | tf_op jit(solution)/shard_map/ppermute | solution.py:361
  25.2 2.5 %collective-permute-start.11 = (bf16[128,768]{1,0:T(8,128)(2,1)S(1)}, bf16[128,768]{1,0:T(8,128)(2,1)S(1)}, u32[]{:S(2)}, u32[]{:S(2)}) collective-permute-start(bf16[128,768]{1,0:T(8,128)(2,1)S(1)} %get-tuple-element.28.refs_0_.refs_7_), channel_id=1, source_target_pairs={{0,24},{4,28},{8,16},{12,20},{16,8},{20,12},{24,0},{28,4},{1,25},{... | collective-permute-start | bytes 589832 | tf_op jit(solution)/shard_map/ppermute | solution.py:316
  27.7 0.5 collective-permute-start.10
  28.2 0.5 collective-permute-start.9
  28.8 0.0 copy-done.6
  28.8 0.0 copy-start
  28.8 3.7 %copy-done = bf16[6144,768]{1,0:T(8,128)(2,1)S(1)} copy-done((bf16[6144,768]{1,0:T(8,128)(2,1)S(1)}, bf16[6144,768]{1,0:T(8,128)(2,1)}, u32[]{:S(2)}) %copy-start) | copy-done | bytes 9437208
  32.4 0.0 copy-start.1
  32.4 1.2 %partial_stats.1 = (f32[128,128]{1,0:T(8,128)S(1)}, bf16[4,128,1536]{2,1,0:T(8,128)(2,1)S(1)}) custom-call(s32[24]{0:T(128)S(1)} %concatenate.3.refs_0_, bf16[128,1536]{1,0:T(8,128)(2,1)S(1)} %copy-done.6, bf16[128,1536]{1,0:T(8,128)(2,1)S(1)} %collective-permute-done.1.refs_2_, bf16[128,1536]{1,0:T(8,128)(2,1)S(1)} %collective-permute-done.refs_3_, ...), custom_call_target="tpu_custom_call" | custom-call | flops 1 | bytes 1 | tf_op jit(solution)/shard_map/partial_stats/pallas_call | solution.py:312
  33.6 0.0 collective-permute-done.2.refs_4_
  33.6 0.6 %collective-permute-done.3.refs_5_ = bf16[128,1536]{1,0:T(8,128)(2,1)S(1)} collective-permute-done((bf16[128,1536]{1,0:T(8,128)(2,1)S(1)}, bf16[128,1536]{1,0:T(8,128)(2,1)S(1)}, u32[]{:S(2)}, u32[]{:S(2)}) %collective-permute-start.3) | collective-permute-done | bytes 393248 | tf_op jit(solution)/shard_map/ppermute | solution.py:361
  34.2 1.7 %norm_rows.1 = (bf16[128,768]{1,0:T(8,128)(2,1)S(1)}, bf16[128,768]{1,0:T(8,128)(2,1)S(1)}, bf16[128,768]{1,0:T(8,128)(2,1)S(1)}, bf16[128,768]{1,0:T(8,128)(2,1...) custom-call(s32[24]{0:T(128)S(1)} %concatenate.3.refs_0_, ...), custom_call_target="tpu_custom_call" | custom-call | flops 1 | bytes 1 | tf_op jit(solution)/shard_map/norm_rows/pallas_call | solution.py:312
  35.9 0.0 collective-permute-done.11.refs_3_.refs_10_
  35.9 0.0 collective-permute-done.10.refs_2_.refs_9_
  35.9 0.0 collective-permute-done.9.refs_1_.refs_8_
  36.0 0.1 pack_values.1
  36.0 0.1 collective-permute-start.12
  36.1 0.5 collective-permute-start.8
  36.6 2.3 %collective-permute-start.4 = (bf16[64,768]{1,0:T(8,128)(2,1)S(1)}, bf16[64,768]{1,0:T(8,128)(2,1)S(1)}, u32[]{:S(2)}, u32[]{:S(2)}) collective-permute-start(bf16[64,768]{1,0:T(8,128)(2,1)S(1)} %get-tuple-element.35), channel_id=1, source_target_pairs={{0,24},{4,28},{8,16},{12,20},{16,8},{20,12},{24,0},{28,4},{1,25},{... | collective-permute-start | bytes 294920 | tf_op jit(solution)/shard_map/ppermute | solution.py:316
  38.9 0.0 collective-permute-start.5
  38.9 1.3 %collective-permute-start.6 = (bf16[128,768]{1,0:T(8,128)(2,1)S(1)}, bf16[128,768]{1,0:T(8,128)(2,1)S(1)}, u32[]{:S(2)}, u32[]{:S(2)}) collective-permute-start(bf16[128,768]{1,0:T(8,128)(2,1)S(1)} %get-tuple-element.37.refs_4_), channel_id=1, source_target_pairs={{0,8},{4,12},{8,0},{12,4},{16,24},{20,28},{24,16},{28,20},{1,9},{5... | collective-permute-start | bytes 589832 | tf_op jit(solution)/shard_map/ppermute | solution.py:316
  40.3 0.0 collective-permute-done.8.refs_6_.refs_11_
  40.3 1.5 %collective-permute-start.7 = (bf16[128,768]{1,0:T(8,128)(2,1)S(1)}, bf16[128,768]{1,0:T(8,128)(2,1)S(1)}, u32[]{:S(2)}, u32[]{:S(2)}) collective-permute-start(bf16[128,768]{1,0:T(8,128)(2,1)S(1)} %get-tuple-element.38.refs_6_), channel_id=1, source_target_pairs={{0,16},{4,20},{8,24},{12,28},{16,0},{20,4},{24,8},{28,12},{1,17},{... | collective-permute-start | bytes 589832 | tf_op jit(solution)/shard_map/ppermute | solution.py:316
  41.8 0.0 collective-permute-done.12.refs_11_.refs_10_
  41.8 0.3 collective-permute-start.14
  42.1 0.0 copy-done.1
  42.1 0.0 copy-start.3
  42.1 0.0 copy-start.5
  42.1 1.9 %project_values.1.refs_2_.refs_0_ = bf16[128,768]{1,0:T(8,128)(2,1)S(1)} custom-call(s32[24]{0:T(128)S(1)} %concatenate.3.refs_0_, bf16[6144,768]{1,0:T(8,128)(2,1)S(1)} %copy-done.1, bf16[128,768]{1,0:T(8,128)(2,1)S(1)} %get-tuple-element.34.refs_1_.refs_2_, bf16[128,768]{1,0:T(8,128)(2,1)S(1)} %get-tuple-element.39.refs_4_.refs_3_, ...), custom_call_target="tpu_custom_call" | custom-call | flops 1 | bytes 1 | tf_op jit(solution)/shard_map/project_values/pallas_call | solution.py:312
  44.0 0.0 collective-permute-done.4.refs_2_.refs_0_
  44.0 0.9 %collective-permute-done.5.refs_3_.refs_1_ = bf16[64,768]{1,0:T(8,128)(2,1)S(1)} collective-permute-done((bf16[64,768]{1,0:T(8,128)(2,1)S(1)}, bf16[64,768]{1,0:T(8,128)(2,1)S(1)}, u32[]{:S(2)}, u32[]{:S(2)}) %collective-permute-start.5) | collective-permute-done | bytes 98336 | tf_op jit(solution)/shard_map/ppermute | solution.py:316
  45.0 2.3 %collective-permute-start.13 = (bf16[128,768]{1,0:T(8,128)(2,1)S(1)}, bf16[128,768]{1,0:T(8,128)(2,1)S(1)}, u32[]{:S(2)}, u32[]{:S(2)}) collective-permute-start(bf16[128,768]{1,0:T(8,128)(2,1)S(1)} %bitcast.11), channel_id=1, source_target_pairs={{0,1},{1,0},{2,3},{3,2},{4,5},{5,4},{6,7},{7,6},{8,9},{9,8},{10,11... | collective-permute-start | bytes 589832 | tf_op jit(solution)/shard_map/ppermute | solution.py:398
  47.3 0.3 collective-permute-start.15
  47.6 0.0 copy-done.3
  47.6 0.0 copy-done.5
  47.6 1.4 %attention_backward.1 = (bf16[128,768]{1,0:T(8,128)(2,1)}, bf16[128,768]{1,0:T(8,128)(2,1)}) custom-call(bf16[128,768]{1,0:T(8,128)(2,1)S(1)} %project_values.1.refs_2_.refs_0_, bf16[128,768]{1,0:T(8,128)(2,1)S(1)} %copy-done.3, bf16[128,768]{1,0:T(8,128)(2,1)S(1)} %copy-done.5, bf16[128,768]{1,0:T(8,128)(2,1)S(1)} %get-tuple-element.48.refs_3_, ...), custom_call_target="tpu_custom_call" | custom-call | flops 1 | bytes 1 | tf_op jit(solution)/shard_map/attention_backward/pallas_call | solution.py:312
  49.0 0.0 copy-start.7
  49.0 0.0 collective-permute-done.6.refs_4_
  49.0 0.1 collective-permute-done.7.refs_5_
  49.1 1.7 %gradient_first.1 = (f32[768,768]{1,0:T(8,128)S(1)}, bf16[384,768]{1,0:T(8,128)(2,1)S(1)}) custom-call(s32[24]{0:T(128)S(1)} %concatenate.3.refs_0_, bf16[128,768]{1,0:T(8,128)(2,1)S(1)} %get-tuple-element.34.refs_1_.refs_2_, bf16[64,768]{1,0:T(8,128)(2,1)S(1)} %collective-permute-done.4.refs_2_.refs_0_, ...), custom_call_target="tpu_custom_call" | custom-call | flops 1 | bytes 1 | tf_op jit(solution)/shard_map/gradient_first/pallas_call | solution.py:312
  50.7 1.6 %collective-permute-done.14.refs_3_ = bf16[128,768]{1,0:T(8,128)(2,1)S(1)} collective-permute-done((bf16[128,768]{1,0:T(8,128)(2,1)S(1)}, bf16[128,768]{1,0:T(8,128)(2,1)S(1)}, u32[]{:S(2)}, u32[]{:S(2)}) %collective-permute-start.14) | collective-permute-done | bytes 196640 | tf_op jit(solution)/shard_map/ppermute | solution.py:316
  52.3 0.0 collective-permute-done.13.refs_2_
  52.3 2.0 %collective-permute-done.15.refs_4_ = bf16[128,768]{1,0:T(8,128)(2,1)S(1)} collective-permute-done((bf16[128,768]{1,0:T(8,128)(2,1)S(1)}, bf16[128,768]{1,0:T(8,128)(2,1)S(1)}, u32[]{:S(2)}, u32[]{:S(2)}) %collective-permute-start.15) | collective-permute-done | bytes 196640 | tf_op jit(solution)/shard_map/ppermute | solution.py:316
  54.4 0.0 copy-done.7
  54.4 1.8 %gradient_last.1 = f32[768,768]{1,0:T(8,128)} custom-call(f32[768,768]{1,0:T(8,128)S(1)} %get-tuple-element.40.refs_0_, bf16[384,768]{1,0:T(8,128)(2,1)S(1)} %get-tuple-element.41.refs_1_, bf16[128,768]{1,0:T(8,128)(2,1)S(1)} %collective-permute-done.13.refs_2_, bf16[128,768]{1,0:T(8,128)(2,1)S(1)} %collective-permute-done.14.refs_3_, ...), custom_call_target="tpu_custom_call" | custom-call | flops 1 | bytes 1 | tf_op jit(solution)/shard_map/gradient_last/pallas_call | solution.py:312
  (2 shorter events, 0.0 us)
Async XLA Ops:
  0.6 28.1 %copy-start.6 = (bf16[128,1536]{1,0:T(8,128)(2,1)S(1)}, bf16[128,1536]{1,0:T(8,128)(2,1)}, u32[]{:S(2)}) copy-start(bf16[128,1536]{1,0:T(8,128)(2,1)} %refs_1_.2) | copy-start | bytes 1179652
  0.6 20.7 %collective-permute-start = (bf16[128,1536]{1,0:T(8,128)(2,1)}, bf16[128,1536]{1,0:T(8,128)(2,1)S(1)}, u32[]{:S(2)}, u32[]{:S(2)}) collective-permute-start(bf16[128,1536]{1,0:T(8,128)(2,1)} %refs_1_.2), channel_id=1, source_target_pairs={{0,1},{1,0},{2,3},{3,2},{4,5},{5,4},{6,7},{7,6},{8,9},{9,8},{10,11... | collective-permute-start | bytes 1179656 | tf_op jit(solution)/shard_map/ppermute | solution.py:348
  3.7 20.2 %collective-permute-start.1 = (bf16[128,1536]{1,0:T(8,128)(2,1)}, bf16[128,1536]{1,0:T(8,128)(2,1)S(1)}, u32[]{:S(2)}, u32[]{:S(2)}) collective-permute-start(bf16[128,1536]{1,0:T(8,128)(2,1)} %refs_1_.2), channel_id=1, source_target_pairs={{0,2},{2,0},{1,3},{3,1},{4,6},{6,4},{5,7},{7,5},{8,10},{10,8},{9,1... | collective-permute-start | bytes 1179656 | tf_op jit(solution)/shard_map/ppermute | solution.py:347
  6.3 12.1 %all-to-all-start = ((bf16[8,32,768]{2,1,0:T(8,128)(2,1)}), bf16[8,32,768]{2,1,0:T(8,128)(2,1)S(1)}, u32[]{:S(2)}, u32[]{:S(2)}) async-start(bf16[8,32,768]{2,1,0:T(8,128)(2,1)} %bitcast.12), calls=%async_computation | async-start | bytes 786432 | tf_op jit(solution)/shard_map/all_to_all | solution.py:344
  11.6 0.9 %copy-start.2 = (bf16[128,768]{1,0:T(8,128)(2,1)S(1)}, bf16[128,768]{1,0:T(8,128)(2,1)}, u32[]{:S(2)}) copy-start(bf16[128,768]{1,0:T(8,128)(2,1)} %refs_1_.4) | copy-start | bytes 589828
  12.5 0.9 %copy-start.4 = (bf16[128,768]{1,0:T(8,128)(2,1)S(1)}, bf16[128,768]{1,0:T(8,128)(2,1)}, u32[]{:S(2)}) copy-start(bf16[128,768]{1,0:T(8,128)(2,1)} %refs_2_.3) | copy-start | bytes 589828
  21.4 12.3 %collective-permute-start.2 = (bf16[128,1536]{1,0:T(8,128)(2,1)}, bf16[128,1536]{1,0:T(8,128)(2,1)S(1)}, u32[]{:S(2)}, u32[]{:S(2)}) collective-permute-start(bf16[128,1536]{1,0:T(8,128)(2,1)} %refs_1_.2), channel_id=1, source_target_pairs={{1,2},{2,1},{5,6},{6,5},{9,10},{10,9},{13,14},{14,13},{17,18},{18,... | collective-permute-start | bytes 1179656 | tf_op jit(solution)/shard_map/ppermute | solution.py:360
  23.9 10.3 %collective-permute-start.3 = (bf16[128,1536]{1,0:T(8,128)(2,1)S(1)}, bf16[128,1536]{1,0:T(8,128)(2,1)S(1)}, u32[]{:S(2)}, u32[]{:S(2)}) collective-permute-start(bf16[128,1536]{1,0:T(8,128)(2,1)S(1)} %collective-permute-done.1.refs_2_), channel_id=1, source_target_pairs={{2,3},{1,0},{6,7},{5,4},{10,11},{9,8},{14,15},{13,12},{18,19},{17,... | collective-permute-start | bytes 1179656 | tf_op jit(solution)/shard_map/ppermute | solution.py:361
  25.2 10.7 %collective-permute-start.11 = (bf16[128,768]{1,0:T(8,128)(2,1)S(1)}, bf16[128,768]{1,0:T(8,128)(2,1)S(1)}, u32[]{:S(2)}, u32[]{:S(2)}) collective-permute-start(bf16[128,768]{1,0:T(8,128)(2,1)S(1)} %get-tuple-element.28.refs_0_.refs_7_), channel_id=1, source_target_pairs={{0,24},{4,28},{8,16},{12,20},{16,8},{20,12},{24,0},{28,4},{1,25},{... | collective-permute-start | bytes 589832 | tf_op jit(solution)/shard_map/ppermute | solution.py:316
  27.7 8.2 %collective-permute-start.10 = (bf16[128,768]{1,0:T(8,128)(2,1)S(1)}, bf16[128,768]{1,0:T(8,128)(2,1)S(1)}, u32[]{:S(2)}, u32[]{:S(2)}) collective-permute-start(bf16[128,768]{1,0:T(8,128)(2,1)S(1)} %get-tuple-element.28.refs_0_.refs_7_), channel_id=1, source_target_pairs={{0,16},{4,20},{8,24},{12,28},{16,0},{20,4},{24,8},{28,12},{1,17},{... | collective-permute-start | bytes 589832 | tf_op jit(solution)/shard_map/ppermute | solution.py:316
  28.2 7.7 %collective-permute-start.9 = (bf16[128,768]{1,0:T(8,128)(2,1)S(1)}, bf16[128,768]{1,0:T(8,128)(2,1)S(1)}, u32[]{:S(2)}, u32[]{:S(2)}) collective-permute-start(bf16[128,768]{1,0:T(8,128)(2,1)S(1)} %get-tuple-element.28.refs_0_.refs_7_), channel_id=1, source_target_pairs={{0,8},{4,12},{8,0},{12,4},{16,24},{20,28},{24,16},{28,20},{1,9},{5... | collective-permute-start | bytes 589832 | tf_op jit(solution)/shard_map/ppermute | solution.py:316
  28.8 3.7 %copy-start = (bf16[6144,768]{1,0:T(8,128)(2,1)S(1)}, bf16[6144,768]{1,0:T(8,128)(2,1)}, u32[]{:S(2)}) copy-start(bf16[6144,768]{1,0:T(8,128)(2,1)} %refs_1_.3) | copy-start | bytes 28311556
  32.4 9.7 %copy-start.1 = (bf16[6144,768]{1,0:T(8,128)(2,1)S(1)}, bf16[6144,768]{1,0:T(8,128)(2,1)}, u32[]{:S(2)}) copy-start(bf16[6144,768]{1,0:T(8,128)(2,1)} %refs_1_.3) | copy-start | bytes 28311556
  36.0 5.8 %collective-permute-start.12 = (bf16[4,128,768]{2,1,0:T(8,128)(2,1)S(1)}, bf16[4,128,768]{2,1,0:T(8,128)(2,1)S(1)}, u32[]{:S(2)}, u32[]{:S(2)}) collective-permute-start(bf16[4,128,768]{2,1,0:T(8,128)(2,1)S(1)} %pack_values.1), channel_id=1, source_target_pairs={{0,4},{4,0},{8,12},{12,8},{16,20},{20,16},{24,28},{28,24},{1,5},{5... | collective-permute-start | bytes 2359304 | tf_op jit(solution)/shard_map/ppermute | solution.py:316
  36.1 4.2 %collective-permute-start.8 = (bf16[128,768]{1,0:T(8,128)(2,1)S(1)}, bf16[128,768]{1,0:T(8,128)(2,1)S(1)}, u32[]{:S(2)}, u32[]{:S(2)}) collective-permute-start(bf16[128,768]{1,0:T(8,128)(2,1)S(1)} %get-tuple-element.39.refs_4_.refs_3_), channel_id=1, source_target_pairs={{0,4},{4,0},{8,12},{12,8},{16,20},{20,16},{24,28},{28,24},{1,5},{5... | collective-permute-start | bytes 589832 | tf_op jit(solution)/shard_map/ppermute | solution.py:316
  36.6 7.4 %collective-permute-start.4 = (bf16[64,768]{1,0:T(8,128)(2,1)S(1)}, bf16[64,768]{1,0:T(8,128)(2,1)S(1)}, u32[]{:S(2)}, u32[]{:S(2)}) collective-permute-start(bf16[64,768]{1,0:T(8,128)(2,1)S(1)} %get-tuple-element.35), channel_id=1, source_target_pairs={{0,24},{4,28},{8,16},{12,20},{16,8},{20,12},{24,0},{28,4},{1,25},{... | collective-permute-start | bytes 294920 | tf_op jit(solution)/shard_map/ppermute | solution.py:316
  38.9 6.1 %collective-permute-start.5 = (bf16[64,768]{1,0:T(8,128)(2,1)S(1)}, bf16[64,768]{1,0:T(8,128)(2,1)S(1)}, u32[]{:S(2)}, u32[]{:S(2)}) collective-permute-start(bf16[64,768]{1,0:T(8,128)(2,1)S(1)} %get-tuple-element.36), channel_id=1, source_target_pairs={{0,28},{4,24},{8,20},{12,16},{16,12},{20,8},{24,4},{28,0},{1,29},{... | collective-permute-start | bytes 294920 | tf_op jit(solution)/shard_map/ppermute | solution.py:316
  38.9 10.0 %collective-permute-start.6 = (bf16[128,768]{1,0:T(8,128)(2,1)S(1)}, bf16[128,768]{1,0:T(8,128)(2,1)S(1)}, u32[]{:S(2)}, u32[]{:S(2)}) collective-permute-start(bf16[128,768]{1,0:T(8,128)(2,1)S(1)} %get-tuple-element.37.refs_4_), channel_id=1, source_target_pairs={{0,8},{4,12},{8,0},{12,4},{16,24},{20,28},{24,16},{28,20},{1,9},{5... | collective-permute-start | bytes 589832 | tf_op jit(solution)/shard_map/ppermute | solution.py:316
  40.3 8.8 %collective-permute-start.7 = (bf16[128,768]{1,0:T(8,128)(2,1)S(1)}, bf16[128,768]{1,0:T(8,128)(2,1)S(1)}, u32[]{:S(2)}, u32[]{:S(2)}) collective-permute-start(bf16[128,768]{1,0:T(8,128)(2,1)S(1)} %get-tuple-element.38.refs_6_), channel_id=1, source_target_pairs={{0,16},{4,20},{8,24},{12,28},{16,0},{20,4},{24,8},{28,12},{1,17},{... | collective-permute-start | bytes 589832 | tf_op jit(solution)/shard_map/ppermute | solution.py:316
  41.8 10.5 %collective-permute-start.14 = (bf16[128,768]{1,0:T(8,128)(2,1)S(1)}, bf16[128,768]{1,0:T(8,128)(2,1)S(1)}, u32[]{:S(2)}, u32[]{:S(2)}) collective-permute-start(bf16[128,768]{1,0:T(8,128)(2,1)S(1)} %get-tuple-element.42.refs_5_), channel_id=1, source_target_pairs={{0,12},{4,8},{8,4},{12,0},{16,28},{20,24},{24,20},{28,16},{1,13},{... | collective-permute-start | bytes 589832 | tf_op jit(solution)/shard_map/ppermute | solution.py:316
  42.1 5.5 %copy-start.3 = (bf16[128,768]{1,0:T(8,128)(2,1)S(1)}, bf16[128,768]{1,0:T(8,128)(2,1)}, u32[]{:S(2)}) copy-start(bf16[128,768]{1,0:T(8,128)(2,1)} %refs_1_.4) | copy-start | bytes 589828
  42.1 5.5 %copy-start.5 = (bf16[128,768]{1,0:T(8,128)(2,1)S(1)}, bf16[128,768]{1,0:T(8,128)(2,1)}, u32[]{:S(2)}) copy-start(bf16[128,768]{1,0:T(8,128)(2,1)} %refs_2_.3) | copy-start | bytes 589828
  45.0 7.4 %collective-permute-start.13 = (bf16[128,768]{1,0:T(8,128)(2,1)S(1)}, bf16[128,768]{1,0:T(8,128)(2,1)S(1)}, u32[]{:S(2)}, u32[]{:S(2)}) collective-permute-start(bf16[128,768]{1,0:T(8,128)(2,1)S(1)} %bitcast.11), channel_id=1, source_target_pairs={{0,1},{1,0},{2,3},{3,2},{4,5},{5,4},{6,7},{7,6},{8,9},{9,8},{10,11... | collective-permute-start | bytes 589832 | tf_op jit(solution)/shard_map/ppermute | solution.py:398
  47.3 7.1 %collective-permute-start.15 = (bf16[128,768]{1,0:T(8,128)(2,1)S(1)}, bf16[128,768]{1,0:T(8,128)(2,1)S(1)}, u32[]{:S(2)}, u32[]{:S(2)}) collective-permute-start(bf16[128,768]{1,0:T(8,128)(2,1)S(1)} %get-tuple-element.47.refs_7_), channel_id=1, source_target_pairs={{0,20},{4,16},{8,28},{12,24},{16,4},{20,0},{24,12},{28,8},{1,21},{... | collective-permute-start | bytes 589832 | tf_op jit(solution)/shard_map/ppermute | solution.py:316
  49.0 5.4 %copy-start.7 = (bf16[128,768]{1,0:T(8,128)(2,1)S(1)}, bf16[128,768]{1,0:T(8,128)(2,1)}, u32[]{:S(2)}) copy-start(bf16[128,768]{1,0:T(8,128)(2,1)} %get-tuple-element.25.refs_5_) | copy-start | bytes 589828
